TPU v7x, 32 devices: a whole 2x2x4 slice. The times are simulated.
32 devices in a mesh: groups: 2 (over y), atoms: 8 (over z, x), samples: 2 (over core).
Axes of the slice: x: 2, y: 2, z: 4, core: 2. Of those that a mesh axis runs over, the one named last changes fastest.
Arguments:
- act: bfloat16 [16, 10240, 128], P('samples', ('groups', 'atoms')), parts along dimension 1, may hold values from -6 to 6
- grad_out: bfloat16 [16, 10240, 128], P('samples', ('groups', 'atoms')), parts along dimension 1, may hold values from -6 to 6
- pair: bfloat16 [320, 32, 16, 128], P(('groups', 'atoms')), parts along dimension 0, may hold values from -500 to 500
- w_query: bfloat16 [128, 128], replicated, may hold values from -0.5 to 0.5
- w_key: bfloat16 [128, 128], replicated, may hold values from -0.5 to 0.5
- w_value: bfloat16 [128, 128], replicated, may hold values from -0.5 to 0.5
- w_gate: bfloat16 [128, 128], replicated, may hold values from -0.5 to 0.5
- w_out: bfloat16 [128, 128], replicated, may hold values from -0.5 to 0.5
- w_pair: bfloat16 [16, 4], replicated, may hold values from -1.5 to 1.5
- w_token: float32 [4], replicated, may hold values from -2 to 2
- offsets: int32 [320], P(('groups', 'atoms')), parts along dimension 0, may hold values from -128 to 32, as said below
- atom_token: int32 [10240], P(('groups', 'atoms')), parts along dimension 0, may hold values from 0 to 639, never falling along the last dimension, each value on 1 to 24 neighbouring positions
- padding: int32 [16], P(('groups', 'atoms')), parts along dimension 0, may hold values from 0 to 64, as said below
Outputs:
- grad_act: bfloat16 [16, 10240, 128], P('samples', ('groups', 'atoms')), parts along dimension 1
- grad_pair: bfloat16 [320, 32, 16, 128], P(('groups', 'atoms'), 'samples'), parts along dimension 0
- grad_weights: float32 [10, 128, 128], P('groups'), parts along dimension 0
- grad_pair_weight: float32 [32, 4], P('groups'), parts along dimension 0
- grad_token_weight: float32 [8], P('groups'), parts along dimension 0
There are 2 independent parts, one for each index of `groups`. A program takes and returns all parts, laid end to end along the dimension named above; an argument that names none is the same for every part. Nothing has to cross between parts.
Inputs may be any that keep to these rules, and one draw needn't show every extreme that they name: Window w reads the 128 atoms that begin at 32 * w + offsets[w], moved into the complex. padding[r] atoms at the end of atom range r are padding. `atom_token`: the atoms of one token are contiguous, at most 24 of them.
All inputs are finite; a program needn't handle non-finite values.
Results may differ from a plain program's by a relative error of at most 0.025.
Values may be sent and summed in bfloat16 or wider, within the bound.
No kernel may reach another device: no remote copies, remote signals or barrier semaphores. Data moves between devices by JAX's collectives and lax.ppermute only.
A program may use at most 128 MiB of HBM per device.

v0:
```python
import math

import jax
import jax.numpy as jnp
from jax import lax
from jax.sharding import PartitionSpec as P

MASKED = -1000000000.0


def with_halo(value, sides, width):
    for axis, dim in sides:
        count, length = (lax.axis_size(axis), value.shape[dim])
        up = [(i, (i + 1) % count) for i in range(count - 1)]
        down = [(j, i) for i, j in up]
        last = lax.slice_in_dim(value, length - width, length, axis=dim)
        initial = lax.slice_in_dim(value, 0, width, axis=dim)
        before = lax.ppermute(last, axis, up)
        after = lax.ppermute(initial, axis, down)
        value = jnp.concatenate([before, value, after], axis=dim)
    return value


def passed_along(value, axis, steps):
    count = lax.axis_size(axis)
    initial, last = (max(0, -steps), min(count, count - steps))
    return lax.ppermute(value, axis, [(source, source + steps) for source in range(initial, last)])


def attend(query, keys, values, gate_logit, grad_y, pair_bias, key_live):
    windows = keys.shape[0]
    head_count = pair_bias.shape[1]
    channels = query.shape[-1]
    head_dim = channels // head_count
    score_scale = 1.0 / math.sqrt(head_dim)
    query_heads = query.reshape(windows, -1, head_count, head_dim)
    key_heads = keys.reshape(windows, -1, head_count, head_dim)
    value_heads = values.reshape(windows, -1, head_count, head_dim)
    scores = (
        jnp.einsum("wihd,wjhd->whij", query_heads, key_heads, preferred_element_type=jnp.float32)
        * score_scale
        + pair_bias
    )
    scores = jnp.where(key_live[:, None, None, :], scores, MASKED)
    row_max = jnp.max(scores, axis=-1, keepdims=True)
    exponent = jnp.exp(scores - row_max)
    attn_probs = exponent / jnp.sum(exponent, axis=-1, keepdims=True)
    probs_b = attn_probs.astype(jnp.bfloat16)
    attended = jnp.einsum(
        "whij,wjhd->wihd", probs_b, value_heads, preferred_element_type=jnp.float32
    ).reshape(query.shape)
    gate_value = jax.nn.sigmoid(gate_logit)
    gated = (gate_value * attended).astype(jnp.bfloat16)
    d_attended = (grad_y * gate_value).astype(jnp.bfloat16)
    d_gate = (grad_y * attended * gate_value * (1.0 - gate_value)).astype(jnp.bfloat16)
    attended_heads = d_attended.reshape(windows, -1, head_count, head_dim)
    d_probs = jnp.einsum(
        "wihd,wjhd->whij", attended_heads, value_heads, preferred_element_type=jnp.float32
    )
    d_scores = attn_probs * (d_probs - jnp.sum(attn_probs * d_probs, axis=-1, keepdims=True))
    ds_b = d_scores.astype(jnp.bfloat16)
    d_query = (
        (
            jnp.einsum("whij,wjhd->wihd", ds_b, key_heads, preferred_element_type=jnp.float32)
            * score_scale
        )
        .astype(jnp.bfloat16)
        .reshape(query.shape)
    )
    d_keys = (
        jnp.einsum("whij,wihd->wjhd", ds_b, query_heads, preferred_element_type=jnp.float32)
        * score_scale
    )
    d_values = jnp.einsum(
        "whij,wihd->wjhd", probs_b, attended_heads, preferred_element_type=jnp.float32
    )
    return (gated, d_query, d_gate, d_keys, d_values, d_scores)


def per_device(
    act,
    grad_out,
    pair,
    w_query,
    w_key,
    w_value,
    w_gate,
    w_out,
    w_pair,
    w_token,
    offsets,
    atom_token,
    padding,
):
    sample_count, atom_count, channels = act.shape
    windows = offsets.shape[0]
    win_rows = atom_count // windows
    key_span = pair.shape[-1]
    ranges = lax.axis_size("atoms")
    anchor = lax.axis_index("atoms") * atom_count
    position = jnp.arange(atom_count, dtype=jnp.int32)
    is_live = position < atom_count - padding[0]
    atom_codes = jnp.where(is_live, atom_token + 1, 0)
    wide_codes = with_halo(atom_codes, (("atoms", 0),), key_span)
    starts = jnp.clip(
        anchor + win_rows * jnp.arange(windows, dtype=jnp.int32) + offsets,
        0,
        ranges * atom_count - key_span,
    )
    key_rows = starts[:, None] - anchor + key_span + jnp.arange(key_span, dtype=jnp.int32)[None, :]
    key_codes = wide_codes[key_rows]
    key_live = key_codes > 0
    same_token = key_codes[:, None, :] == (atom_token + 1).reshape(windows, win_rows)[:, :, None]
    pair_bias = jnp.einsum(
        "wicj,ch->whij", pair, w_pair, preferred_element_type=jnp.float32
    ) + w_token[None, :, None, None] * same_token[:, None, :, :].astype(jnp.float32)
    projection = jnp.concatenate([w_query, w_key, w_value, w_gate], axis=1)
    flat_act = act.reshape(sample_count * atom_count, channels)
    mixed = jnp.dot(flat_act, projection, preferred_element_type=jnp.float32).reshape(
        sample_count, atom_count, 4 * channels
    )
    query = mixed[..., :channels].astype(jnp.bfloat16)
    key_value = mixed[..., channels : 3 * channels].astype(jnp.bfloat16)
    gate_logit = mixed[..., 3 * channels :]
    wide_kv = with_halo(key_value, (("atoms", 1),), key_span)
    flat_grad = grad_out.reshape(sample_count * atom_count, channels)
    grad_y = jnp.dot(flat_grad, w_out.T, preferred_element_type=jnp.float32).reshape(
        sample_count, atom_count, channels
    )

    def one_sample(bias_sum, inputs):
        sample_query, sample_kv, sample_gate, sample_grad_y = inputs
        windowed = sample_kv[key_rows]
        gated, d_query, d_gate, d_keys, d_values, d_scores = attend(
            sample_query,
            windowed[..., :channels],
            windowed[..., channels:],
            sample_gate,
            sample_grad_y,
            pair_bias,
            key_live,
        )
        d_windowed = jnp.concatenate(
            [
                d_keys.reshape(windows, key_span, channels),
                d_values.reshape(windows, key_span, channels),
            ],
            axis=-1,
        )
        d_wide = jnp.zeros(sample_kv.shape, jnp.float32).at[key_rows].add(d_windowed)
        return (bias_sum + d_scores, (gated, d_query, d_gate, d_wide))

    bias_local, (gated, d_query, d_gate, d_wide) = lax.scan(
        one_sample, jnp.zeros(pair_bias.shape, jnp.float32), (query, wide_kv, gate_logit, grad_y)
    )
    inner_grad = d_wide[:, key_span : key_span + atom_count]
    from_upper = passed_along(d_wide[:, :key_span].astype(jnp.bfloat16), "atoms", -1).astype(
        jnp.float32
    )
    from_lower = passed_along(
        d_wide[:, key_span + atom_count :].astype(jnp.bfloat16), "atoms", 1
    ).astype(jnp.float32)
    kv_grad = (
        inner_grad.at[:, :key_span].add(from_lower).at[:, atom_count - key_span :].add(from_upper)
    )
    kv_rounded = kv_grad.astype(jnp.bfloat16)
    stacked = jnp.concatenate([d_query, kv_rounded, d_gate], axis=-1).reshape(
        sample_count * atom_count, 4 * channels
    )
    grad_act = (
        jnp.dot(stacked, projection.T, preferred_element_type=jnp.float32)
        .astype(jnp.bfloat16)
        .reshape(sample_count, atom_count, channels)
    )
    weight_part = jnp.dot(flat_act.T, stacked, preferred_element_type=jnp.float32)
    out_part = jnp.dot(gated.reshape(-1, channels).T, flat_grad, preferred_element_type=jnp.float32)
    pair_weight_part = jnp.einsum(
        "wicj,whij->ch", pair, bias_local, preferred_element_type=jnp.float32
    )
    token_part = jnp.sum(jnp.where(same_token[:, None, :, :], bias_local, 0.0), axis=(0, 2, 3))
    weight_sum, out_sum, grad_pair_weight, grad_token_weight = lax.psum(
        (weight_part, out_part, pair_weight_part, token_part), ("atoms", "samples")
    )
    grad_weights = jnp.concatenate(
        [weight_sum.reshape(channels, 4, channels).transpose(1, 0, 2), out_sum[None]], axis=0
    )
    sample_ways = lax.axis_size("samples")
    share_rows = win_rows // sample_ways
    bias_total = lax.psum(bias_local.astype(jnp.bfloat16), "samples").astype(jnp.float32)
    my_share = lax.dynamic_slice_in_dim(
        bias_total, lax.axis_index("samples") * share_rows, share_rows, 2
    )
    grad_pair = jnp.einsum(
        "whij,ch->wicj", my_share, w_pair.astype(jnp.float32), precision=lax.Precision.HIGHEST
    ).astype(jnp.bfloat16)
    return (grad_act, grad_pair, grad_weights, grad_pair_weight, grad_token_weight)


def solution(mesh):
    in_specs = (
        P("samples", ("groups", "atoms"), None),
        P("samples", ("groups", "atoms"), None),
        P(("groups", "atoms"), None, None, None),
        P(),
        P(),
        P(),
        P(),
        P(),
        P(),
        P(),
        P(("groups", "atoms")),
        P(("groups", "atoms")),
        P(("groups", "atoms")),
    )
    out_specs = (
        P("samples", ("groups", "atoms"), None),
        P(("groups", "atoms"), "samples", None, None),
        P("groups", None, None),
        P("groups", None),
        P("groups"),
    )
    return jax.shard_map(
        per_device, mesh=mesh, in_specs=in_specs, out_specs=out_specs, check_vma=False
    )
```

profile of v0, /device:TPU:0, one launch (start us, length us, event | category | flops | bytes accessed | tf_op | source)
XLA Modules:
  0.0 949.3 jit_solution(12060509717389246733)
XLA Ops:
  17.8 11.4 %copy.63 = f32[5120,512]{1,0:T(8,128)} copy(f32[5120,512]{0,1:T(8,128)} %convolution_bitcast_fusion.1) | data formatting | bytes 20971520 | tf_op jit(solution)/shard_map/reshape | solution.py:119
  62.7 9.4 gather_fusion.1
  78.0 686.5 %while.21 = (s32[]{:T(128)}, f32[20,4,32,128]{3,2,1,0:T(8,128)}, bf16[8,640,128]{2,1,0:T(8,128)(2,1)}, bf16[8,640,128]{1,2,0:T(8,128)(2,1)}, bf16[8,640,128]{1,2...) while((s32[]{:T(128)}, f32[20,4,32,128]{3,2,1,0:T(8,128)}, ...), condition=%wide.region_5.6_spmd.clone, body=%wide.region_0.5_spmd.clone.sunk | while | flops 135430016 | bytes 73126840 | solution.py:153
  79.2 8.1 gather_fusion
  136.6 15.7 %scatter_custom_fusion.6 = f32[896,256]{1,0:T(8,128)} fusion(s32[2560]{0:T(1024)S(1)} %fusion.106, f32[2560,256]{1,0:T(8,128)} %bitcast.143, f32[]{:T(128)} %constant.105.clone.5..sunk), kind=kCustom, calls=%fused_computation.21.clone.1 | custom fusion | flops 655360 | bytes 918016 | tf_op jit(solution)/shard_map/while/body/eval_jaxpr/scatter-add | solution.py:150
  164.7 8.1 gather_fusion
  222.5 15.7 %scatter_custom_fusion.6 = f32[896,256]{1,0:T(8,128)} fusion(s32[2560]{0:T(1024)S(1)} %fusion.106, f32[2560,256]{1,0:T(8,128)} %bitcast.143, f32[]{:T(128)} %constant.105.clone.5..sunk), kind=kCustom, calls=%fused_computation.21.clone.1 | custom fusion | flops 655360 | bytes 918016 | tf_op jit(solution)/shard_map/while/body/eval_jaxpr/scatter-add | solution.py:150
  250.5 8.1 gather_fusion
  308.3 15.7 %scatter_custom_fusion.6 = f32[896,256]{1,0:T(8,128)} fusion(s32[2560]{0:T(1024)S(1)} %fusion.106, f32[2560,256]{1,0:T(8,128)} %bitcast.143, f32[]{:T(128)} %constant.105.clone.5..sunk), kind=kCustom, calls=%fused_computation.21.clone.1 | custom fusion | flops 655360 | bytes 918016 | tf_op jit(solution)/shard_map/while/body/eval_jaxpr/scatter-add | solution.py:150
  336.4 8.1 gather_fusion
  394.2 15.7 %scatter_custom_fusion.6 = f32[896,256]{1,0:T(8,128)} fusion(s32[2560]{0:T(1024)S(1)} %fusion.106, f32[2560,256]{1,0:T(8,128)} %bitcast.143, f32[]{:T(128)} %constant.105.clone.5..sunk), kind=kCustom, calls=%fused_computation.21.clone.1 | custom fusion | flops 655360 | bytes 918016 | tf_op jit(solution)/shard_map/while/body/eval_jaxpr/scatter-add | solution.py:150
  422.2 8.1 gather_fusion
  480.0 15.7 %scatter_custom_fusion.6 = f32[896,256]{1,0:T(8,128)} fusion(s32[2560]{0:T(1024)S(1)} %fusion.106, f32[2560,256]{1,0:T(8,128)} %bitcast.143, f32[]{:T(128)} %constant.105.clone.5..sunk), kind=kCustom, calls=%fused_computation.21.clone.1 | custom fusion | flops 655360 | bytes 918016 | tf_op jit(solution)/shard_map/while/body/eval_jaxpr/scatter-add | solution.py:150
  508.1 8.1 gather_fusion
  528.2 7.5 convolution_bitcast_fusion.5
  565.9 15.7 %scatter_custom_fusion.6 = f32[896,256]{1,0:T(8,128)} fusion(s32[2560]{0:T(1024)S(1)} %fusion.106, f32[2560,256]{1,0:T(8,128)} %bitcast.143, f32[]{:T(128)} %constant.105.clone.5..sunk), kind=kCustom, calls=%fused_computation.21.clone.1 | custom fusion | flops 655360 | bytes 918016 | tf_op jit(solution)/shard_map/while/body/eval_jaxpr/scatter-add | solution.py:150
  594.0 8.1 gather_fusion
  614.1 7.5 convolution_bitcast_fusion.5
  651.8 15.7 %scatter_custom_fusion.6 = f32[896,256]{1,0:T(8,128)} fusion(s32[2560]{0:T(1024)S(1)} %fusion.106, f32[2560,256]{1,0:T(8,128)} %bitcast.143, f32[]{:T(128)} %constant.105.clone.5..sunk), kind=kCustom, calls=%fused_computation.21.clone.1 | custom fusion | flops 655360 | bytes 918016 | tf_op jit(solution)/shard_map/while/body/eval_jaxpr/scatter-add | solution.py:150
  679.8 8.1 gather_fusion
  737.6 15.7 %scatter_custom_fusion.6 = f32[896,256]{1,0:T(8,128)} fusion(s32[2560]{0:T(1024)S(1)} %fusion.106, f32[2560,256]{1,0:T(8,128)} %bitcast.143, f32[]{:T(128)} %constant.105.clone.5..sunk), kind=kCustom, calls=%fused_computation.21.clone.1 | custom fusion | flops 655360 | bytes 918016 | tf_op jit(solution)/shard_map/while/body/eval_jaxpr/scatter-add | solution.py:150
  783.0 39.5 %all-reduce = (f32[16,4]{0,1:T(4,128)}, f32[4]{0:T(128)}) all-reduce(f32[16,4]{0,1:T(4,128)S(1)} %fusion.22, f32[4]{0:T(128)S(1)} %select_reduce_fusion), channel_id=1, replica_groups=mesh['groups'=2,'atoms'=8,'samples'=2] {'atoms','samples'}, use_global_device_ids=true, to_apply=%region_9.10 | all-reduce | flops 68 | bytes 544 | tf_op jit(solution)/shard_map/psum | solution.py:181
  836.4 7.8 copy.54
  857.2 83.5 %all-reduce.7.cloned.1.call-done = (f32[1,128,128]{2,1,0:T(8,128)}, f32[4,128,128]{2,1,0:T(8,128)}) async-done(((f32[1,128,128]{2,1,0:T(8,128)}, f32[4,128,128]{2,1,0:T(8,128)}), (f32[1,128,128]{2,1,0:T(8,128)}, f32[4,128,128]{2,1,0:T(8,128)})) %all-reduce.7.cloned.1.call-update) | async-done | bytes 327696 | tf_op jit(solution)/shard_map/psum | solution.py:181
  (446 shorter events, 576.4 us)
Async XLA Ops:
  7.2 65.1 %copy-start = (bf16[20,32,16,128]{3,2,1,0:T(8,128)(2,1)S(1)}, bf16[20,32,16,128]{3,2,1,0:T(8,128)(2,1)}, u32[]{:S(2)}) copy-start(bf16[20,32,16,128]{3,2,1,0:T(8,128)(2,1)} %param.21) | copy-start | bytes 7864324
  7.2 847.5 %all-reduce.5.cloned.1.call-start = ((), (), s32[]{:S(2)}) async-start(), calls=%async_computation | async-start | bytes 1310720 | tf_op jit(solution)/shard_map/psum | solution.py:189
  33.9 13.9 %copy-start.9 = (bf16[8,640,512]{2,1,0:T(8,128)(2,1)}, bf16[8,640,512]{2,1,0:T(8,128)(2,1)S(1)}, u32[]{:S(2)}) copy-start(bf16[8,640,512]{2,1,0:T(8,128)(2,1)S(1)} %convert.8) | copy-start | bytes 15728644
  33.9 8.0 copy-start.16
  35.1 39.1 %collective-permute-start.2 = (bf16[8,128,256]{2,1,0:T(8,128)(2,1)}, bf16[8,128,256]{2,1,0:T(8,128)(2,1)S(1)}, u32[]{:S(2)}, u32[]{:S(2)}) collective-permute-start(bf16[8,128,256]{2,1,0:T(8,128)(2,1)} %get-tuple-element.218), channel_id=1, source_target_pairs={{0,2},{2,4},{4,6},{6,8},{8,10},{10,12},{12,14},{1,3},{3,5},{5,7},{... | collective-permute-start | bytes 1572872 | tf_op jit(solution)/shard_map/ppermute | solution.py:18
  39.9 34.2 %collective-permute-start.3 = (bf16[8,128,256]{2,1,0:T(8,128)(2,1)}, bf16[8,128,256]{2,1,0:T(8,128)(2,1)}, u32[]{:S(2)}, u32[]{:S(2)}) collective-permute-start(bf16[8,128,256]{2,1,0:T(8,128)(2,1)} %get-tuple-element.219), channel_id=1, source_target_pairs={{2,0},{4,2},{6,4},{8,6},{10,8},{12,10},{14,12},{3,1},{5,3},{7,5},{... | collective-permute-start | bytes 1572872 | tf_op jit(solution)/shard_map/ppermute | solution.py:19
  41.9 20.7 %collective-permute-start = (s32[128]{0:T(128)S(1)}, s32[128]{0:T(128)S(1)}, u32[]{:S(2)}, u32[]{:S(2)}) collective-permute-start(s32[128]{0:T(128)S(1)} %get-tuple-element.226), channel_id=1, source_target_pairs={{0,2},{2,4},{4,6},{6,8},{8,10},{10,12},{12,14},{1,3},{3,5},{5,7},{... | collective-permute-start | bytes 1544 | tf_op jit(solution)/shard_map/ppermute | solution.py:18
  46.5 16.2 %collective-permute-start.1 = (s32[128]{0:T(128)S(1)}, s32[128]{0:T(128)S(1)}, u32[]{:S(2)}, u32[]{:S(2)}) collective-permute-start(s32[128]{0:T(128)S(1)} %get-tuple-element.227), channel_id=1, source_target_pairs={{2,0},{4,2},{6,4},{8,6},{10,8},{12,10},{14,12},{3,1},{5,3},{7,5},{... | collective-permute-start | bytes 1544 | tf_op jit(solution)/shard_map/ppermute | solution.py:19
  62.6 9.6 %copy-start.17 = (bf16[16,4]{0,1:T(4,128)(2,1)S(1)}, bf16[16,4]{0,1:T(4,128)(2,1)}, u32[]{:S(2)}) copy-start(bf16[16,4]{0,1:T(4,128)(2,1)} %param.27) | copy-start | bytes 388
  62.6 9.6 %copy-start.18 = (f32[4]{0:T(128)S(1)}, f32[4]{0:T(128)}, u32[]{:S(2)}) copy-start(f32[4]{0:T(128)} %param.28) | copy-start | bytes 52
  99.3 7.5 copy-start.10
  184.8 7.5 copy-start.10
  270.6 7.5 copy-start.10
  356.5 7.5 copy-start.10
  442.4 7.5 copy-start.10
  528.2 7.5 copy-start.10
  614.1 7.5 copy-start.10
  700.0 7.5 copy-start.10
  764.6 11.0 %copy-start.8 = (f32[8,896,256]{1,2,0:T(8,128)S(1)}, f32[8,896,256]{1,2,0:T(8,128)}, u32[]{:S(2)}) copy-start(f32[8,896,256]{1,2,0:T(8,128)} %get-tuple-element.101) | copy-start | bytes 22020100
  768.3 5.7 copy-start.6
  769.6 55.8 %collective-permute-start.4 = (bf16[8,128,256]{1,2,0:T(8,128)(2,1)}, bf16[8,128,256]{1,2,0:T(8,128)(2,1)S(1)}, u32[]{:S(2)}, u32[]{:S(2)}) collective-permute-start(bf16[8,128,256]{1,2,0:T(8,128)(2,1)} %get-tuple-element.221), channel_id=1, source_target_pairs={{0,2},{2,4},{4,6},{6,8},{8,10},{10,12},{12,14},{1,3},{3,5},{5,7},{... | collective-permute-start | bytes 1572872 | tf_op jit(solution)/shard_map/ppermute | solution.py:27
  780.1 47.7 %collective-permute-start.5 = (bf16[8,128,256]{1,2,0:T(8,128)(2,1)}, bf16[8,128,256]{1,2,0:T(8,128)(2,1)}, u32[]{:S(2)}, u32[]{:S(2)}) collective-permute-start(bf16[8,128,256]{1,2,0:T(8,128)(2,1)} %get-tuple-element.220), channel_id=1, source_target_pairs={{2,0},{4,2},{6,4},{8,6},{10,8},{12,10},{14,12},{3,1},{5,3},{7,5},{... | collective-permute-start | bytes 1572872 | tf_op jit(solution)/shard_map/ppermute | solution.py:27
  781.4 159.4 %all-reduce.7.cloned.1.call-start = ((), (), s32[]{:S(2)}) async-start(), calls=%async_computation.1 | async-start | bytes 655360 | tf_op jit(solution)/shard_map/psum | solution.py:181
  844.3 5.3 copy-start.14
  (54 other events, 143.3 us)
Sparse Core Ops, SparseCore 0:
  781.5 22.2 all-reduce.4
  854.7 85.9 all-reduce.6
where the time goes:
time: 956 us; the launch traced here: 949 us
  local copies, waits for them, and re-layouts  353 us (37%)
  other arithmetic  235 us (25%)
  matrix products  197 us (21%)
  waiting for transfers between devices  90.2 us (9%)
  blocking collectives  39.5 us (4%)
  starting transfers between devices  17.7 us (2%)
  between operations  15 us (2%)
    scatter-add x8, other arithmetic, one_sample(): jnp.zeros(sample_kv.shape, jnp.float32).at[key_rows].add(d_windowed)  125 us
    psum x1, waiting for transfers between devices, per_device(): lax.psum((weight_part, out_part, pair_weight_part, token_part), ('atoms',...  83.5 us
    dynamic_update_slice x48, local copies, waits for them, and re-layouts, per_device(): lax.scan(one_sample, jnp.zeros(pair_bias.shape, jnp.float32), (query, wid...  71.6 us
    gather x8, local copies, waits for them, and re-layouts, one_sample(): windowed = sample_kv[key_rows]  65.1 us
    dot_general x8, matrix products, attend(): jnp.einsum('whij,wjhd->wihd', probs_b, value_heads, preferred_element_typ...  60.3 us
    dot_general x8, matrix products, attend(): jnp.einsum('whij,wihd->wjhd', probs_b, attended_heads, preferred_element_...  59.8 us
    psum x1, blocking collectives, per_device(): lax.psum((weight_part, out_part, pair_weight_part, token_part), ('atoms',...  39.5 us
    while x128, local copies, waits for them, and re-layouts  28 us
  transfers between devices with their start and end apart: 8, of which 2 were waited for; matrix products, arithmetic and copies ran while one was open for 6% of the time, Pallas kernels for 0%

commit v1 on v0

v1 whole, which is shorter than its diff:
```python
import functools
import math

import jax
import jax.numpy as jnp
from jax import lax
from jax.experimental import pallas as pl
from jax.experimental.pallas import tpu as pltpu
from jax.sharding import PartitionSpec as P

BF16 = jnp.bfloat16
F32 = jnp.float32
MASKED = -1000000000.0
LOG2E = math.log2(math.e)
CODE_ROWS = 16
CODE_BASE = 128
SMALL_ROWS = 16
VMEM_LIMIT = 56 * 1024 * 1024


def dot(a, b):
    return lax.dot_general(a, b, (((1,), (0,)), ((), ())), preferred_element_type=F32)


def dot_nt(a, b):
    return lax.dot_general(a, b, (((1,), (1,)), ((), ())), preferred_element_type=F32)


def dot_tn(a, b):
    return lax.dot_general(a, b, (((0,), (0,)), ((), ())), preferred_element_type=F32)


def column_of(row, span):
    return jnp.broadcast_to(row, (span, row.shape[-1])).T


class Side:
    def __init__(self, windows, query_row, rows, pieces, origin):
        self.windows = windows
        self.query_row = query_row
        self.rows = rows
        self.pieces = pieces
        self.origin = origin


def attention_kernel(geo, sides, edge, *refs):
    samples, atoms, channels, heads, win_rows, span, cp, out_half = geo
    refs = list(refs)
    take = lambda n: [refs.pop(0) for _ in range(n)]
    meta_ref, wtok_ref = take(2)
    act_ref, gout_ref, codes_ref, qcode_ref, pair_hbm = take(5)
    wq_ref, wk_ref, wv_ref, wg_ref, wo_ref, wpair_ref = take(6)
    if edge:
        lo_ref, hi_ref, ga_in_ref, acc_in_ref = take(4)
        ga_ref, ga_lo_ref, ga_hi_ref, acc_ref, mine_ref, other_ref = take(6)
    else:
        ga_ref, acc_ref, mine_ref, other_ref = take(4)
    pair_ref, pair_sem, wexp_ref, pw_ref, code_ref, q_ref, datt_ref, g_ref, gy_ref = take(9)
    dq_ref, dgate_ref, gated_ref, bias_ref, bsum_ref = take(5)
    n_blocks = len(sides) * samples
    k_refs = take(n_blocks)
    v_refs = take(n_blocks)
    dk_refs = take(n_blocks)
    dv_refs = take(n_blocks)

    half_rows = win_rows // 2
    head_dim = channels // heads
    scale = 1.0 / math.sqrt(head_dim)
    halo = {"lo": None, "hi": None}
    if edge:
        halo = {"lo": lo_ref, "hi": hi_ref}

    copies = []
    first = 0
    for n, side in enumerate(sides):
        count = len(side.windows)
        copies.append(
            pltpu.make_async_copy(
                pair_hbm.at[pl.ds(side.windows[0], count)],
                pair_ref.at[pl.ds(first, count)],
                pair_sem.at[n],
            )
        )
        first += count
    for copy in copies:
        copy.start()

    def act_piece(source, row, rows, s):
        if source == "act":
            return act_ref[s, row : row + rows, :]
        return halo[source][s * span : s * span + rows, :]

    lane = lax.broadcasted_iota(jnp.int32, (1, channels), 1)
    head_masks = [(lane // head_dim == h).astype(F32) for h in range(heads)]
    head_masks_b = [m.astype(BF16) for m in head_masks]

    lanes = 2 * heads * half_rows
    s_lane = lax.broadcasted_iota(jnp.int32, (1, lanes), 1)
    lane_head = (s_lane // half_rows) % heads
    lane_row = (s_lane // (heads * half_rows)) * half_rows + s_lane % half_rows
    wtok = jnp.zeros((1, lanes), F32)
    for h in range(heads):
        wtok = jnp.where(lane_head == h, wtok_ref[h], wtok)
    pick = (
        lax.broadcasted_iota(jnp.int32, (heads, lanes), 0)
        == (lax.broadcasted_iota(jnp.int32, (heads, lanes), 1) // half_rows) % heads
    ).astype(BF16)
    wlane = dot(wpair_ref[...], pick).astype(BF16)
    for i in range(win_rows):
        wexp_ref[i * cp : (i + 1) * cp, :] = jnp.where(lane_row == i, wlane, 0.0).astype(BF16)
    pw_ref[...] = jnp.zeros_like(pw_ref)

    for n, side in enumerate(sides):
        for source, row, rows, at in side.pieces:
            for r in range(0, rows, span):
                if source == "act":
                    code_row = codes_ref[:, row + r : row + r + span]
                else:
                    two = halo[source][samples * span : samples * span + CODE_ROWS, :].astype(F32)
                    code_row = two[0:1, :] * CODE_BASE + two[1:2, :]
                code_ref[n, at + r : at + r + span, :] = column_of(code_row, span)

    w_kv = jnp.concatenate([wk_ref[...], wv_ref[...]], axis=1)
    w_qg = jnp.concatenate([wq_ref[...], wg_ref[...]], axis=1)
    for n, side in enumerate(sides):
        queries = len(side.windows) * win_rows
        for s in range(samples):
            block = n * samples + s
            for source, row, rows, at in side.pieces:
                kv = dot(act_piece(source, row, rows, s), w_kv)
                k_refs[block][at : at + rows, :] = kv[:, :channels]
                v_refs[block][at : at + rows, :] = kv[:, channels:]
            dk_refs[block][...] = jnp.zeros_like(dk_refs[block])
            dv_refs[block][...] = jnp.zeros_like(dv_refs[block])
            qrow = side.query_row
            qg = dot(act_ref[s, qrow : qrow + queries, :], w_qg)
            q_ref[block] = qg[:, :channels].astype(BF16)
            gate = jax.nn.sigmoid(qg[:, channels:])
            gy = dot_nt(gout_ref[s, qrow : qrow + queries, :], wo_ref[...])
            g_ref[block] = gate
            gy_ref[block] = gy
            datt_ref[block] = (gy * gate).astype(BF16)

    for copy in copies:
        copy.wait()

    def by_head(rows):
        return jnp.concatenate(
            [
                rows[half * half_rows : (half + 1) * half_rows] * head_masks_b[h]
                for half in range(2)
                for h in range(heads)
            ],
            axis=0,
        )

    def own_head(wide):
        halves = []
        for half in range(2):
            total = None
            for h in range(heads):
                at = (half * heads + h) * half_rows
                term = wide[at : at + half_rows] * head_masks[h]
                total = term if total is None else total + term
            halves.append(total)
        return jnp.concatenate(halves, axis=0)

    def one_window(n, side, first, w, tok_sum):
        slot = first + w
        start = meta_ref[side.windows[0] + w] - side.origin
        key_codes = code_ref[n, pl.ds(start, span), :]
        same = key_codes == qcode_ref[pl.ds(side.windows[0] + w, 1), :]
        pair_w = pair_ref[slot]
        bias = dot_tn(pair_w, wexp_ref[...]) + jnp.where(same, wtok, 0.0)
        bias_ref[...] = jnp.where(key_codes > 0.0, bias, MASKED) * LOG2E
        qrows = pl.ds(pl.multiple_of(w * win_rows, win_rows), win_rows)
        for s in range(samples):
            block = n * samples + s
            keys = pl.ds(start, span)
            kb = k_refs[block][keys, :].astype(BF16)
            vb = v_refs[block][keys, :].astype(BF16)
            qh = by_head(q_ref[block, qrows, :])
            dh = by_head(datt_ref[block, qrows, :])
            x = dot_nt(kb, qh) * (scale * LOG2E) + bias_ref[...]
            dp = dot_nt(vb, dh)
            e = jnp.exp2(x - jnp.max(x, axis=0, keepdims=True))
            p = e * (1.0 / jnp.sum(e, axis=0, keepdims=True))
            t = p * dp
            ds = t - p * jnp.sum(t, axis=0, keepdims=True)
            if s == 0:
                bsum_ref[...] = ds
            else:
                bsum_ref[...] += ds
            pb = p.astype(BF16)
            dsb = ds.astype(BF16)
            dk_refs[block][keys, :] += dot(dsb, qh)
            dv_refs[block][keys, :] += dot(pb, dh)
            att = own_head(dot_tn(pb, vb))
            dq_ref[block, qrows, :] = (own_head(dot_tn(dsb, kb)) * scale).astype(BF16)
            gate = g_ref[block, qrows, :]
            ga = gate * att
            gated_ref[block, qrows, :] = ga.astype(BF16)
            dgate_ref[block, qrows, :] = (gy_ref[block, qrows, :] * ga * (1.0 - gate)).astype(BF16)
        total = bsum_ref[...]
        total_b = total.astype(BF16)
        pw_ref[...] += dot(pair_w, total_b)
        straight = total.T
        bsum_ref[...] = straight
        core = meta_ref[meta_ref.shape[0] - 1]
        width = heads * half_rows
        mine_ref[slot] = bsum_ref[pl.ds(pl.multiple_of(core * width, width), width), :]
        other_ref[slot] = bsum_ref[
            pl.ds(pl.multiple_of((1 - core) * width, width), width), :
        ].astype(BF16)
        return tok_sum + jnp.sum(jnp.where(same, total, 0.0), axis=0, keepdims=True)

    tok_sum = jnp.zeros((1, lanes), F32)
    first = 0
    for n, side in enumerate(sides):
        count = len(side.windows)
        tok_sum = lax.fori_loop(
            0, count, functools.partial(one_window, n, side, first), tok_sum
        )
        first += count

    if edge:
        ga_ref[...] = ga_in_ref[...]
    acc_kv = jnp.zeros((channels, 2 * channels), F32)
    acc_qg = jnp.zeros((channels, 2 * channels), F32)
    acc_o = jnp.zeros((channels, channels), F32)
    for n, side in enumerate(sides):
        queries = len(side.windows) * win_rows
        qrow = side.query_row
        for s in range(samples):
            block = n * samples + s
            for source, row, rows, at in side.pieces:
                dk = dk_refs[block][at : at + rows, :] * scale
                dv = dv_refs[block][at : at + rows, :]
                dkv_b = jnp.concatenate([dk.astype(BF16), dv.astype(BF16)], axis=1)
                part = dot_nt(dkv_b, w_kv)
                if source == "lo":
                    ga_lo_ref[s] = part.astype(BF16)
                elif source == "hi":
                    ga_hi_ref[s] = part.astype(BF16)
                elif edge:
                    ga_ref[s, row : row + rows, :] += part
                else:
                    ga_ref[s, row : row + rows, :] = part
                acc_kv = acc_kv + dot_tn(act_piece(source, row, rows, s), dkv_b)
            dqg = jnp.concatenate([dq_ref[block], dgate_ref[block]], axis=1)
            ga_ref[s, qrow : qrow + queries, :] += dot_nt(dqg, w_qg)
            acc_qg = acc_qg + dot_tn(act_ref[s, qrow : qrow + queries, :], dqg)
            acc_o = acc_o + dot_tn(gated_ref[block], gout_ref[s, qrow : qrow + queries, :])

    diag = lax.broadcasted_iota(jnp.int32, (win_rows * cp, lanes), 0) // cp == lane_row
    pw = jnp.where(diag, pw_ref[...], 0.0).reshape(win_rows, cp, lanes).sum(axis=0)
    parts = [
        acc_qg[:, :channels],
        acc_kv[:, :channels],
        acc_kv[:, channels:],
        acc_qg[:, channels:],
        acc_o,
    ]
    first_half, second_half = [], []
    left = out_half
    for part in parts:
        if left >= channels:
            first_half.append(part)
            left -= channels
        elif left > 0:
            first_half.append(part[:left])
            second_half.append(part[left:])
            left = 0
        else:
            second_half.append(part)
    tok_rows = jnp.where(
        lax.broadcasted_iota(jnp.int32, (SMALL_ROWS, lanes), 0) == 0, tok_sum, 0.0
    )
    at = 0
    for part in first_half + [pw] + second_half + [tok_rows]:
        rows = part.shape[0]
        if edge:
            acc_ref[at : at + rows, :] = part + acc_in_ref[at : at + rows, :]
        else:
            acc_ref[at : at + rows, :] = part
        at += rows


def pair_kernel(wpair_ref, m1_ref, r1_ref, m2_ref, r2_ref, out_ref, *, order, heads, cp):
    rows = m1_ref.shape[1]
    half_rows = rows // heads
    lane = lax.broadcasted_iota(jnp.int32, (1, rows), 1)
    pick = (
        lax.broadcasted_iota(jnp.int32, (heads, rows), 0)
        == lax.broadcasted_iota(jnp.int32, (heads, rows), 1) // half_rows
    ).astype(BF16)
    wlane = dot(wpair_ref[...], pick)
    wexp = jnp.concatenate(
        [jnp.where(lane % half_rows == i, wlane, 0.0) for i in range(half_rows)], axis=0
    ).astype(BF16)
    for which, (m_ref, r_ref) in enumerate(((m1_ref, r1_ref), (m2_ref, r2_ref))):
        for slot, window in enumerate(order[which]):
            total = (m_ref[slot] + r_ref[slot].astype(F32)).astype(BF16)
            out_ref[window] = dot(wexp, total).astype(BF16)


def per_device(
    act,
    grad_out,
    pair,
    w_query,
    w_key,
    w_value,
    w_gate,
    w_out,
    w_pair,
    w_token,
    offsets,
    atom_token,
    padding,
):
    samples, atoms, channels = act.shape
    windows = offsets.shape[0]
    win_rows = atoms // windows
    span = pair.shape[-1]
    cp, heads = w_pair.shape
    half_rows = win_rows // 2
    lanes = heads * win_rows
    ranges = lax.axis_size("atoms")
    cores = lax.axis_size("samples")
    assert cores == 2 and ranges & (ranges - 1) == 0
    core = lax.axis_index("samples")
    anchor = lax.axis_index("atoms") * atoms
    position = jnp.arange(atoms, dtype=jnp.int32)
    codes = jnp.where(position < atoms - padding[0], atom_token + 1, 0)
    starts = (
        jnp.clip(
            anchor + win_rows * jnp.arange(windows, dtype=jnp.int32) + offsets,
            0,
            ranges * atoms - span,
        )
        - anchor
    )
    edge_count = span // win_rows
    inner = tuple(range(edge_count, windows - edge_count))
    low, high = tuple(range(edge_count)), tuple(range(windows - edge_count, windows))
    own = edge_count * win_rows + span
    edge_rows = own + span
    index = jnp.arange(windows, dtype=jnp.int32)
    low_limit = jnp.where(
        index < edge_count, -span, jnp.where(index < windows - edge_count, 0, atoms - own)
    )
    high_limit = jnp.where(
        index < edge_count,
        own - span,
        jnp.where(index < windows - edge_count, atoms - span, atoms),
    )
    starts = jnp.clip(starts, low_limit, high_limit)
    meta = jnp.concatenate([starts, core[None].astype(jnp.int32)])
    qcode = jnp.broadcast_to(
        (atom_token + 1).astype(F32).reshape(windows, 2, 1, half_rows),
        (windows, 2, heads, half_rows),
    ).reshape(windows, lanes)
    codes_f = codes.astype(F32).reshape(1, atoms)

    def payload(first):
        part = lax.slice_in_dim(act, first, first + span, axis=1).reshape(-1, channels)
        code = lax.slice_in_dim(codes, first, first + span)[None]
        extra = jnp.concatenate(
            [code // CODE_BASE, code % CODE_BASE, jnp.zeros((CODE_ROWS - 2, span), jnp.int32)]
        )
        return jnp.concatenate([part, extra.astype(BF16)])

    up = [(i, i + 1) for i in range(ranges - 1)]
    down = [(j, i) for i, j in up]
    halo_lo = lax.ppermute(payload(atoms - span), "atoms", up)
    halo_hi = lax.ppermute(payload(0), "atoms", down)

    out_half = 5 * channels // 2
    acc_rows = 5 * channels + 2 * SMALL_ROWS
    geo = (samples, atoms, channels, heads, win_rows, span, cp, out_half)
    pair_flat = pair.reshape(windows, win_rows * cp, span)
    vmem = pl.BlockSpec(memory_space=pltpu.VMEM)
    smem = pl.BlockSpec(memory_space=pltpu.SMEM)
    hbm = pl.BlockSpec(memory_space=pl.ANY)
    width = heads * half_rows

    def call(sides, edge, args):
        count = sum(len(side.windows) for side in sides)
        queries = len(sides[0].windows) * win_rows
        rows = sides[0].rows
        blocks = len(sides) * samples
        out_shape = [jax.ShapeDtypeStruct((samples, atoms, channels), F32)]
        if edge:
            out_shape += [jax.ShapeDtypeStruct((samples, span, channels), BF16)] * 2
        out_shape += [
            jax.ShapeDtypeStruct((acc_rows, channels), F32),
            jax.ShapeDtypeStruct((count, width, span), F32),
            jax.ShapeDtypeStruct((count, width, span), BF16),
        ]
        per_query = (blocks, queries, channels)
        scratch = [
            pltpu.VMEM((count, win_rows * cp, span), BF16),
            pltpu.SemaphoreType.DMA((len(sides),)),
            pltpu.VMEM((win_rows * cp, lanes), BF16),
            pltpu.VMEM((win_rows * cp, lanes), F32),
            pltpu.VMEM((len(sides), rows, span), F32),
            pltpu.VMEM(per_query, BF16),
            pltpu.VMEM(per_query, BF16),
            pltpu.VMEM(per_query, F32),
            pltpu.VMEM(per_query, F32),
            pltpu.VMEM(per_query, BF16),
            pltpu.VMEM(per_query, BF16),
            pltpu.VMEM(per_query, BF16),
            pltpu.VMEM((span, lanes), F32),
            pltpu.VMEM((span, lanes), F32),
        ]
        scratch += [pltpu.VMEM((rows, channels), F32)] * (4 * blocks)
        units = 6 * count * samples + 8 * count + 14 * blocks
        return pl.pallas_call(
            functools.partial(attention_kernel, geo, sides, edge),
            out_shape=out_shape,
            in_specs=[smem] * 2 + [vmem] * 4 + [hbm] + [vmem] * (len(args) - 7),
            out_specs=[vmem] * len(out_shape),
            scratch_shapes=scratch,
            compiler_params=pltpu.CompilerParams(vmem_limit_bytes=VMEM_LIMIT),
            cost_estimate=pl.CostEstimate(
                flops=2 * units * 128 * 128 * 128 * 4,
                bytes_accessed=12_000_000,
                transcendentals=count * samples * span * lanes,
            ),
        )(*args)

    common = (
        meta,
        w_token,
        act,
        grad_out,
        codes_f,
        qcode,
        pair_flat,
        w_query,
        w_key,
        w_value,
        w_gate,
        w_out,
        w_pair,
    )
    inner_side = Side(inner, span, atoms, [("act", 0, atoms, 0)], 0)
    ga1, acc1, mine1, other1 = call([inner_side], False, common)
    swap = [(0, 1), (1, 0)]
    recv1 = lax.ppermute(other1, "samples", swap)

    low_side = Side(low, 0, edge_rows, [("lo", 0, span, 0), ("act", 0, own, span)], -span)
    high_side = Side(
        high,
        atoms - span,
        edge_rows,
        [("act", atoms - own, own, 0), ("hi", 0, span, own)],
        atoms - own,
    )
    ga2, ga_lo, ga_hi, acc, mine2, other2 = call(
        [low_side, high_side], True, common + (halo_lo, halo_hi, ga1, acc1)
    )
    recv2 = lax.ppermute(other2, "samples", swap)
    from_upper = lax.ppermute(ga_lo, "atoms", down)
    from_lower = lax.ppermute(ga_hi, "atoms", up)

    part_rows = acc_rows // 2
    wide = part_rows - SMALL_ROWS

    def encode(value):
        big, small = value[:wide].astype(BF16), value[wide:]
        top = small.astype(BF16)
        return jnp.concatenate([big, top, (small - top.astype(F32)).astype(BF16)])

    def decode(sent):
        sent = sent.astype(F32)
        return jnp.concatenate(
            [sent[:wide], sent[wide : wide + SMALL_ROWS] + sent[wide + SMALL_ROWS :]]
        )

    acc = acc.reshape(2, part_rows, channels)
    mine = encode(lax.dynamic_index_in_dim(acc, core, 0, keepdims=False))
    other = encode(lax.dynamic_index_in_dim(acc, 1 - core, 0, keepdims=False))
    total = decode(mine) + decode(lax.ppermute(other, "samples", swap))
    step = 1
    while step < ranges:
        sent = encode(total)
        got = lax.ppermute(sent, "atoms", [(i, i ^ step) for i in range(ranges)])
        total = decode(sent) + decode(got)
        step *= 2
    sent = encode(total)
    got = lax.ppermute(sent, "samples", swap)
    is_first = core == 0
    first = decode(jnp.where(is_first, sent, got))
    second = decode(jnp.where(is_first, got, sent))
    grad_weights = jnp.concatenate([first[:wide], second[:wide]]).reshape(5, channels, channels)
    grad_pair_weight = first[wide:].reshape(cp, 2, heads, half_rows).sum(axis=(1, 3))
    grad_token_weight = second[wide].reshape(2, heads, half_rows).sum(axis=(0, 2))

    grad_pair = pl.pallas_call(
        functools.partial(pair_kernel, order=(inner, low + high), heads=heads, cp=cp),
        out_shape=jax.ShapeDtypeStruct((windows, half_rows * cp, span), BF16),
        in_specs=[vmem] * 5,
        out_specs=vmem,
        compiler_params=pltpu.CompilerParams(vmem_limit_bytes=VMEM_LIMIT),
        cost_estimate=pl.CostEstimate(
            flops=2 * windows * 256 * 256 * 256, bytes_accessed=4_000_000, transcendentals=0
        ),
    )(w_pair, mine1, recv1, mine2, recv2).reshape(windows, half_rows, cp, span)

    grad_act = (
        ga2.at[:, :span]
        .add(from_lower.astype(F32))
        .at[:, atoms - span :]
        .add(from_upper.astype(F32))
        .astype(BF16)
    )
    return (grad_act, grad_pair, grad_weights, grad_pair_weight, grad_token_weight)


def solution(mesh):
    in_specs = (
        P("samples", ("groups", "atoms"), None),
        P("samples", ("groups", "atoms"), None),
        P(("groups", "atoms"), None, None, None),
        P(),
        P(),
        P(),
        P(),
        P(),
        P(),
        P(),
        P(("groups", "atoms")),
        P(("groups", "atoms")),
        P(("groups", "atoms")),
    )
    out_specs = (
        P("samples", ("groups", "atoms"), None),
        P(("groups", "atoms"), "samples", None, None),
        P("groups", None, None),
        P("groups", None),
        P("groups"),
    )
    return jax.shard_map(
        per_device, mesh=mesh, in_specs=in_specs, out_specs=out_specs, check_vma=False
    )
```

time: 956 us -> 122 us (0.13)
  local copies, waits for them, and re-layouts: 353 us -> 7.84 us
  other arithmetic: 235 us -> 6.12 us
  matrix products: 197 us -> 0 us
  waiting for transfers between devices: 90.2 us -> 12.6 us
  Pallas kernels: 0 us -> 69.6 us
  blocking collectives: 39.5 us -> 0 us
  between operations: 15 us -> 1.84 us
    dot_general x56 -> x0, matrix products: 197 us -> none  [the longest x8 60.3 us: attend(): jnp.einsum('whij,wjhd->wihd', probs_b, value_heads, preferred_element_typ...]
    scatter-add x10 -> x2, other arithmetic: 130 us -> 0.25 us  [per_device(): grad_act = ga2.at[:, :span].add(from_lower.astype(F32)).at[:, atoms - spa...]
    psum x2 -> x0, waiting for transfers between devices: 83.5 us -> none  [the longest x1 83.5 us: per_device(): lax.psum((weight_part, out_part, pair_weight_part, token_part), ('atoms',...]
    gather x9 -> x0, local copies, waits for them, and re-layouts: 74.5 us -> none  [the longest x8 65.1 us: one_sample(): windowed = sample_kv[key_rows]]
    dynamic_update_slice x48 -> x0, local copies, waits for them, and re-layouts: 71.6 us -> none  [per_device(): lax.scan(one_sample, jnp.zeros(pair_bias.shape, jnp.float32), (query, wid...]
    pallas_call x0 -> x3, Pallas kernels: none -> 69.6 us  [the longest x2 66.8 us: call(): pl.pallas_call(functools.partial(attention_kernel, geo, sides, edge), out...]
    reshape x26 -> x3, local copies, waits for them, and re-layouts: 47.5 us -> 1.38 us  [the longest x1 0.71 us: per_device(): qcode = jnp.broadcast_to((atom_token + 1).astype(F32).reshape(windows, 2,...]
    convert_element_type x17 -> x20, other arithmetic: 46.1 us -> 2.96 us  [the longest x1 1.27 us: per_device(): grad_act = ga2.at[:, :span].add(from_lower.astype(F32)).at[:, atoms - spa...]
  transfers between devices with their start and end apart: 8 -> 11, of which waited for: 2 -> 3; matrix products, arithmetic and copies ran while one was open for 6% -> 7% of each run, Pallas kernels for 0% -> 57%
where the time goes in v1:
time: 122 us; the launch traced here: 121 us
  Pallas kernels  69.6 us (57%)
  starting transfers between devices  23.1 us (19%)
  waiting for transfers between devices  12.6 us (10%)
  local copies, waits for them, and re-layouts  7.84 us (6%)
  other arithmetic  6.12 us (5%)
  between operations  1.84 us (2%)
    pallas_call x2, Pallas kernels, call(): pl.pallas_call(functools.partial(attention_kernel, geo, sides, edge), out...  66.8 us
    ppermute x3, waiting for transfers between devices, per_device(): got = lax.ppermute(sent, 'atoms', [(i, i ^ step) for i in range(ranges)])  12.6 us
    ppermute x3, starting transfers between devices, per_device(): got = lax.ppermute(sent, 'atoms', [(i, i ^ step) for i in range(ranges)])  10.3 us
    ppermute x1, starting transfers between devices, per_device(): halo_lo = lax.ppermute(payload(atoms - span), 'atoms', up)  4.86 us
    ppermute x1, starting transfers between devices, per_device(): from_lower = lax.ppermute(ga_hi, 'atoms', up)  4.61 us
    unnamed x12, local copies, waits for them, and re-layouts  3.51 us
    pallas_call x1, Pallas kernels, per_device(): pl.pallas_call(functools.partial(pair_kernel, order=(inner, low + high),...  2.82 us
  transfers between devices with their start and end apart: 11, of which 3 were waited for; matrix products, arithmetic and copies ran while one was open for 7% of the time, Pallas kernels for 57%

profile of v1, /device:TPU:0, one launch (start us, length us, event | category | flops | bytes accessed | tf_op | source)
XLA Modules:
  0.0 121.1 jit_solution(5542233422643655640)
XLA Ops:
  1.3 0.7 fusion.22
  2.0 1.1 fusion.24
  3.4 4.9 %collective-permute-start = (bf16[1040,128]{1,0:T(8,128)(2,1)S(1)}, bf16[1040,128]{1,0:T(8,128)(2,1)S(1)}, u32[]{:S(2)}, u32[]{:S(2)}) collective-permute-start(bf16[1040,128]{1,0:T(8,128)(2,1)S(1)} %concatenate.65), channel_id=1, source_target_pairs={{0,2},{2,4},{4,6},{6,8},{8,10},{10,12},{12,14},{1,3},{3,5},{5,7},{... | collective-permute-start | bytes 798728 | tf_op jit(solution)/shard_map/ppermute | solution.py:376
  8.5 1.3 %collective-permute-start.1 = (bf16[1040,128]{1,0:T(8,128)(2,1)S(1)}, bf16[1040,128]{1,0:T(8,128)(2,1)S(1)}, u32[]{:S(2)}, u32[]{:S(2)}) collective-permute-start(bf16[1040,128]{1,0:T(8,128)(2,1)S(1)} %concatenate.66), channel_id=1, source_target_pairs={{2,0},{4,2},{6,4},{8,6},{10,8},{12,10},{14,12},{3,1},{5,3},{7,5},{... | collective-permute-start | bytes 798728 | tf_op jit(solution)/shard_map/ppermute | solution.py:377
  9.9 0.7 reshape.160.refs_5_
  11.2 1.4 %copy.25.refs_12_.wpair_ref = bf16[16,4]{1,0:T(8,128)(2,1)} copy(bf16[16,4]{0,1:T(4,128)(2,1)} %param.25) | data formatting | bytes 256 | tf_op args[8]
  12.5 0.7 fusion.6
  13.8 37.9 %shard_map.164 = (f32[8,640,128]{2,1,0:T(8,128)}, f32[672,128]{1,0:T(8,128)}, f32[12,64,128]{2,1,0:T(8,128)}, bf16[12,64,128]{2,1,0:T(8,128)(2,1)}) custom-call(s32[21]{0:T(128)} %pad_add_fusion.refs_0_, f32[4]{0:T(128)} %refs_1_.3, bf16[8,640,128]{2,1,0:T(8,128)(2,1)} %refs_2_.3, bf16[8,640,128]{2,1,0:T(8,128)(2,1)} %refs_3_.3, f32[1,640]{1,0:T(1,128)} %reshape.159.refs_4_, ...), custom_call_target="tpu_custom_call" | custom-call | flops 13153337344 | bytes 12000000 | tf_op jit(solution)/shard_map/pallas_call | solution.py:420
  51.8 0.7 copy-done.1
  52.6 28.9 %shard_map.165 = (f32[8,640,128]{2,1,0:T(8,128)}, bf16[8,128,128]{2,1,0:T(8,128)(2,1)}, bf16[8,128,128]{2,1,0:T(8,128)(2,1)}, f32[672,128]{1,0:T(8,128)}, f32[8,...) custom-call(s32[21]{0:T(128)} %pad_add_fusion.refs_0_, f32[4]{0:T(128)} %refs_1_.3, bf16[8,640,128]{2,1,0:T(8,128)(2,1)} %refs_2_.3, ...), custom_call_target="tpu_custom_call" | custom-call | flops 11274289152 | bytes 12000000 | tf_op jit(solution)/shard_map/pallas_call | solution.py:420
  81.5 1.0 fusion.1
  82.5 0.8 subtract_convert_fusion.5
  84.0 4.6 %collective-permute-start.2 = (bf16[8,128,128]{2,1,0:T(8,128)(2,1)}, bf16[8,128,128]{2,1,0:T(8,128)(2,1)S(1)}, u32[]{:S(2)}, u32[]{:S(2)}) collective-permute-start(bf16[8,128,128]{2,1,0:T(8,128)(2,1)} %get-tuple-element.42), channel_id=1, source_target_pairs={{0,2},{2,4},{4,6},{6,8},{8,10},{10,12},{12,14},{1,3},{3,5},{5,7},{... | collective-permute-start | bytes 786440 | tf_op jit(solution)/shard_map/ppermute | solution.py:467
  88.6 1.3 %collective-permute-start.3 = (bf16[8,128,128]{2,1,0:T(8,128)(2,1)}, bf16[8,128,128]{2,1,0:T(8,128)(2,1)S(1)}, u32[]{:S(2)}, u32[]{:S(2)}) collective-permute-start(bf16[8,128,128]{2,1,0:T(8,128)(2,1)} %get-tuple-element.43), channel_id=1, source_target_pairs={{2,0},{4,2},{6,4},{8,6},{10,8},{12,10},{14,12},{3,1},{5,3},{7,5},{... | collective-permute-start | bytes 786440 | tf_op jit(solution)/shard_map/ppermute | solution.py:466
  90.1 3.1 %collective-permute-start.7 = (bf16[352,128]{1,0:T(8,128)(2,1)S(1)}, bf16[352,128]{1,0:T(8,128)(2,1)S(1)}, u32[]{:S(2)}, u32[]{:S(2)}) collective-permute-start(bf16[352,128]{1,0:T(8,128)(2,1)S(1)} %get-tuple-element.87), channel_id=1, source_target_pairs={{0,2},{2,0},{4,6},{6,4},{8,10},{10,8},{12,14},{14,12},{1,3},{3,1},... | collective-permute-start | bytes 270344 | tf_op jit(solution)/shard_map/ppermute | solution.py:490
  94.0 2.8 %shard_map.166 = bf16[20,256,128]{2,1,0:T(8,128)(2,1)} custom-call(bf16[16,4]{1,0:T(8,128)(2,1)} %copy.25.refs_12_.wpair_ref, f32[12,64,128]{2,1,0:T(8,128)} %get-tuple-element.44.m1_ref, bf16[12,64,128]{2,1,0:T(8,128)(2,1)} %copy-done.3, f32[8,64,128]{2,1,0:T(8,128)} %get-tuple-element.46.m2_ref, bf16[8,64,128]{2,1,0:T(8,128)(2,1)} %copy-done.4), custom_call_target="tpu_custom_call" | custom-call | flops 671088640 | bytes 4000000 | tf_op jit(solution)/shard_map/pallas_call | solution.py:502
  96.8 5.7 %collective-permute-done.7 = bf16[352,128]{1,0:T(8,128)(2,1)S(1)} collective-permute-done((bf16[352,128]{1,0:T(8,128)(2,1)S(1)}, bf16[352,128]{1,0:T(8,128)(2,1)S(1)}, u32[]{:S(2)}, u32[]{:S(2)}) %collective-permute-start.7) | collective-permute-done | bytes 90144 | tf_op jit(solution)/shard_map/ppermute | solution.py:490
  102.7 4.4 %collective-permute-start.8 = (bf16[352,128]{1,0:T(8,128)(2,1)S(1)}, bf16[352,128]{1,0:T(8,128)(2,1)S(1)}, u32[]{:S(2)}, u32[]{:S(2)}) collective-permute-start(bf16[352,128]{1,0:T(8,128)(2,1)S(1)} %get-tuple-element.85), channel_id=1, source_target_pairs={{0,4},{2,6},{4,0},{6,2},{8,12},{10,14},{12,8},{14,10},{1,5},{3,7},... | collective-permute-start | bytes 270344 | tf_op jit(solution)/shard_map/ppermute | solution.py:490
  107.2 2.7 %collective-permute-done.8 = bf16[352,128]{1,0:T(8,128)(2,1)S(1)} collective-permute-done((bf16[352,128]{1,0:T(8,128)(2,1)S(1)}, bf16[352,128]{1,0:T(8,128)(2,1)S(1)}, u32[]{:S(2)}, u32[]{:S(2)}) %collective-permute-start.8) | collective-permute-done | bytes 90144 | tf_op jit(solution)/shard_map/ppermute | solution.py:490
  110.1 2.8 %collective-permute-start.9 = (bf16[352,128]{1,0:T(8,128)(2,1)S(1)}, bf16[352,128]{1,0:T(8,128)(2,1)S(1)}, u32[]{:S(2)}, u32[]{:S(2)}) collective-permute-start(bf16[352,128]{1,0:T(8,128)(2,1)S(1)} %get-tuple-element.83), channel_id=1, source_target_pairs={{0,8},{2,10},{4,12},{6,14},{8,0},{10,2},{12,4},{14,6},{1,9},{3,11}... | collective-permute-start | bytes 270344 | tf_op jit(solution)/shard_map/ppermute | solution.py:490
  112.9 4.1 %collective-permute-done.9 = bf16[352,128]{1,0:T(8,128)(2,1)S(1)} collective-permute-done((bf16[352,128]{1,0:T(8,128)(2,1)S(1)}, bf16[352,128]{1,0:T(8,128)(2,1)S(1)}, u32[]{:S(2)}, u32[]{:S(2)}) %collective-permute-start.9) | collective-permute-done | bytes 90144 | tf_op jit(solution)/shard_map/ppermute | solution.py:490
  117.4 1.3 %convert_element_type.117 = bf16[8,640,128]{2,1,0:T(8,128)(2,1)} convert(f32[8,640,128]{2,1,0:T(8,128)S(1)} %fusion) | non-fusion elementwise | flops 655360 | bytes 3932160 | tf_op jit(solution)/shard_map/convert_element_type | solution.py:518
  119.7 0.7 copy.27
  120.3 0.7 pad_maximum_fusion
  (83 shorter events, 5.1 us)
Async XLA Ops:
  3.4 48.4 %collective-permute-start = (bf16[1040,128]{1,0:T(8,128)(2,1)S(1)}, bf16[1040,128]{1,0:T(8,128)(2,1)S(1)}, u32[]{:S(2)}, u32[]{:S(2)}) collective-permute-start(bf16[1040,128]{1,0:T(8,128)(2,1)S(1)} %concatenate.65), channel_id=1, source_target_pairs={{0,2},{2,4},{4,6},{6,8},{8,10},{10,12},{12,14},{1,3},{3,5},{5,7},{... | collective-permute-start | bytes 798728 | tf_op jit(solution)/shard_map/ppermute | solution.py:376
  8.5 43.3 %collective-permute-start.1 = (bf16[1040,128]{1,0:T(8,128)(2,1)S(1)}, bf16[1040,128]{1,0:T(8,128)(2,1)S(1)}, u32[]{:S(2)}, u32[]{:S(2)}) collective-permute-start(bf16[1040,128]{1,0:T(8,128)(2,1)S(1)} %concatenate.66), channel_id=1, source_target_pairs={{2,0},{4,2},{6,4},{8,6},{10,8},{12,10},{14,12},{3,1},{5,3},{7,5},{... | collective-permute-start | bytes 798728 | tf_op jit(solution)/shard_map/ppermute | solution.py:377
  51.7 41.5 %collective-permute-start.4 = (bf16[12,64,128]{2,1,0:T(8,128)(2,1)}, bf16[12,64,128]{2,1,0:T(8,128)(2,1)S(1)}, u32[]{:S(2)}, u32[]{:S(2)}) collective-permute-start(bf16[12,64,128]{2,1,0:T(8,128)(2,1)} %get-tuple-element.45), channel_id=1, source_target_pairs={{0,1},{1,0},{2,3},{3,2},{4,5},{5,4},{6,7},{7,6},{8,9},{9,8},{10,11... | collective-permute-start | bytes 589832 | tf_op jit(solution)/shard_map/ppermute | solution.py:452
  51.8 0.7 copy-start.1
  51.8 0.8 copy-start.2
  83.4 6.6 %collective-permute-start.6 = (bf16[352,128]{1,0:T(8,128)(2,1)S(1)}, bf16[352,128]{1,0:T(8,128)(2,1)S(1)}, u32[]{:S(2)}, u32[]{:S(2)}) collective-permute-start(bf16[352,128]{1,0:T(8,128)(2,1)S(1)} %pad_maximum_fusion.1), channel_id=1, source_target_pairs={{0,1},{1,0},{2,3},{3,2},{4,5},{5,4},{6,7},{7,6},{8,9},{9,8},{10,11... | collective-permute-start | bytes 270344 | tf_op jit(solution)/shard_map/ppermute | solution.py:486
  83.9 9.3 %collective-permute-start.5 = (bf16[8,64,128]{2,1,0:T(8,128)(2,1)}, bf16[8,64,128]{2,1,0:T(8,128)(2,1)S(1)}, u32[]{:S(2)}, u32[]{:S(2)}) collective-permute-start(bf16[8,64,128]{2,1,0:T(8,128)(2,1)} %get-tuple-element.47), channel_id=1, source_target_pairs={{0,1},{1,0},{2,3},{3,2},{4,5},{5,4},{6,7},{7,6},{8,9},{9,8},{10,11... | collective-permute-start | bytes 393224 | tf_op jit(solution)/shard_map/ppermute | solution.py:465
  84.0 23.1 %collective-permute-start.2 = (bf16[8,128,128]{2,1,0:T(8,128)(2,1)}, bf16[8,128,128]{2,1,0:T(8,128)(2,1)S(1)}, u32[]{:S(2)}, u32[]{:S(2)}) collective-permute-start(bf16[8,128,128]{2,1,0:T(8,128)(2,1)} %get-tuple-element.42), channel_id=1, source_target_pairs={{0,2},{2,4},{4,6},{6,8},{8,10},{10,12},{12,14},{1,3},{3,5},{5,7},{... | collective-permute-start | bytes 786440 | tf_op jit(solution)/shard_map/ppermute | solution.py:467
  88.6 28.6 %collective-permute-start.3 = (bf16[8,128,128]{2,1,0:T(8,128)(2,1)}, bf16[8,128,128]{2,1,0:T(8,128)(2,1)S(1)}, u32[]{:S(2)}, u32[]{:S(2)}) collective-permute-start(bf16[8,128,128]{2,1,0:T(8,128)(2,1)} %get-tuple-element.43), channel_id=1, source_target_pairs={{2,0},{4,2},{6,4},{8,6},{10,8},{12,10},{14,12},{3,1},{5,3},{7,5},{... | collective-permute-start | bytes 786440 | tf_op jit(solution)/shard_map/ppermute | solution.py:466
  90.1 17.0 %copy-start = (f32[8,640,128]{2,1,0:T(8,128)S(1)}, f32[8,640,128]{2,1,0:T(8,128)}, u32[]{:S(2)}) copy-start(f32[8,640,128]{2,1,0:T(8,128)} %get-tuple-element.41) | copy-start | bytes 7864324
  90.1 12.4 %collective-permute-start.7 = (bf16[352,128]{1,0:T(8,128)(2,1)S(1)}, bf16[352,128]{1,0:T(8,128)(2,1)S(1)}, u32[]{:S(2)}, u32[]{:S(2)}) collective-permute-start(bf16[352,128]{1,0:T(8,128)(2,1)S(1)} %get-tuple-element.87), channel_id=1, source_target_pairs={{0,2},{2,0},{4,6},{6,4},{8,10},{10,8},{12,14},{14,12},{1,3},{3,1},... | collective-permute-start | bytes 270344 | tf_op jit(solution)/shard_map/ppermute | solution.py:490
  93.2 0.7 copy-start.3
  93.3 0.7 copy-start.4
  102.7 7.2 %collective-permute-start.8 = (bf16[352,128]{1,0:T(8,128)(2,1)S(1)}, bf16[352,128]{1,0:T(8,128)(2,1)S(1)}, u32[]{:S(2)}, u32[]{:S(2)}) collective-permute-start(bf16[352,128]{1,0:T(8,128)(2,1)S(1)} %get-tuple-element.85), channel_id=1, source_target_pairs={{0,4},{2,6},{4,0},{6,2},{8,12},{10,14},{12,8},{14,10},{1,5},{3,7},... | collective-permute-start | bytes 270344 | tf_op jit(solution)/shard_map/ppermute | solution.py:490
  110.1 7.0 %collective-permute-start.9 = (bf16[352,128]{1,0:T(8,128)(2,1)S(1)}, bf16[352,128]{1,0:T(8,128)(2,1)S(1)}, u32[]{:S(2)}, u32[]{:S(2)}) collective-permute-start(bf16[352,128]{1,0:T(8,128)(2,1)S(1)} %get-tuple-element.83), channel_id=1, source_target_pairs={{0,8},{2,10},{4,12},{6,14},{8,0},{10,2},{12,4},{14,6},{1,9},{3,11}... | collective-permute-start | bytes 270344 | tf_op jit(solution)/shard_map/ppermute | solution.py:490
  117.2 1.5 %collective-permute-start.10 = (bf16[352,128]{1,0:T(8,128)(2,1)S(1)}, bf16[352,128]{1,0:T(8,128)(2,1)S(1)}, u32[]{:S(2)}, u32[]{:S(2)}) collective-permute-start(bf16[352,128]{1,0:T(8,128)(2,1)S(1)} %pad_maximum_fusion.5), channel_id=1, source_target_pairs={{0,1},{1,0},{2,3},{3,2},{4,5},{5,4},{6,7},{7,6},{8,9},{9,8},{10,11... | collective-permute-start | bytes 270344 | tf_op jit(solution)/shard_map/ppermute | solution.py:494

commit v2 on v1

--- a/solution.py
+++ b/solution.py
@@ -174,25 +174,32 @@
         bias = dot_tn(pair_w, wexp_ref[...]) + jnp.where(same, wtok, 0.0)
         bias_ref[...] = jnp.where(key_codes > 0.0, bias, MASKED) * LOG2E
         qrows = pl.ds(pl.multiple_of(w * win_rows, win_rows), win_rows)
-        for s in range(samples):
+        keys = pl.ds(start, span)
+
+        def products(s):
             block = n * samples + s
-            keys = pl.ds(start, span)
             kb = k_refs[block][keys, :].astype(BF16)
             vb = v_refs[block][keys, :].astype(BF16)
             qh = by_head(q_ref[block, qrows, :])
             dh = by_head(datt_ref[block, qrows, :])
-            x = dot_nt(kb, qh) * (scale * LOG2E) + bias_ref[...]
-            dp = dot_nt(vb, dh)
+            return block, kb, vb, qh, dh, dot_nt(kb, qh), dot_nt(vb, dh)
+
+        def softmax(state):
+            block, kb, vb, qh, dh, x, dp = state
+            x = x * (scale * LOG2E) + bias_ref[...]
             e = jnp.exp2(x - jnp.max(x, axis=0, keepdims=True))
             p = e * (1.0 / jnp.sum(e, axis=0, keepdims=True))
             t = p * dp
             ds = t - p * jnp.sum(t, axis=0, keepdims=True)
-            if s == 0:
+            return block, kb, vb, qh, dh, p.astype(BF16), ds
+
+        def gradients(state, first_sample):
+            block, kb, vb, qh, dh, pb, ds = state
+            dsb = ds.astype(BF16)
+            if first_sample:
                 bsum_ref[...] = ds
             else:
                 bsum_ref[...] += ds
-            pb = p.astype(BF16)
-            dsb = ds.astype(BF16)
             dk_refs[block][keys, :] += dot(dsb, qh)
             dv_refs[block][keys, :] += dot(pb, dh)
             att = own_head(dot_tn(pb, vb))
@@ -201,6 +208,11 @@
             ga = gate * att
             gated_ref[block, qrows, :] = ga.astype(BF16)
             dgate_ref[block, qrows, :] = (gy_ref[block, qrows, :] * ga * (1.0 - gate)).astype(BF16)
+
+        states = [products(s) for s in range(samples)]
+        states = [softmax(state) for state in states]
+        for s, state in enumerate(states):
+            gradients(state, s == 0)
         total = bsum_ref[...]
         total_b = total.astype(BF16)
         pw_ref[...] += dot(pair_w, total_b)
@@ -470,9 +482,9 @@
     wide = part_rows - SMALL_ROWS
 
     def encode(value):
-        big, small = value[:wide].astype(BF16), value[wide:]
-        top = small.astype(BF16)
-        return jnp.concatenate([big, top, (small - top.astype(F32)).astype(BF16)])
+        small = value[wide:]
+        top = lax.reduce_precision(value, 8, 7)
+        return jnp.concatenate([top, small - top[wide:]]).astype(BF16)
 
     def decode(sent):
         sent = sent.astype(F32)

time: 122 us -> 88.6 us (0.73)
  Pallas kernels: 69.6 us -> 36.8 us
    pallas_call x2, Pallas kernels: 66.8 us -> 33.9 us  [call(): pl.pallas_call(functools.partial(attention_kernel, geo, sides, edge), out...]
  transfers between devices with their start and end apart: 11 -> 11, of which waited for: 3 -> 3; matrix products, arithmetic and copies ran while one was open for 7% -> 9% of each run, Pallas kernels for 57% -> 42%
where the time goes in v2:
time: 88.6 us; the launch traced here: 88.1 us
  Pallas kernels  36.8 us (42%)
  starting transfers between devices  23.1 us (26%)
  waiting for transfers between devices  12.5 us (14%)
  other arithmetic  7.18 us (8%)
  local copies, waits for them, and re-layouts  6.79 us (8%)
  between operations  1.81 us (2%)
    pallas_call x2, Pallas kernels, call(): pl.pallas_call(functools.partial(attention_kernel, geo, sides, edge), out...  33.9 us
    ppermute x3, waiting for transfers between devices, per_device(): got = lax.ppermute(sent, 'atoms', [(i, i ^ step) for i in range(ranges)])  12.5 us
    ppermute x3, starting transfers between devices, per_device(): got = lax.ppermute(sent, 'atoms', [(i, i ^ step) for i in range(ranges)])  10.3 us
    ppermute x1, starting transfers between devices, per_device(): halo_lo = lax.ppermute(payload(atoms - span), 'atoms', up)  4.86 us
    ppermute x1, starting transfers between devices, per_device(): from_lower = lax.ppermute(ga_hi, 'atoms', up)  4.53 us
    unnamed x12, local copies, waits for them, and re-layouts  3.51 us
    pallas_call x1, Pallas kernels, per_device(): pl.pallas_call(functools.partial(pair_kernel, order=(inner, low + high),...  2.82 us
  transfers between devices with their start and end apart: 11, of which 3 were waited for; matrix products, arithmetic and copies ran while one was open for 9% of the time, Pallas kernels for 42%

profile of v2, /device:TPU:0, one launch (start us, length us, event | category | flops | bytes accessed | tf_op | source)
XLA Modules:
  0.0 88.1 jit_solution(3779447071982802708)
XLA Ops:
  1.3 0.7 fusion.20
  2.0 1.1 %fusion.22 = (bf16[8,128,128]{2,1,0:T(8,128)(2,1)S(1)}, bf16[8,128,128]{2,1,0:T(8,128)(2,1)S(1)}) fusion(bf16[8,640,128]{2,1,0:T(8,128)(2,1)} %refs_2_.3), kind=kLoop, calls=%fused_computation.79 | loop fusion | bytes 1048576 | tf_op jit(solution)/shard_map/slice | solution.py:379
  3.4 4.9 %collective-permute-start = (bf16[1040,128]{1,0:T(8,128)(2,1)S(1)}, bf16[1040,128]{1,0:T(8,128)(2,1)S(1)}, u32[]{:S(2)}, u32[]{:S(2)}) collective-permute-start(bf16[1040,128]{1,0:T(8,128)(2,1)S(1)} %concatenate.71), channel_id=1, source_target_pairs={{0,2},{2,4},{4,6},{6,8},{8,10},{10,12},{12,14},{1,3},{3,5},{5,7},{... | collective-permute-start | bytes 798728 | tf_op jit(solution)/shard_map/ppermute | solution.py:388
  8.5 1.3 %collective-permute-start.1 = (bf16[1040,128]{1,0:T(8,128)(2,1)S(1)}, bf16[1040,128]{1,0:T(8,128)(2,1)S(1)}, u32[]{:S(2)}, u32[]{:S(2)}) collective-permute-start(bf16[1040,128]{1,0:T(8,128)(2,1)S(1)} %concatenate.72), channel_id=1, source_target_pairs={{2,0},{4,2},{6,4},{8,6},{10,8},{12,10},{14,12},{3,1},{5,3},{7,5},{... | collective-permute-start | bytes 798728 | tf_op jit(solution)/shard_map/ppermute | solution.py:389
  9.9 0.7 reshape.166.refs_5_
  11.2 1.4 %copy.25.refs_12_.wpair_ref = bf16[16,4]{1,0:T(8,128)(2,1)} copy(bf16[16,4]{0,1:T(4,128)(2,1)} %param.25) | data formatting | bytes 256 | tf_op args[8]
  12.5 0.7 fusion.10
  13.8 18.2 %shard_map.164 = (f32[8,640,128]{2,1,0:T(8,128)}, f32[672,128]{1,0:T(8,128)}, f32[12,64,128]{2,1,0:T(8,128)}, bf16[12,64,128]{2,1,0:T(8,128)(2,1)}) custom-call(s32[21]{0:T(128)} %pad_add_fusion.refs_0_, f32[4]{0:T(128)} %refs_1_.3, bf16[8,640,128]{2,1,0:T(8,128)(2,1)} %refs_2_.3, bf16[8,640,128]{2,1,0:T(8,128)(2,1)} %refs_3_.3, f32[1,640]{1,0:T(1,128)} %reshape.165.refs_4_, ...), custom_call_target="tpu_custom_call" | custom-call | flops 13153337344 | bytes 12000000 | tf_op jit(solution)/shard_map/pallas_call | solution.py:432
  32.1 0.7 copy-done.1
  32.9 15.8 %shard_map.165 = (f32[8,640,128]{2,1,0:T(8,128)}, bf16[8,128,128]{2,1,0:T(8,128)(2,1)}, bf16[8,128,128]{2,1,0:T(8,128)(2,1)}, f32[672,128]{1,0:T(8,128)}, f32[8,...) custom-call(s32[21]{0:T(128)} %pad_add_fusion.refs_0_, f32[4]{0:T(128)} %refs_1_.3, bf16[8,640,128]{2,1,0:T(8,128)(2,1)} %refs_2_.3, ...), custom_call_target="tpu_custom_call" | custom-call | flops 11274289152 | bytes 12000000 | tf_op jit(solution)/shard_map/pallas_call | solution.py:432
  48.7 1.1 %convert_bitcast_fusion.1 = (bf16[336,128]{1,0:T(8,128)(2,1)S(1)}, f32[1,336,128]{2,1,0:T(8,128)S(1)}, bf16[336,128]{1,0:T(8,128)(2,1)S(1)}, f32[1,336,128]{2,1,0:T(8,128)S(1)}) fusion(f32[2,336,128]{2,1,0:T(8,128)} %bitcast.26, s32[]{:T(128)S(6)} %select_n.82, s32[]{:T(128)S(6)} %select_n.83), kind=kLoop, calls=%fused_computation.19 | loop fusion | flops 172032 | bytes 860168 | tf_op jit(solution)/shard_map/reduce_precision | solution.py:486
  49.7 0.7 fusion.7
  51.1 4.5 %collective-permute-start.2 = (bf16[8,128,128]{2,1,0:T(8,128)(2,1)}, bf16[8,128,128]{2,1,0:T(8,128)(2,1)S(1)}, u32[]{:S(2)}, u32[]{:S(2)}) collective-permute-start(bf16[8,128,128]{2,1,0:T(8,128)(2,1)} %get-tuple-element.42), channel_id=1, source_target_pairs={{0,2},{2,4},{4,6},{6,8},{8,10},{10,12},{12,14},{1,3},{3,5},{5,7},{... | collective-permute-start | bytes 786440 | tf_op jit(solution)/shard_map/ppermute | solution.py:479
  55.7 1.3 %collective-permute-start.3 = (bf16[8,128,128]{2,1,0:T(8,128)(2,1)}, bf16[8,128,128]{2,1,0:T(8,128)(2,1)S(1)}, u32[]{:S(2)}, u32[]{:S(2)}) collective-permute-start(bf16[8,128,128]{2,1,0:T(8,128)(2,1)} %get-tuple-element.43), channel_id=1, source_target_pairs={{2,0},{4,2},{6,4},{8,6},{10,8},{12,10},{14,12},{3,1},{5,3},{7,5},{... | collective-permute-start | bytes 786440 | tf_op jit(solution)/shard_map/ppermute | solution.py:478
  57.2 3.1 %collective-permute-start.7 = (bf16[352,128]{1,0:T(8,128)(2,1)S(1)}, bf16[352,128]{1,0:T(8,128)(2,1)S(1)}, u32[]{:S(2)}, u32[]{:S(2)}) collective-permute-start(bf16[352,128]{1,0:T(8,128)(2,1)S(1)} %get-tuple-element.87), channel_id=1, source_target_pairs={{0,2},{2,0},{4,6},{6,4},{8,10},{10,8},{12,14},{14,12},{1,3},{3,1},... | collective-permute-start | bytes 270344 | tf_op jit(solution)/shard_map/ppermute | solution.py:502
  61.0 2.8 %shard_map.166 = bf16[20,256,128]{2,1,0:T(8,128)(2,1)} custom-call(bf16[16,4]{1,0:T(8,128)(2,1)} %copy.25.refs_12_.wpair_ref, f32[12,64,128]{2,1,0:T(8,128)} %get-tuple-element.44.m1_ref, bf16[12,64,128]{2,1,0:T(8,128)(2,1)} %copy-done.3, f32[8,64,128]{2,1,0:T(8,128)} %get-tuple-element.46.m2_ref, bf16[8,64,128]{2,1,0:T(8,128)(2,1)} %copy-done.4), custom_call_target="tpu_custom_call" | custom-call | flops 671088640 | bytes 4000000 | tf_op jit(solution)/shard_map/pallas_call | solution.py:514
  63.8 5.8 %collective-permute-done.7 = bf16[352,128]{1,0:T(8,128)(2,1)S(1)} collective-permute-done((bf16[352,128]{1,0:T(8,128)(2,1)S(1)}, bf16[352,128]{1,0:T(8,128)(2,1)S(1)}, u32[]{:S(2)}, u32[]{:S(2)}) %collective-permute-start.7) | collective-permute-done | bytes 90144 | tf_op jit(solution)/shard_map/ppermute | solution.py:502
  69.7 4.4 %collective-permute-start.8 = (bf16[352,128]{1,0:T(8,128)(2,1)S(1)}, bf16[352,128]{1,0:T(8,128)(2,1)S(1)}, u32[]{:S(2)}, u32[]{:S(2)}) collective-permute-start(bf16[352,128]{1,0:T(8,128)(2,1)S(1)} %get-tuple-element.85), channel_id=1, source_target_pairs={{0,4},{2,6},{4,0},{6,2},{8,12},{10,14},{12,8},{14,10},{1,5},{3,7},... | collective-permute-start | bytes 270344 | tf_op jit(solution)/shard_map/ppermute | solution.py:502
  74.3 2.7 %collective-permute-done.8 = bf16[352,128]{1,0:T(8,128)(2,1)S(1)} collective-permute-done((bf16[352,128]{1,0:T(8,128)(2,1)S(1)}, bf16[352,128]{1,0:T(8,128)(2,1)S(1)}, u32[]{:S(2)}, u32[]{:S(2)}) %collective-permute-start.8) | collective-permute-done | bytes 90144 | tf_op jit(solution)/shard_map/ppermute | solution.py:502
  77.1 2.9 %collective-permute-start.9 = (bf16[352,128]{1,0:T(8,128)(2,1)S(1)}, bf16[352,128]{1,0:T(8,128)(2,1)S(1)}, u32[]{:S(2)}, u32[]{:S(2)}) collective-permute-start(bf16[352,128]{1,0:T(8,128)(2,1)S(1)} %get-tuple-element.83), channel_id=1, source_target_pairs={{0,8},{2,10},{4,12},{6,14},{8,0},{10,2},{12,4},{14,6},{1,9},{3,11}... | collective-permute-start | bytes 270344 | tf_op jit(solution)/shard_map/ppermute | solution.py:502
  80.0 4.1 %collective-permute-done.9 = bf16[352,128]{1,0:T(8,128)(2,1)S(1)} collective-permute-done((bf16[352,128]{1,0:T(8,128)(2,1)S(1)}, bf16[352,128]{1,0:T(8,128)(2,1)S(1)}, u32[]{:S(2)}, u32[]{:S(2)}) %collective-permute-start.9) | collective-permute-done | bytes 90144 | tf_op jit(solution)/shard_map/ppermute | solution.py:502
  84.4 1.3 %convert_element_type.57 = bf16[8,640,128]{2,1,0:T(8,128)(2,1)} convert(f32[8,640,128]{2,1,0:T(8,128)S(1)} %fusion) | non-fusion elementwise | flops 655360 | bytes 3932160 | tf_op jit(solution)/shard_map/convert_element_type | solution.py:530
  86.7 0.7 copy.27
  87.4 0.7 pad_maximum_fusion
  (79 shorter events, 5.1 us)
Async XLA Ops:
  3.4 28.7 %collective-permute-start = (bf16[1040,128]{1,0:T(8,128)(2,1)S(1)}, bf16[1040,128]{1,0:T(8,128)(2,1)S(1)}, u32[]{:S(2)}, u32[]{:S(2)}) collective-permute-start(bf16[1040,128]{1,0:T(8,128)(2,1)S(1)} %concatenate.71), channel_id=1, source_target_pairs={{0,2},{2,4},{4,6},{6,8},{8,10},{10,12},{12,14},{1,3},{3,5},{5,7},{... | collective-permute-start | bytes 798728 | tf_op jit(solution)/shard_map/ppermute | solution.py:388
  8.5 23.6 %collective-permute-start.1 = (bf16[1040,128]{1,0:T(8,128)(2,1)S(1)}, bf16[1040,128]{1,0:T(8,128)(2,1)S(1)}, u32[]{:S(2)}, u32[]{:S(2)}) collective-permute-start(bf16[1040,128]{1,0:T(8,128)(2,1)S(1)} %concatenate.72), channel_id=1, source_target_pairs={{2,0},{4,2},{6,4},{8,6},{10,8},{12,10},{14,12},{3,1},{5,3},{7,5},{... | collective-permute-start | bytes 798728 | tf_op jit(solution)/shard_map/ppermute | solution.py:389
  32.0 28.3 %collective-permute-start.4 = (bf16[12,64,128]{2,1,0:T(8,128)(2,1)}, bf16[12,64,128]{2,1,0:T(8,128)(2,1)S(1)}, u32[]{:S(2)}, u32[]{:S(2)}) collective-permute-start(bf16[12,64,128]{2,1,0:T(8,128)(2,1)} %get-tuple-element.45), channel_id=1, source_target_pairs={{0,1},{1,0},{2,3},{3,2},{4,5},{5,4},{6,7},{7,6},{8,9},{9,8},{10,11... | collective-permute-start | bytes 589832 | tf_op jit(solution)/shard_map/ppermute | solution.py:464
  32.1 0.7 copy-start.1
  32.1 0.8 copy-start.2
  50.5 6.5 %collective-permute-start.6 = (bf16[352,128]{1,0:T(8,128)(2,1)S(1)}, bf16[352,128]{1,0:T(8,128)(2,1)S(1)}, u32[]{:S(2)}, u32[]{:S(2)}) collective-permute-start(bf16[352,128]{1,0:T(8,128)(2,1)S(1)} %pad_maximum_fusion.1), channel_id=1, source_target_pairs={{0,1},{1,0},{2,3},{3,2},{4,5},{5,4},{6,7},{7,6},{8,9},{9,8},{10,11... | collective-permute-start | bytes 270344 | tf_op jit(solution)/shard_map/ppermute | solution.py:498
  51.1 9.2 %collective-permute-start.5 = (bf16[8,64,128]{2,1,0:T(8,128)(2,1)}, bf16[8,64,128]{2,1,0:T(8,128)(2,1)S(1)}, u32[]{:S(2)}, u32[]{:S(2)}) collective-permute-start(bf16[8,64,128]{2,1,0:T(8,128)(2,1)} %get-tuple-element.47), channel_id=1, source_target_pairs={{0,1},{1,0},{2,3},{3,2},{4,5},{5,4},{6,7},{7,6},{8,9},{9,8},{10,11... | collective-permute-start | bytes 393224 | tf_op jit(solution)/shard_map/ppermute | solution.py:477
  51.1 23.0 %collective-permute-start.2 = (bf16[8,128,128]{2,1,0:T(8,128)(2,1)}, bf16[8,128,128]{2,1,0:T(8,128)(2,1)S(1)}, u32[]{:S(2)}, u32[]{:S(2)}) collective-permute-start(bf16[8,128,128]{2,1,0:T(8,128)(2,1)} %get-tuple-element.42), channel_id=1, source_target_pairs={{0,2},{2,4},{4,6},{6,8},{8,10},{10,12},{12,14},{1,3},{3,5},{5,7},{... | collective-permute-start | bytes 786440 | tf_op jit(solution)/shard_map/ppermute | solution.py:479
  55.7 28.6 %collective-permute-start.3 = (bf16[8,128,128]{2,1,0:T(8,128)(2,1)}, bf16[8,128,128]{2,1,0:T(8,128)(2,1)S(1)}, u32[]{:S(2)}, u32[]{:S(2)}) collective-permute-start(bf16[8,128,128]{2,1,0:T(8,128)(2,1)} %get-tuple-element.43), channel_id=1, source_target_pairs={{2,0},{4,2},{6,4},{8,6},{10,8},{12,10},{14,12},{3,1},{5,3},{7,5},{... | collective-permute-start | bytes 786440 | tf_op jit(solution)/shard_map/ppermute | solution.py:478
  57.2 17.0 %copy-start = (f32[8,640,128]{2,1,0:T(8,128)S(1)}, f32[8,640,128]{2,1,0:T(8,128)}, u32[]{:S(2)}) copy-start(f32[8,640,128]{2,1,0:T(8,128)} %get-tuple-element.41) | copy-start | bytes 7864324
  57.2 12.4 %collective-permute-start.7 = (bf16[352,128]{1,0:T(8,128)(2,1)S(1)}, bf16[352,128]{1,0:T(8,128)(2,1)S(1)}, u32[]{:S(2)}, u32[]{:S(2)}) collective-permute-start(bf16[352,128]{1,0:T(8,128)(2,1)S(1)} %get-tuple-element.87), channel_id=1, source_target_pairs={{0,2},{2,0},{4,6},{6,4},{8,10},{10,8},{12,14},{14,12},{1,3},{3,1},... | collective-permute-start | bytes 270344 | tf_op jit(solution)/shard_map/ppermute | solution.py:502
  60.3 0.7 copy-start.3
  60.3 0.7 copy-start.4
  69.7 7.2 %collective-permute-start.8 = (bf16[352,128]{1,0:T(8,128)(2,1)S(1)}, bf16[352,128]{1,0:T(8,128)(2,1)S(1)}, u32[]{:S(2)}, u32[]{:S(2)}) collective-permute-start(bf16[352,128]{1,0:T(8,128)(2,1)S(1)} %get-tuple-element.85), channel_id=1, source_target_pairs={{0,4},{2,6},{4,0},{6,2},{8,12},{10,14},{12,8},{14,10},{1,5},{3,7},... | collective-permute-start | bytes 270344 | tf_op jit(solution)/shard_map/ppermute | solution.py:502
  77.1 7.0 %collective-permute-start.9 = (bf16[352,128]{1,0:T(8,128)(2,1)S(1)}, bf16[352,128]{1,0:T(8,128)(2,1)S(1)}, u32[]{:S(2)}, u32[]{:S(2)}) collective-permute-start(bf16[352,128]{1,0:T(8,128)(2,1)S(1)} %get-tuple-element.83), channel_id=1, source_target_pairs={{0,8},{2,10},{4,12},{6,14},{8,0},{10,2},{12,4},{14,6},{1,9},{3,11}... | collective-permute-start | bytes 270344 | tf_op jit(solution)/shard_map/ppermute | solution.py:502
  84.2 1.5 %collective-permute-start.10 = (bf16[352,128]{1,0:T(8,128)(2,1)S(1)}, bf16[352,128]{1,0:T(8,128)(2,1)S(1)}, u32[]{:S(2)}, u32[]{:S(2)}) collective-permute-start(bf16[352,128]{1,0:T(8,128)(2,1)S(1)} %pad_maximum_fusion.5), channel_id=1, source_target_pairs={{0,1},{1,0},{2,3},{3,2},{4,5},{5,4},{6,7},{7,6},{8,9},{9,8},{10,11... | collective-permute-start | bytes 270344 | tf_op jit(solution)/shard_map/ppermute | solution.py:506

commit v3 on v2

v3 whole, which is shorter than its diff:
```python
import functools
import math

import jax
import jax.numpy as jnp
from jax import lax
from jax.experimental import pallas as pl
from jax.experimental.pallas import tpu as pltpu
from jax.sharding import PartitionSpec as P

BF16 = jnp.bfloat16
F32 = jnp.float32
MASKED = -1000000000.0
LOG2E = math.log2(math.e)
CODE_ROWS = 16
CODE_BASE = 128
SMALL_ROWS = 16
VMEM_LIMIT = 56 * 1024 * 1024
EARLY_SHARE = 5


def dot(a, b):
    return lax.dot_general(a, b, (((1,), (0,)), ((), ())), preferred_element_type=F32)


def dot_nt(a, b):
    return lax.dot_general(a, b, (((1,), (1,)), ((), ())), preferred_element_type=F32)


def dot_tn(a, b):
    return lax.dot_general(a, b, (((0,), (0,)), ((), ())), preferred_element_type=F32)


def column_of(row, span):
    return jnp.broadcast_to(row, (span, row.shape[-1])).T


class Side:
    def __init__(self, windows, win_rows, rows, pieces, origin):
        self.first = windows[0]
        self.count = len(windows)
        self.queries = len(windows) * win_rows
        self.query_row = windows[0] * win_rows
        self.rows = rows
        self.pieces = pieces
        self.origin = origin


def payload_kernel(high_ref, low_ref, tok_ref, padding_ref, up_ref, down_ref):
    samples, span, _ = high_ref.shape
    rows = tok_ref.shape[0]
    atoms = rows * span
    index = lax.broadcasted_iota(jnp.int32, (CODE_ROWS, span), 0)
    place = lax.broadcasted_iota(jnp.int32, (1, span), 1)
    for out_ref, act_ref, row in ((up_ref, high_ref, rows - 1), (down_ref, low_ref, 0)):
        for s in range(samples):
            out_ref[s * span : (s + 1) * span, :] = act_ref[s]
        live = place + row * span < atoms - padding_ref[0]
        code = jnp.where(live, tok_ref[row : row + 1, :] + 1, 0)
        top, low = code // CODE_BASE, code % CODE_BASE
        both = jnp.where(index == 0, top, jnp.where(index == 1, low, 0))
        out_ref[samples * span :, :] = both.astype(F32).astype(BF16)


def attention_kernel(geo, sides, edge, chained, last, *refs):
    samples, atoms, channels, heads, win_rows, span, cp, out_half = geo
    refs = list(refs)
    take = lambda n: [refs.pop(0) for _ in range(n)]
    place_ref, offsets_ref, padding_ref, wtok_ref = take(4)
    tok_ref, act_hbm, gout_hbm, pair_hbm = take(4)
    wq_ref, wk_ref, wv_ref, wg_ref, wo_ref, wpair_ref = take(6)
    halo = {}
    if edge:
        halo["lo"], halo["hi"] = take(2)
    if chained:
        (acc_in_ref,) = take(1)
    ga_refs = take(len(sides))
    if edge:
        ga_lo_ref, ga_hi_ref = take(2)
    if last:
        acc_mine_ref, acc_other_ref = take(2)
    else:
        (acc_ref,) = take(1)
    mine_ref, other_ref = take(2)
    pair_ref, pair_sem, wexp_ref, pw_ref, code_ref, qcode_ref, halo_code_ref = take(7)
    act_ref, gout_ref, in_sem, q_ref, datt_ref, g_ref, gy_ref = take(7)
    dq_ref, dgate_ref, gated_ref, bias_ref, bsum_ref = take(5)
    if last:
        (acc_ref,) = take(1)
    n_blocks = len(sides) * samples
    k_refs = take(n_blocks)
    v_refs = take(n_blocks)
    dk_refs = take(n_blocks)
    dv_refs = take(n_blocks)

    half_rows = win_rows // 2
    head_dim = channels // heads
    scale = 1.0 / math.sqrt(head_dim)
    anchor = place_ref[0] * atoms
    all_atoms = place_ref[2] * atoms
    core = place_ref[1]

    block_copies = []
    for n, side in enumerate(sides):
        for s in range(samples):
            block = n * samples + s
            mine = []
            for source, row, rows, at in side.pieces:
                if source == "act":
                    origin = act_hbm.at[s, pl.ds(row, rows)]
                else:
                    origin = halo[source].at[pl.ds(s * span, rows)]
                mine.append((origin, act_ref.at[block, pl.ds(at, rows)]))
            mine.append(
                (gout_hbm.at[s, pl.ds(side.query_row, side.queries)], gout_ref.at[block])
            )
            block_copies.append(
                [
                    pltpu.make_async_copy(source, target, in_sem.at[block, i])
                    for i, (source, target) in enumerate(mine)
                ]
            )
    code_copies = []
    if edge:
        for i, name in enumerate(("lo", "hi")):
            code_copies.append(
                pltpu.make_async_copy(
                    halo[name].at[pl.ds(samples * span, CODE_ROWS)],
                    halo_code_ref.at[i],
                    pair_sem.at[len(sides) + i],
                )
            )
    pair_copies = []
    first = 0
    for n, side in enumerate(sides):
        pair_copies.append(
            pltpu.make_async_copy(
                pair_hbm.at[pl.ds(side.first, side.count)],
                pair_ref.at[pl.ds(first, side.count)],
                pair_sem.at[n],
            )
        )
        first += side.count
    for copy in code_copies:
        copy.start()
    for copies in block_copies:
        for copy in copies:
            copy.start()
    for copy in pair_copies:
        copy.start()

    lane = lax.broadcasted_iota(jnp.int32, (1, channels), 1)
    head_masks = [(lane // head_dim == h).astype(F32) for h in range(heads)]
    head_masks_b = [m.astype(BF16) for m in head_masks]

    lanes = 2 * heads * half_rows
    s_lane = lax.broadcasted_iota(jnp.int32, (1, lanes), 1)
    lane_head = (s_lane // half_rows) % heads
    lane_row = (s_lane // (heads * half_rows)) * half_rows + s_lane % half_rows
    wtok = jnp.zeros((1, lanes), F32)
    for h in range(heads):
        wtok = jnp.where(lane_head == h, wtok_ref[h], wtok)
    pick = (
        lax.broadcasted_iota(jnp.int32, (heads, lanes), 0)
        == (lax.broadcasted_iota(jnp.int32, (heads, lanes), 1) // half_rows) % heads
    ).astype(BF16)
    wlane = dot_tn(wpair_ref[...], pick).astype(BF16)
    for i in range(win_rows):
        wexp_ref[i * cp : (i + 1) * cp, :] = jnp.where(lane_row == i, wlane, 0.0).astype(BF16)
    pw_ref[...] = jnp.zeros_like(pw_ref)

    per_row = span // win_rows
    code = tok_ref[...] + 1
    top = (code // CODE_BASE).astype(F32).astype(BF16)
    low = (code % CODE_BASE).astype(F32).astype(BF16)
    source_lane = lax.broadcasted_iota(jnp.int32, (span, lanes), 0)
    for m in range(per_row):
        spread = (source_lane == m * win_rows + lane_row).astype(F32).astype(BF16)
        qcode_ref[m, : code.shape[0], :] = dot(top, spread) * CODE_BASE + dot(low, spread)

    live = jnp.where(
        lax.broadcasted_iota(jnp.int32, code.shape, 0) * span
        + lax.broadcasted_iota(jnp.int32, code.shape, 1)
        < atoms - padding_ref[0],
        code,
        0,
    ).astype(F32)
    for r in range(code.shape[0]):
        if any(
            r * span < row + rows and row < (r + 1) * span
            for side in sides
            for source, row, rows, _ in side.pieces
            if source == "act"
        ):
            code_ref[(r + 1) * span : (r + 2) * span, :] = column_of(live[r : r + 1], span)
    for copy in code_copies:
        copy.wait()
    if edge:
        for i, at in enumerate((0, atoms + span)):
            two = halo_code_ref[i].astype(F32)
            row = two[0:1, :] * CODE_BASE + two[1:2, :]
            code_ref[at : at + span, :] = column_of(row, span)

    w_kv = jnp.concatenate([wk_ref[...], wv_ref[...]], axis=1)
    w_qg = jnp.concatenate([wq_ref[...], wg_ref[...]], axis=1)
    for n, side in enumerate(sides):
        for s in range(samples):
            block = n * samples + s
            for copy in block_copies[block]:
                copy.wait()
            kv = dot(act_ref[block], w_kv)
            k_refs[block][...] = kv[:, :channels]
            v_refs[block][...] = kv[:, channels:]
            dk_refs[block][...] = jnp.zeros_like(dk_refs[block])
            dv_refs[block][...] = jnp.zeros_like(dv_refs[block])
            at = side.query_row - side.origin
            qg = dot(act_ref[block, at : at + side.queries, :], w_qg)
            q_ref[block] = qg[:, :channels].astype(BF16)
            gate = jax.nn.sigmoid(qg[:, channels:])
            gy = dot_nt(gout_ref[block], wo_ref[...])
            g_ref[block] = gate
            gy_ref[block] = gy
            datt_ref[block] = (gy * gate).astype(BF16)

    for copy in pair_copies:
        copy.wait()

    def by_head(rows):
        return jnp.concatenate(
            [
                rows[half * half_rows : (half + 1) * half_rows] * head_masks_b[h]
                for half in range(2)
                for h in range(heads)
            ],
            axis=0,
        )

    def own_head(wide):
        halves = []
        for half in range(2):
            total = None
            for h in range(heads):
                at = (half * heads + h) * half_rows
                term = wide[at : at + half_rows] * head_masks[h]
                total = term if total is None else total + term
            halves.append(total)
        return jnp.concatenate(halves, axis=0)

    def one_window(n, side, first, w, tok_sum):
        slot = first + w
        window = side.first + w
        start = jnp.clip(
            anchor + window * win_rows + offsets_ref[window], 0, all_atoms - span
        ) - (anchor + side.origin)
        start = jnp.clip(start, 0, side.rows - span)
        key_codes = code_ref[pl.ds(start + (side.origin + span), span), :]
        query_codes = qcode_ref[window % per_row, pl.ds(window // per_row, 1), :]
        same = key_codes == query_codes
        pair_w = pair_ref[slot]
        bias = dot_tn(pair_w, wexp_ref[...]) + jnp.where(same, wtok, 0.0)
        bias_ref[...] = jnp.where(key_codes > 0.0, bias, MASKED) * LOG2E
        qrows = pl.ds(pl.multiple_of(w * win_rows, win_rows), win_rows)
        keys = pl.ds(start, span)

        def products(s):
            block = n * samples + s
            kb = k_refs[block][keys, :].astype(BF16)
            vb = v_refs[block][keys, :].astype(BF16)
            qh = by_head(q_ref[block, qrows, :])
            dh = by_head(datt_ref[block, qrows, :])
            return block, kb, vb, qh, dh, dot_nt(kb, qh), dot_nt(vb, dh)

        def softmax(state):
            block, kb, vb, qh, dh, x, dp = state
            x = x * (scale * LOG2E) + bias_ref[...]
            e = jnp.exp2(x - jnp.max(x, axis=0, keepdims=True))
            p = e * (1.0 / jnp.sum(e, axis=0, keepdims=True))
            t = p * dp
            ds = t - p * jnp.sum(t, axis=0, keepdims=True)
            return block, kb, vb, qh, dh, p.astype(BF16), ds

        def gradients(state, first_sample):
            block, kb, vb, qh, dh, pb, ds = state
            dsb = ds.astype(BF16)
            if first_sample:
                bsum_ref[...] = ds
            else:
                bsum_ref[...] += ds
            dk_refs[block][keys, :] += dot(dsb, qh)
            dv_refs[block][keys, :] += dot(pb, dh)
            att = own_head(dot_tn(pb, vb))
            dq_ref[block, qrows, :] = (own_head(dot_tn(dsb, kb)) * scale).astype(BF16)
            gate = g_ref[block, qrows, :]
            ga = gate * att
            gated_ref[block, qrows, :] = ga.astype(BF16)
            dgate_ref[block, qrows, :] = (gy_ref[block, qrows, :] * ga * (1.0 - gate)).astype(BF16)

        states = [products(s) for s in range(samples)]
        states = [softmax(state) for state in states]
        for s, state in enumerate(states):
            gradients(state, s == 0)
        total = bsum_ref[...]
        total_b = total.astype(BF16)
        pw_ref[...] += dot(pair_w, total_b)
        straight = total.T
        bsum_ref[...] = straight
        width = heads * half_rows
        mine_ref[slot] = bsum_ref[pl.ds(pl.multiple_of(core * width, width), width), :]
        other_ref[slot] = bsum_ref[
            pl.ds(pl.multiple_of((1 - core) * width, width), width), :
        ].astype(BF16)
        return tok_sum + jnp.sum(jnp.where(same, total, 0.0), axis=0, keepdims=True)

    tok_sum = jnp.zeros((1, lanes), F32)
    first = 0
    for n, side in enumerate(sides):
        tok_sum = lax.fori_loop(
            0, side.count, functools.partial(one_window, n, side, first), tok_sum
        )
        first += side.count

    acc_kv = jnp.zeros((channels, 2 * channels), F32)
    acc_qg = jnp.zeros((channels, 2 * channels), F32)
    acc_o = jnp.zeros((channels, channels), F32)
    for n, side in enumerate(sides):
        at = side.query_row - side.origin
        for s in range(samples):
            block = n * samples + s
            dkv_b = jnp.concatenate(
                [(dk_refs[block][...] * scale).astype(BF16), dv_refs[block][...].astype(BF16)],
                axis=1,
            )
            dqg = jnp.concatenate([dq_ref[block], dgate_ref[block]], axis=1)
            part = dot_nt(dkv_b, w_kv)
            middle = part[at : at + side.queries] + dot_nt(dqg, w_qg)
            runs = [(0, part[:at]), (at, middle), (at + side.queries, part[at + side.queries :])]
            for run_at, run in runs:
                if run.shape[0] == 0:
                    continue
                run = run.astype(BF16)
                for source, _, rows, piece_at in side.pieces:
                    low = max(run_at, piece_at)
                    high = min(run_at + run.shape[0], piece_at + rows)
                    if low >= high:
                        continue
                    value = run[low - run_at : high - run_at]
                    if source == "lo":
                        ga_lo_ref[s, low - piece_at : high - piece_at, :] = value
                    elif source == "hi":
                        ga_hi_ref[s, low - piece_at : high - piece_at, :] = value
                    else:
                        ga_refs[n][s, low - piece_at : high - piece_at, :] = value
            acc_kv = acc_kv + dot_tn(act_ref[block], dkv_b)
            acc_qg = acc_qg + dot_tn(act_ref[block, at : at + side.queries, :], dqg)
            acc_o = acc_o + dot_tn(gated_ref[block], gout_ref[block])

    diag = lax.broadcasted_iota(jnp.int32, (win_rows * cp, lanes), 0) // cp == lane_row
    pw = jnp.where(diag, pw_ref[...], 0.0).reshape(win_rows, cp, lanes).sum(axis=0)
    parts = [
        acc_qg[:, :channels],
        acc_kv[:, :channels],
        acc_kv[:, channels:],
        acc_qg[:, channels:],
        acc_o,
    ]
    first_half, second_half = [], []
    left = out_half
    for part in parts:
        if left >= channels:
            first_half.append(part)
            left -= channels
        elif left > 0:
            first_half.append(part[:left])
            second_half.append(part[left:])
            left = 0
        else:
            second_half.append(part)
    tok_rows = jnp.where(
        lax.broadcasted_iota(jnp.int32, (SMALL_ROWS, lanes), 0) == 0, tok_sum, 0.0
    )
    for half, group in enumerate((first_half + [pw], second_half + [tok_rows])):
        at = 0
        for part in group:
            rows = part.shape[0]
            if chained:
                part = part + acc_in_ref[half, at : at + rows, :]
            acc_ref[half, at : at + rows, :] = part
            at += rows
    if last:
        acc_mine_ref[...] = acc_ref[core]
        value = acc_ref[1 - core]
        wide = value.shape[0] - SMALL_ROWS
        top = value.astype(BF16)
        acc_other_ref[: wide + SMALL_ROWS, :] = top
        rest = value[wide:] - top[wide:].astype(F32)
        acc_other_ref[wide + SMALL_ROWS :, :] = rest.astype(BF16)


def pair_kernel(wpair_ref, *refs, order, heads, cp):
    out_ref = refs[-1]
    rows = refs[0].shape[1]
    half_rows = rows // heads
    lane = lax.broadcasted_iota(jnp.int32, (1, rows), 1)
    pick = (
        lax.broadcasted_iota(jnp.int32, (heads, rows), 0)
        == lax.broadcasted_iota(jnp.int32, (heads, rows), 1) // half_rows
    ).astype(BF16)
    wlane = dot_tn(wpair_ref[...], pick)
    wexp = jnp.concatenate(
        [jnp.where(lane % half_rows == i, wlane, 0.0) for i in range(half_rows)], axis=0
    ).astype(BF16)
    for which, group in enumerate(order):
        m_ref, r_ref = refs[2 * which], refs[2 * which + 1]
        for slot, window in enumerate(group):
            total = (m_ref[slot] + r_ref[slot].astype(F32)).astype(BF16)
            out_ref[window] = dot(wexp, total).astype(BF16)


def act_sum_kernel(firsts, *refs):
    out_ref = refs[-1]
    atoms = out_ref.shape[1]
    marks = {0, atoms}
    for first, ref in zip(firsts, refs):
        marks |= {first, first + ref.shape[1]}
    marks = sorted(marks)
    for low, high in zip(marks[:-1], marks[1:]):
        total = None
        for first, ref in zip(firsts, refs):
            if first <= low and high <= first + ref.shape[1]:
                term = ref[:, low - first : high - first, :].astype(F32)
                total = term if total is None else total + term
        out_ref[:, low:high, :] = total.astype(BF16)


def finish_kernel(place_ref, sent_ref, got_ref, gw_ref, gpw_ref, gtok_ref, *, heads):
    rows = sent_ref.shape[0]
    wide = rows - 2 * SMALL_ROWS
    channels = gw_ref.shape[1]
    is_first = place_ref[1] == 0
    sent, got = sent_ref[...].astype(F32), got_ref[...].astype(F32)
    first = jnp.where(is_first, sent, got)
    second = jnp.where(is_first, got, sent)
    gw_ref[:wide, :] = first[:wide]
    gw_ref[wide:, :] = second[:wide]
    pw = first[wide : wide + SMALL_ROWS] + first[wide + SMALL_ROWS :]
    tok = second[wide : wide + 1] + second[wide + SMALL_ROWS : wide + SMALL_ROWS + 1]
    half_rows = channels // (2 * heads)
    head = (lax.broadcasted_iota(jnp.int32, (heads, channels), 1) // half_rows) % heads
    pick = (head == lax.broadcasted_iota(jnp.int32, (heads, channels), 0)).astype(F32)
    gpw_ref[...] = lax.dot_general(
        pick,
        pw,
        (((1,), (1,)), ((), ())),
        precision=lax.Precision.HIGHEST,
        preferred_element_type=F32,
    )
    for h in range(heads):
        gtok_ref[h] = jnp.sum(tok * pick[h : h + 1])


def per_device(
    act,
    grad_out,
    pair,
    w_query,
    w_key,
    w_value,
    w_gate,
    w_out,
    w_pair,
    w_token,
    offsets,
    atom_token,
    padding,
):
    samples, atoms, channels = act.shape
    windows = offsets.shape[0]
    win_rows = atoms // windows
    span = pair.shape[-1]
    cp, heads = w_pair.shape
    half_rows = win_rows // 2
    lanes = heads * win_rows
    ranges = lax.axis_size("atoms")
    cores = lax.axis_size("samples")
    assert cores == 2 and ranges & (ranges - 1) == 0
    core = lax.axis_index("samples")
    place = jnp.stack([lax.axis_index("atoms"), core, jnp.int32(ranges)]).astype(jnp.int32)
    tok = atom_token.reshape(atoms // span, span)
    w_pair_t = w_pair.T
    vmem = pl.BlockSpec(memory_space=pltpu.VMEM)
    smem = pl.BlockSpec(memory_space=pltpu.SMEM)
    hbm = pl.BlockSpec(memory_space=pl.ANY)

    up = [(i, i + 1) for i in range(ranges - 1)]
    down = [(j, i) for i, j in up]
    last_block = atoms // span - 1
    to_up, to_down = pl.pallas_call(
        payload_kernel,
        out_shape=[jax.ShapeDtypeStruct((samples * span + CODE_ROWS, channels), BF16)] * 2,
        grid=(1,),
        in_specs=[
            pl.BlockSpec((samples, span, channels), lambda i: (0, last_block, 0)),
            pl.BlockSpec((samples, span, channels), lambda i: (0, 0, 0)),
            vmem,
            smem,
        ],
        out_specs=[vmem, vmem],
    )(act, act, tok, padding)
    halo_lo = lax.ppermute(to_up, "atoms", up)
    halo_hi = lax.ppermute(to_down, "atoms", down)

    out_half = 5 * channels // 2
    part_rows = out_half + SMALL_ROWS
    coded_rows = part_rows + SMALL_ROWS
    geo = (samples, atoms, channels, heads, win_rows, span, cp, out_half)
    pair_flat = pair.reshape(windows, win_rows * cp, span)
    width = heads * half_rows
    common = (
        place,
        offsets,
        padding,
        w_token,
        tok,
        act,
        grad_out,
        pair_flat,
        w_query,
        w_key,
        w_value,
        w_gate,
        w_out,
        w_pair_t,
    )
    shape = jax.ShapeDtypeStruct

    def call(sides, halos=(), acc_in=None, last=False):
        edge, chained = len(halos) > 0, acc_in is not None
        args = common + tuple(halos) + ((acc_in,) if chained else ())
        in_specs = [smem] * 4 + [vmem] + [hbm] * 3 + [vmem] * 6 + [hbm] * len(halos)
        in_specs += [vmem] * chained
        count = sum(side.count for side in sides)
        queries, rows = sides[0].queries, sides[0].rows
        blocks = len(sides) * samples
        own_rows = [sum(p[2] for p in side.pieces if p[0] == "act") for side in sides]
        out_shape = [shape((samples, n, channels), BF16) for n in own_rows]
        if edge:
            out_shape += [shape((samples, span, channels), BF16)] * 2
        if last:
            out_shape += [shape((part_rows, channels), F32), shape((coded_rows, channels), BF16)]
        else:
            out_shape += [shape((2, part_rows, channels), F32)]
        out_shape += [shape((count, width, span), F32), shape((count, width, span), BF16)]
        per_query = (blocks, queries, channels)
        scratch = [
            pltpu.VMEM((count, win_rows * cp, span), BF16),
            pltpu.SemaphoreType.DMA((len(sides) + 2,)),
            pltpu.VMEM((win_rows * cp, lanes), BF16),
            pltpu.VMEM((win_rows * cp, lanes), F32),
            pltpu.VMEM((atoms + 2 * span, span), F32),
            pltpu.VMEM((span // win_rows, -(-atoms // span // 8) * 8, lanes), F32),
            pltpu.VMEM((2, CODE_ROWS, span), BF16),
            pltpu.VMEM((blocks, rows, channels), BF16),
            pltpu.VMEM(per_query, BF16),
            pltpu.SemaphoreType.DMA((blocks, 3)),
            pltpu.VMEM(per_query, BF16),
            pltpu.VMEM(per_query, BF16),
            pltpu.VMEM(per_query, F32),
            pltpu.VMEM(per_query, F32),
            pltpu.VMEM(per_query, BF16),
            pltpu.VMEM(per_query, BF16),
            pltpu.VMEM(per_query, BF16),
            pltpu.VMEM((span, lanes), F32),
            pltpu.VMEM((span, lanes), F32),
        ]
        if last:
            scratch += [pltpu.VMEM((2, part_rows, channels), F32)]
        scratch += [pltpu.VMEM((rows, channels), F32)] * (4 * blocks)
        units = 6 * count * samples + 8 * count + 14 * blocks
        return pl.pallas_call(
            functools.partial(attention_kernel, geo, sides, edge, chained, last),
            out_shape=out_shape,
            in_specs=in_specs,
            out_specs=[vmem] * len(out_shape),
            scratch_shapes=scratch,
            compiler_params=pltpu.CompilerParams(vmem_limit_bytes=VMEM_LIMIT),
            cost_estimate=pl.CostEstimate(
                flops=2 * units * 128 * 128 * 128 * 4,
                bytes_accessed=12_000_000,
                transcendentals=count * samples * span * lanes,
            ),
        )(*args)

    edge_count = span // win_rows
    early_count = (windows - 2 * edge_count) * EARLY_SHARE // 12
    early = tuple(range(edge_count, edge_count + early_count))
    late = tuple(range(edge_count + early_count, windows - edge_count))
    low, high = tuple(range(edge_count)), tuple(range(windows - edge_count, windows))
    early_end = (early[-1] + 1) * win_rows + span
    late_first = late[0] * win_rows - span
    own = edge_count * win_rows + span
    swap = [(0, 1), (1, 0)]

    early_side = Side(early, win_rows, early_end, [("act", 0, early_end, 0)], 0)
    ga_early, acc, mine1, other1 = call([early_side])
    recv1 = lax.ppermute(other1, "samples", swap)

    low_side = Side(low, win_rows, own + span, [("lo", 0, span, 0), ("act", 0, own, span)], -span)
    high_side = Side(
        high,
        win_rows,
        own + span,
        [("act", atoms - own, own, 0), ("hi", 0, span, own)],
        atoms - own,
    )
    ga_low, ga_high, ga_lo, ga_hi, acc, mine2, other2 = call(
        [low_side, high_side], (halo_lo, halo_hi), acc
    )
    recv2 = lax.ppermute(other2, "samples", swap)
    from_upper = lax.ppermute(ga_lo, "atoms", down)
    from_lower = lax.ppermute(ga_hi, "atoms", up)

    late_rows = atoms - late_first
    late_side = Side(
        late, win_rows, late_rows, [("act", late_first, late_rows, 0)], late_first
    )
    ga_late, acc_mine, acc_other, mine3, other3 = call([late_side], (), acc, True)

    wide = out_half

    def encode(value):
        top = lax.reduce_precision(value, 8, 7)
        return jnp.concatenate([top, value[wide:] - top[wide:]]).astype(BF16)

    def decode(sent):
        sent = sent.astype(F32)
        return jnp.concatenate(
            [sent[:wide], sent[wide : wide + SMALL_ROWS] + sent[wide + SMALL_ROWS :]]
        )

    acc_other, other3, from_upper, from_lower = lax.optimization_barrier(
        (acc_other, other3, from_upper, from_lower)
    )
    recv3 = lax.ppermute(other3, "samples", swap)
    total = acc_mine + decode(lax.ppermute(acc_other, "samples", swap))
    grad_pair = pl.pallas_call(
        functools.partial(pair_kernel, order=(early, low + high, late), heads=heads, cp=cp),
        out_shape=shape((windows, half_rows * cp, span), BF16),
        in_specs=[vmem] * 7,
        out_specs=vmem,
        compiler_params=pltpu.CompilerParams(vmem_limit_bytes=VMEM_LIMIT),
        cost_estimate=pl.CostEstimate(
            flops=2 * windows * 256 * 256 * 256, bytes_accessed=4_000_000, transcendentals=0
        ),
    )(w_pair_t, mine1, recv1, mine2, recv2, mine3, recv3)

    pieces = [
        (0, ga_early),
        (late_first, ga_late),
        (0, ga_low),
        (atoms - own, ga_high),
        (0, from_lower),
        (atoms - span, from_upper),
    ]
    grad_act = pl.pallas_call(
        functools.partial(act_sum_kernel, [first for first, _ in pieces]),
        out_shape=shape((samples, atoms, channels), BF16),
        grid=(2,),
        in_specs=[
            pl.BlockSpec((samples // 2,) + part.shape[1:], lambda s: (s, 0, 0))
            for _, part in pieces
        ],
        out_specs=pl.BlockSpec((samples // 2, atoms, channels), lambda s: (s, 0, 0)),
        compiler_params=pltpu.CompilerParams(vmem_limit_bytes=VMEM_LIMIT),
        cost_estimate=pl.CostEstimate(
            flops=4 * samples * atoms * channels, bytes_accessed=6_000_000, transcendentals=0
        ),
    )(*[part for _, part in pieces])
    step = ranges // 2
    while step >= 1:
        if step == ranges // 4:
            total, grad_pair = lax.optimization_barrier((total, grad_pair))
        if step == ranges // 8:
            total, grad_act = lax.optimization_barrier((total, grad_act))
        sent = encode(total)
        got = lax.ppermute(sent, "atoms", [(i, i ^ step) for i in range(ranges)])
        total = decode(sent) + decode(got)
        step //= 2
    sent = encode(total)
    got = lax.ppermute(sent, "samples", swap)
    grad_weights, grad_pair_weight, grad_token_weight = pl.pallas_call(
        functools.partial(finish_kernel, heads=heads),
        out_shape=[
            shape((5 * channels, channels), F32),
            shape((heads, cp), F32),
            shape((heads,), F32),
        ],
        in_specs=[smem, vmem, vmem],
        out_specs=[vmem, vmem, smem],
    )(place, sent, got)

    return (
        grad_act,
        grad_pair.reshape(windows, half_rows, cp, span),
        grad_weights.reshape(5, channels, channels),
        grad_pair_weight.T,
        grad_token_weight,
    )


def solution(mesh):
    in_specs = (
        P("samples", ("groups", "atoms"), None),
        P("samples", ("groups", "atoms"), None),
        P(("groups", "atoms"), None, None, None),
        P(),
        P(),
        P(),
        P(),
        P(),
        P(),
        P(),
        P(("groups", "atoms")),
        P(("groups", "atoms")),
        P(("groups", "atoms")),
    )
    out_specs = (
        P("samples", ("groups", "atoms"), None),
        P(("groups", "atoms"), "samples", None, None),
        P("groups", None, None),
        P("groups", None),
        P("groups"),
    )
    return jax.shard_map(
        per_device, mesh=mesh, in_specs=in_specs, out_specs=out_specs, check_vma=False
    )
```

time: 88.6 us -> 86.1 us (0.972)
  Pallas kernels: 36.8 us -> 51.2 us
  other arithmetic: 7.18 us -> 0.94 us
  local copies, waits for them, and re-layouts: 6.79 us -> 2.17 us
  waiting for transfers between devices: 12.5 us -> 9.02 us
  starting transfers between devices: 23.1 us -> 20.4 us
    pallas_call x3 -> x7, Pallas kernels: 36.8 us -> 51.2 us  [the longest x3 41.7 us: call(): pl.pallas_call(functools.partial(attention_kernel, geo, sides, edge, chai...]
    ppermute x3, waiting for transfers between devices: 12.5 us -> 7.72 us  [per_device(): got = lax.ppermute(sent, 'atoms', [(i, i ^ step) for i in range(ranges)])]
    ppermute x3, starting transfers between devices: 10.3 us -> 6.42 us  [per_device(): got = lax.ppermute(sent, 'atoms', [(i, i ^ step) for i in range(ranges)])]
    convert_element_type x2 -> x0, other arithmetic: 1.96 us -> none  [the longest x1 1.27 us: per_device(): grad_act = ga2.at[:, :span].add(from_lower.astype(F32)).at[:, atoms - spa...]
    unnamed x12 -> x24, local copies, waits for them, and re-layouts: 3.51 us -> 2.08 us
    reshape x3 -> x0, local copies, waits for them, and re-layouts: 1.38 us -> none  [the longest x1 0.71 us: per_device(): qcode = jnp.broadcast_to((atom_token + 1).astype(F32).reshape(windows, 2,...]
    concatenate x4 -> x3, other arithmetic: 1.35 us -> 0.05 us  [encode(): return jnp.concatenate([top, value[wide:] - top[wide:]]).astype(BF16)]
    ppermute x1, waiting for transfers between devices: 0.01 us -> 1.28 us  [per_device(): got = lax.ppermute(sent, 'samples', swap)]
  transfers between devices with their start and end apart: 11 -> 12, of which waited for: 3 -> 4; matrix products, arithmetic and copies ran while one was open for 9% -> 1% of each run, Pallas kernels for 42% -> 35%
where the time goes in v3:
time: 86.1 us; the launch traced here: 85.6 us
  Pallas kernels  51.2 us (59%)
  starting transfers between devices  20.4 us (24%)
  waiting for transfers between devices  9.02 us (10%)
  local copies, waits for them, and re-layouts  2.17 us (3%)
  between operations  1.88 us (2%)
  other arithmetic  0.94 us (1%)
    pallas_call x3, Pallas kernels, call(): pl.pallas_call(functools.partial(attention_kernel, geo, sides, edge, chai...  41.7 us
    ppermute x3, waiting for transfers between devices, per_device(): got = lax.ppermute(sent, 'atoms', [(i, i ^ step) for i in range(ranges)])  7.72 us
    ppermute x3, starting transfers between devices, per_device(): got = lax.ppermute(sent, 'atoms', [(i, i ^ step) for i in range(ranges)])  6.42 us
    ppermute x1, starting transfers between devices, per_device(): from_lower = lax.ppermute(ga_hi, 'atoms', up)  5.4 us
    ppermute x1, starting transfers between devices, per_device(): halo_lo = lax.ppermute(to_up, 'atoms', up)  4.85 us
    pallas_call x1, Pallas kernels, per_device(): pl.pallas_call(functools.partial(act_sum_kernel, [first for first, _ in p...  2.98 us
    pallas_call x1, Pallas kernels, per_device(): pl.pallas_call(functools.partial(pair_kernel, order=(early, low + high, l...  2.96 us
    unnamed x24, local copies, waits for them, and re-layouts  2.08 us
  transfers between devices with their start and end apart: 12, of which 4 were waited for; matrix products, arithmetic and copies ran while one was open for 1% of the time, Pallas kernels for 35%

profile of v3, /device:TPU:0, one launch (start us, length us, event | category | flops | bytes accessed | tf_op | source)
XLA Modules:
  0.0 85.6 jit_solution(3795960531611341627)
XLA Ops:
  1.3 1.9 %shard_map.164 = (bf16[1040,128]{1,0:T(8,128)(2,1)}, bf16[1040,128]{1,0:T(8,128)(2,1)}) custom-call(bf16[8,640,128]{2,1,0:T(8,128)(2,1)} %refs_5_.5, bf16[8,640,128]{2,1,0:T(8,128)(2,1)} %refs_5_.5, s32[5,128]{1,0:T(8,128)} %bitcast.8, s32[1]{0:T(128)S(6)} %copy.18.padding_ref.refs_2_), custom_call_target="tpu_custom_call" | custom-call | tf_op jit(solution)/shard_map/pallas_call | solution.py:497
  3.1 4.8 %collective-permute-start = (bf16[1040,128]{1,0:T(8,128)(2,1)}, bf16[1040,128]{1,0:T(8,128)(2,1)S(1)}, u32[]{:S(2)}, u32[]{:S(2)}) collective-permute-start(bf16[1040,128]{1,0:T(8,128)(2,1)} %get-tuple-element.34), channel_id=1, source_target_pairs={{0,2},{2,4},{4,6},{6,8},{8,10},{10,12},{12,14},{1,3},{3,5},{5,7},{... | collective-permute-start | bytes 798728 | tf_op jit(solution)/shard_map/ppermute | solution.py:509
  8.0 1.3 %collective-permute-start.1 = (bf16[1040,128]{1,0:T(8,128)(2,1)}, bf16[1040,128]{1,0:T(8,128)(2,1)S(1)}, u32[]{:S(2)}, u32[]{:S(2)}) collective-permute-start(bf16[1040,128]{1,0:T(8,128)(2,1)} %get-tuple-element.35), channel_id=1, source_target_pairs={{2,0},{4,2},{6,4},{8,6},{10,8},{12,10},{14,12},{3,1},{5,3},{7,5},{... | collective-permute-start | bytes 798728 | tf_op jit(solution)/shard_map/ppermute | solution.py:510
  9.3 0.6 pad_add_fusion.refs_0_.place_ref
  9.9 10.9 %shard_map.165 = (bf16[8,416,128]{2,1,0:T(8,128)(2,1)}, f32[2,336,128]{2,1,0:T(8,128)}, f32[5,64,128]{2,1,0:T(8,128)}, bf16[5,64,128]{2,1,0:T(8,128)(2,1)}) custom-call(s32[3]{0:T(128)} %pad_add_fusion.refs_0_.place_ref, s32[20]{0:T(128)} %refs_1_.5, s32[1]{0:T(128)S(6)} %copy.18.padding_ref.refs_2_, f32[4]{0:T(128)} %refs_3_.5, s32[5,128]{1,0:T(8,128)} %bitcast.9, ...), custom_call_target="tpu_custom_call" | custom-call | flops 6576668672 | bytes 12000000 | tf_op jit(solution)/shard_map/pallas_call | solution.py:579
  20.8 0.7 copy-done.5
  21.5 17.6 %shard_map.166 = (bf16[8,256,128]{2,1,0:T(8,128)(2,1)}, bf16[8,256,128]{2,1,0:T(8,128)(2,1)}, bf16[8,128,128]{2,1,0:T(8,128)(2,1)}, bf16[8,128,128]{2,1,0:T(8,12...) custom-call(s32[3]{0:T(128)} %pad_add_fusion.refs_0_.place_ref, s32[20]{0:T(128)} %refs_1_.5, ...), custom_call_target="tpu_custom_call" | custom-call | flops 11274289152 | bytes 12000000 | tf_op jit(solution)/shard_map/pallas_call | solution.py:579
  39.2 1.3 %collective-permute-start.2 = (bf16[8,128,128]{2,1,0:T(8,128)(2,1)}, bf16[8,128,128]{2,1,0:T(8,128)(2,1)S(1)}, u32[]{:S(2)}, u32[]{:S(2)}) collective-permute-start(bf16[8,128,128]{2,1,0:T(8,128)(2,1)} %get-tuple-element.41), channel_id=1, source_target_pairs={{2,0},{4,2},{6,4},{8,6},{10,8},{12,10},{14,12},{3,1},{5,3},{7,5},{... | collective-permute-start | bytes 786440 | tf_op jit(solution)/shard_map/ppermute | solution.py:619
  40.5 5.4 %collective-permute-start.3 = (bf16[8,128,128]{2,1,0:T(8,128)(2,1)}, bf16[8,128,128]{2,1,0:T(8,128)(2,1)S(1)}, u32[]{:S(2)}, u32[]{:S(2)}) collective-permute-start(bf16[8,128,128]{2,1,0:T(8,128)(2,1)} %get-tuple-element.42), channel_id=1, source_target_pairs={{0,2},{2,4},{4,6},{6,8},{8,10},{10,12},{12,14},{1,3},{3,5},{5,7},{... | collective-permute-start | bytes 786440 | tf_op jit(solution)/shard_map/ppermute | solution.py:620
  45.9 13.2 %shard_map.167 = (bf16[8,480,128]{2,1,0:T(8,128)(2,1)}, f32[336,128]{1,0:T(8,128)}, bf16[352,128]{1,0:T(8,128)(2,1)}, f32[7,64,128]{2,1,0:T(8,128)}, bf16[7,64,128]{2,1,0:T(8,128)(2,1)}) custom-call(s32[3]{0:T(128)} %pad_add_fusion.refs_0_.place_ref, s32[20]{0:T(128)} %refs_1_.5, s32[1]{0:T(128)S(6)} %copy.18.padding_ref.refs_2_, f32[4]{0:T(128)} %refs_3_.5, ...), custom_call_target="tpu_custom_call" | custom-call | flops 8455716864 | bytes 12000000 | tf_op jit(solution)/shard_map/pallas_call | solution.py:579
  59.2 0.5 collective-permute-start.6
  59.8 0.4 collective-permute-start.8
  60.2 3.0 %shard_map.169 = bf16[8,640,128]{2,1,0:T(8,128)(2,1)} custom-call(bf16[8,416,128]{2,1,0:T(8,128)(2,1)} %get-tuple-element.51.refs_0_, bf16[8,480,128]{2,1,0:T(8,128)(2,1)} %get-tuple-element.52.refs_1_, bf16[8,256,128]{2,1,0:T(8,128)(2,1)} %get-tuple-element.53.refs_2_, bf16[8,256,128]{2,1,0:T(8,128)(2,1)} %get-tuple-element.54.refs_3_, ...), custom_call_target="tpu_custom_call" | custom-call | flops 2621440 | bytes 6000000 | tf_op jit(solution)/shard_map/pallas_call | solution.py:664
  63.4 3.9 %collective-permute-start.5 = (bf16[352,128]{1,0:T(8,128)(2,1)S(1)}, bf16[352,128]{1,0:T(8,128)(2,1)S(1)}, u32[]{:S(2)}, u32[]{:S(2)}) collective-permute-start(bf16[352,128]{1,0:T(8,128)(2,1)S(1)} %get-tuple-element.75), channel_id=1, source_target_pairs={{0,8},{2,10},{4,12},{6,14},{8,0},{10,2},{12,4},{14,6},{1,9},{3,11}... | collective-permute-start | bytes 270344 | tf_op jit(solution)/shard_map/ppermute | solution.py:685
  67.3 0.6 copy-done.11
  68.0 3.0 %shard_map.168 = bf16[20,256,128]{2,1,0:T(8,128)(2,1)} custom-call(bf16[4,16]{1,0:T(4,128)(2,1)} %bitcast.20, f32[5,64,128]{2,1,0:T(8,128)} %get-tuple-element.44.refs_0_, bf16[5,64,128]{2,1,0:T(8,128)(2,1)} %copy-done.11, f32[8,64,128]{2,1,0:T(8,128)} %get-tuple-element.46.refs_2_, bf16[8,64,128]{2,1,0:T(8,128)(2,1)} %copy-done.8, ...), custom_call_target="tpu_custom_call" | custom-call | flops 671088640 | bytes 4000000 | tf_op jit(solution)/shard_map/pallas_call | solution.py:645
  71.0 1.1 %collective-permute-done.5 = bf16[352,128]{1,0:T(8,128)(2,1)S(1)} collective-permute-done((bf16[352,128]{1,0:T(8,128)(2,1)S(1)}, bf16[352,128]{1,0:T(8,128)(2,1)S(1)}, u32[]{:S(2)}, u32[]{:S(2)}) %collective-permute-start.5) | collective-permute-done | bytes 90144 | tf_op jit(solution)/shard_map/ppermute | solution.py:685
  72.2 0.8 collective-permute-start.9
  73.0 3.8 %collective-permute-done.9 = bf16[352,128]{1,0:T(8,128)(2,1)S(1)} collective-permute-done((bf16[352,128]{1,0:T(8,128)(2,1)S(1)}, bf16[352,128]{1,0:T(8,128)(2,1)S(1)}, u32[]{:S(2)}, u32[]{:S(2)}) %collective-permute-start.9) | collective-permute-done | bytes 90144 | tf_op jit(solution)/shard_map/ppermute | solution.py:685
  77.0 1.7 %collective-permute-start.10 = (bf16[352,128]{1,0:T(8,128)(2,1)S(1)}, bf16[352,128]{1,0:T(8,128)(2,1)S(1)}, u32[]{:S(2)}, u32[]{:S(2)}) collective-permute-start(bf16[352,128]{1,0:T(8,128)(2,1)S(1)} %get-tuple-element.72), channel_id=1, source_target_pairs={{0,2},{2,0},{4,6},{6,4},{8,10},{10,8},{12,14},{14,12},{1,3},{3,1},... | collective-permute-start | bytes 270344 | tf_op jit(solution)/shard_map/ppermute | solution.py:685
  78.7 2.8 %collective-permute-done.10 = bf16[352,128]{1,0:T(8,128)(2,1)S(1)} collective-permute-done((bf16[352,128]{1,0:T(8,128)(2,1)S(1)}, bf16[352,128]{1,0:T(8,128)(2,1)S(1)}, u32[]{:S(2)}, u32[]{:S(2)}) %collective-permute-start.10) | collective-permute-done | bytes 90144 | tf_op jit(solution)/shard_map/ppermute | solution.py:685
  81.8 1.3 %collective-permute-done.11.got_ref = bf16[352,128]{1,0:T(8,128)(2,1)S(1)} collective-permute-done((bf16[352,128]{1,0:T(8,128)(2,1)S(1)}, bf16[352,128]{1,0:T(8,128)(2,1)S(1)}, u32[]{:S(2)}, u32[]{:S(2)}) %collective-permute-start.11) | collective-permute-done | bytes 90144 | tf_op jit(solution)/shard_map/ppermute | solution.py:689
  83.1 0.6 copy-done.4
  83.7 1.7 %shard_map.170 = (f32[640,128]{1,0:T(8,128)}, f32[4,16]{1,0:T(4,128)}, f32[4]{0:T(128)}) custom-call(s32[3]{0:T(128)} %pad_add_fusion.refs_0_.place_ref, bf16[352,128]{1,0:T(8,128)(2,1)} %copy-done, bf16[352,128]{1,0:T(8,128)(2,1)} %copy-done.4), custom_call_target="tpu_custom_call" | custom-call | tf_op jit(solution)/shard_map/pallas_call | solution.py:690
  (66 shorter events, 0.9 us)
Async XLA Ops:
  3.1 17.6 %collective-permute-start = (bf16[1040,128]{1,0:T(8,128)(2,1)}, bf16[1040,128]{1,0:T(8,128)(2,1)S(1)}, u32[]{:S(2)}, u32[]{:S(2)}) collective-permute-start(bf16[1040,128]{1,0:T(8,128)(2,1)} %get-tuple-element.34), channel_id=1, source_target_pairs={{0,2},{2,4},{4,6},{6,8},{8,10},{10,12},{12,14},{1,3},{3,5},{5,7},{... | collective-permute-start | bytes 798728 | tf_op jit(solution)/shard_map/ppermute | solution.py:509
  8.0 12.8 %collective-permute-start.1 = (bf16[1040,128]{1,0:T(8,128)(2,1)}, bf16[1040,128]{1,0:T(8,128)(2,1)S(1)}, u32[]{:S(2)}, u32[]{:S(2)}) collective-permute-start(bf16[1040,128]{1,0:T(8,128)(2,1)} %get-tuple-element.35), channel_id=1, source_target_pairs={{2,0},{4,2},{6,4},{8,6},{10,8},{12,10},{14,12},{3,1},{5,3},{7,5},{... | collective-permute-start | bytes 798728 | tf_op jit(solution)/shard_map/ppermute | solution.py:510
  20.8 0.7 copy-start.5
  20.8 0.8 copy-start.6
  39.2 19.9 %collective-permute-start.2 = (bf16[8,128,128]{2,1,0:T(8,128)(2,1)}, bf16[8,128,128]{2,1,0:T(8,128)(2,1)S(1)}, u32[]{:S(2)}, u32[]{:S(2)}) collective-permute-start(bf16[8,128,128]{2,1,0:T(8,128)(2,1)} %get-tuple-element.41), channel_id=1, source_target_pairs={{2,0},{4,2},{6,4},{8,6},{10,8},{12,10},{14,12},{3,1},{5,3},{7,5},{... | collective-permute-start | bytes 786440 | tf_op jit(solution)/shard_map/ppermute | solution.py:619
  40.5 18.6 %collective-permute-start.3 = (bf16[8,128,128]{2,1,0:T(8,128)(2,1)}, bf16[8,128,128]{2,1,0:T(8,128)(2,1)S(1)}, u32[]{:S(2)}, u32[]{:S(2)}) collective-permute-start(bf16[8,128,128]{2,1,0:T(8,128)(2,1)} %get-tuple-element.42), channel_id=1, source_target_pairs={{0,2},{2,4},{4,6},{6,8},{8,10},{10,12},{12,14},{1,3},{3,5},{5,7},{... | collective-permute-start | bytes 786440 | tf_op jit(solution)/shard_map/ppermute | solution.py:620
  45.9 13.3 %copy-start.10 = (bf16[5,64,128]{2,1,0:T(8,128)(2,1)S(1)}, bf16[5,64,128]{2,1,0:T(8,128)(2,1)}, u32[]{:S(2)}) copy-start(bf16[5,64,128]{2,1,0:T(8,128)(2,1)} %get-tuple-element.45) | copy-start | bytes 245764
  45.9 13.8 %copy-start.7 = (bf16[8,64,128]{2,1,0:T(8,128)(2,1)S(1)}, bf16[8,64,128]{2,1,0:T(8,128)(2,1)}, u32[]{:S(2)}) copy-start(bf16[8,64,128]{2,1,0:T(8,128)(2,1)} %get-tuple-element.47) | copy-start | bytes 393220
  59.1 1.1 %copy-start.1 = (bf16[8,128,128]{2,1,0:T(8,128)(2,1)}, bf16[8,128,128]{2,1,0:T(8,128)(2,1)S(1)}, u32[]{:S(2)}) copy-start(bf16[8,128,128]{2,1,0:T(8,128)(2,1)S(1)} %collective-permute-done.2.refs_5_) | copy-start | bytes 786436
  59.1 1.1 %copy-start.2 = (bf16[8,128,128]{2,1,0:T(8,128)(2,1)}, bf16[8,128,128]{2,1,0:T(8,128)(2,1)S(1)}, u32[]{:S(2)}) copy-start(bf16[8,128,128]{2,1,0:T(8,128)(2,1)S(1)} %collective-permute-done.3.refs_4_) | copy-start | bytes 786436
  59.1 4.1 %collective-permute-start.4 = (bf16[352,128]{1,0:T(8,128)(2,1)}, bf16[352,128]{1,0:T(8,128)(2,1)S(1)}, u32[]{:S(2)}, u32[]{:S(2)}) collective-permute-start(bf16[352,128]{1,0:T(8,128)(2,1)} %get-tuple-element.43), channel_id=1, source_target_pairs={{0,1},{1,0},{2,3},{3,2},{4,5},{5,4},{6,7},{7,6},{8,9},{9,8},{10,11... | collective-permute-start | bytes 270344 | tf_op jit(solution)/shard_map/ppermute | solution.py:644
  59.2 8.1 %collective-permute-start.6 = (bf16[5,64,128]{2,1,0:T(8,128)(2,1)S(1)}, bf16[5,64,128]{2,1,0:T(8,128)(2,1)S(1)}, u32[]{:S(2)}, u32[]{:S(2)}) collective-permute-start(bf16[5,64,128]{2,1,0:T(8,128)(2,1)S(1)} %copy-done.10), channel_id=1, source_target_pairs={{0,1},{1,0},{2,3},{3,2},{4,5},{5,4},{6,7},{7,6},{8,9},{9,8},{10,11... | collective-permute-start | bytes 245768 | tf_op jit(solution)/shard_map/ppermute | solution.py:605
  59.7 7.6 %collective-permute-start.7 = (bf16[8,64,128]{2,1,0:T(8,128)(2,1)S(1)}, bf16[8,64,128]{2,1,0:T(8,128)(2,1)S(1)}, u32[]{:S(2)}, u32[]{:S(2)}) collective-permute-start(bf16[8,64,128]{2,1,0:T(8,128)(2,1)S(1)} %copy-done.7), channel_id=1, source_target_pairs={{0,1},{1,0},{2,3},{3,2},{4,5},{5,4},{6,7},{7,6},{8,9},{9,8},{10,11... | collective-permute-start | bytes 393224 | tf_op jit(solution)/shard_map/ppermute | solution.py:618
  59.8 7.5 %collective-permute-start.8 = (bf16[7,64,128]{2,1,0:T(8,128)(2,1)}, bf16[7,64,128]{2,1,0:T(8,128)(2,1)S(1)}, u32[]{:S(2)}, u32[]{:S(2)}) collective-permute-start(bf16[7,64,128]{2,1,0:T(8,128)(2,1)} %get-tuple-element.49), channel_id=1, source_target_pairs={{0,1},{1,0},{2,3},{3,2},{4,5},{5,4},{6,7},{7,6},{8,9},{9,8},{10,11... | collective-permute-start | bytes 344072 | tf_op jit(solution)/shard_map/ppermute | solution.py:643
  60.2 3.0 %copy-start.3 = (f32[336,128]{1,0:T(8,128)S(1)}, f32[336,128]{1,0:T(8,128)}, u32[]{:S(2)}) copy-start(f32[336,128]{1,0:T(8,128)} %get-tuple-element.38) | copy-start | bytes 516100
  63.4 8.7 %collective-permute-start.5 = (bf16[352,128]{1,0:T(8,128)(2,1)S(1)}, bf16[352,128]{1,0:T(8,128)(2,1)S(1)}, u32[]{:S(2)}, u32[]{:S(2)}) collective-permute-start(bf16[352,128]{1,0:T(8,128)(2,1)S(1)} %get-tuple-element.75), channel_id=1, source_target_pairs={{0,8},{2,10},{4,12},{6,14},{8,0},{10,2},{12,4},{14,6},{1,9},{3,11}... | collective-permute-start | bytes 270344 | tf_op jit(solution)/shard_map/ppermute | solution.py:685
  67.3 0.6 copy-start.11
  67.3 0.7 copy-start.8
  67.3 0.7 copy-start.9
  72.2 4.6 %collective-permute-start.9 = (bf16[352,128]{1,0:T(8,128)(2,1)S(1)}, bf16[352,128]{1,0:T(8,128)(2,1)S(1)}, u32[]{:S(2)}, u32[]{:S(2)}) collective-permute-start(bf16[352,128]{1,0:T(8,128)(2,1)S(1)} %get-tuple-element.73), channel_id=1, source_target_pairs={{0,4},{2,6},{4,0},{6,2},{8,12},{10,14},{12,8},{14,10},{1,5},{3,7},... | collective-permute-start | bytes 270344 | tf_op jit(solution)/shard_map/ppermute | solution.py:685
  77.0 4.6 %collective-permute-start.10 = (bf16[352,128]{1,0:T(8,128)(2,1)S(1)}, bf16[352,128]{1,0:T(8,128)(2,1)S(1)}, u32[]{:S(2)}, u32[]{:S(2)}) collective-permute-start(bf16[352,128]{1,0:T(8,128)(2,1)S(1)} %get-tuple-element.72), channel_id=1, source_target_pairs={{0,2},{2,0},{4,6},{6,4},{8,10},{10,8},{12,14},{14,12},{1,3},{3,1},... | collective-permute-start | bytes 270344 | tf_op jit(solution)/shard_map/ppermute | solution.py:685
  81.7 1.4 %copy-start = (bf16[352,128]{1,0:T(8,128)(2,1)}, bf16[352,128]{1,0:T(8,128)(2,1)S(1)}, u32[]{:S(2)}) copy-start(bf16[352,128]{1,0:T(8,128)(2,1)S(1)} %pad_maximum_fusion.3.sent_ref) | copy-start | bytes 270340
  81.7 1.4 %collective-permute-start.11 = (bf16[352,128]{1,0:T(8,128)(2,1)S(1)}, bf16[352,128]{1,0:T(8,128)(2,1)S(1)}, u32[]{:S(2)}, u32[]{:S(2)}) collective-permute-start(bf16[352,128]{1,0:T(8,128)(2,1)S(1)} %pad_maximum_fusion.3.sent_ref), channel_id=1, source_target_pairs={{0,1},{1,0},{2,3},{3,2},{4,5},{5,4},{6,7},{7,6},{8,9},{9,8},{10,11... | collective-permute-start | bytes 270344 | tf_op jit(solution)/shard_map/ppermute | solution.py:689
  83.1 0.6 copy-start.4

commit v4 on v3

--- a/solution.py
+++ b/solution.py
@@ -16,7 +16,7 @@
 CODE_BASE = 128
 SMALL_ROWS = 16
 VMEM_LIMIT = 56 * 1024 * 1024
-EARLY_SHARE = 5
+EARLY_SHARE = 6
 
 
 def dot(a, b):
@@ -46,13 +46,27 @@
         self.origin = origin
 
 
-def payload_kernel(high_ref, low_ref, tok_ref, padding_ref, up_ref, down_ref):
+class HaloCopy:
+    def __init__(self, is_odd, when_odd, when_even, target, sem):
+        self.is_odd = is_odd
+        self.options = [pltpu.make_async_copy(s, target, sem) for s in (when_even, when_odd)]
+
+    def start(self):
+        pl.when(self.is_odd)(self.options[1].start)
+        pl.when(jnp.logical_not(self.is_odd))(self.options[0].start)
+
+    def wait(self):
+        self.options[0].wait()
+
+
+def payload_kernel(high_ref, low_ref, tok_ref, padding_ref, out_a_ref, out_b_ref):
     samples, span, _ = high_ref.shape
     rows = tok_ref.shape[0]
     atoms = rows * span
     index = lax.broadcasted_iota(jnp.int32, (CODE_ROWS, span), 0)
     place = lax.broadcasted_iota(jnp.int32, (1, span), 1)
-    for out_ref, act_ref, row in ((up_ref, high_ref, rows - 1), (down_ref, low_ref, 0)):
+
+    def write(out_ref, act_ref, row):
         for s in range(samples):
             out_ref[s * span : (s + 1) * span, :] = act_ref[s]
         live = place + row * span < atoms - padding_ref[0]
@@ -61,22 +75,33 @@
         both = jnp.where(index == 0, top, jnp.where(index == 1, low, 0))
         out_ref[samples * span :, :] = both.astype(F32).astype(BF16)
 
+    is_odd = lax.axis_index("atoms") % 2 == 1
+
+    @pl.when(is_odd)
+    def _():
+        write(out_a_ref, low_ref, 0)
+        write(out_b_ref, high_ref, rows - 1)
+
+    @pl.when(jnp.logical_not(is_odd))
+    def _():
+        write(out_a_ref, high_ref, rows - 1)
+        write(out_b_ref, low_ref, 0)
+
 
 def attention_kernel(geo, sides, edge, chained, last, *refs):
     samples, atoms, channels, heads, win_rows, span, cp, out_half = geo
     refs = list(refs)
     take = lambda n: [refs.pop(0) for _ in range(n)]
-    place_ref, offsets_ref, padding_ref, wtok_ref = take(4)
+    offsets_ref, padding_ref, wtok_ref = take(3)
     tok_ref, act_hbm, gout_hbm, pair_hbm = take(4)
     wq_ref, wk_ref, wv_ref, wg_ref, wo_ref, wpair_ref = take(6)
-    halo = {}
     if edge:
-        halo["lo"], halo["hi"] = take(2)
+        halo_a, halo_b = take(2)
     if chained:
         (acc_in_ref,) = take(1)
     ga_refs = take(len(sides))
     if edge:
-        ga_lo_ref, ga_hi_ref = take(2)
+        ga_out_refs = take(2)
     if last:
         acc_mine_ref, acc_other_ref = take(2)
     else:
@@ -87,6 +112,8 @@
     dq_ref, dgate_ref, gated_ref, bias_ref, bsum_ref = take(5)
     if last:
         (acc_ref,) = take(1)
+    if edge:
+        ga_halo_ref, ga_sem = take(2)
     n_blocks = len(sides) * samples
     k_refs = take(n_blocks)
     v_refs = take(n_blocks)
@@ -96,36 +123,47 @@
     half_rows = win_rows // 2
     head_dim = channels // heads
     scale = 1.0 / math.sqrt(head_dim)
-    anchor = place_ref[0] * atoms
-    all_atoms = place_ref[2] * atoms
-    core = place_ref[1]
+    rank = lax.axis_index("atoms")
+    core = lax.axis_index("samples")
+    anchor = rank * atoms
+    all_atoms = lax.axis_size("atoms") * atoms
+    odd = rank % 2
+    is_odd = odd == 1
+
+    def halo_copy(source, row, rows, target, sem):
+        refs = (halo_a, halo_b) if source == "lo" else (halo_b, halo_a)
+        return HaloCopy(is_odd, *[ref.at[pl.ds(row, rows)] for ref in refs], target, sem)
+
 
     block_copies = []
     for n, side in enumerate(sides):
         for s in range(samples):
             block = n * samples + s
             mine = []
-            for source, row, rows, at in side.pieces:
+            for i, (source, row, rows, at) in enumerate(side.pieces):
+                target, sem = act_ref.at[block, pl.ds(at, rows)], in_sem.at[block, i]
                 if source == "act":
-                    origin = act_hbm.at[s, pl.ds(row, rows)]
+                    mine.append(
+                        pltpu.make_async_copy(act_hbm.at[s, pl.ds(row, rows)], target, sem)
+                    )
                 else:
-                    origin = halo[source].at[pl.ds(s * span, rows)]
-                mine.append((origin, act_ref.at[block, pl.ds(at, rows)]))
+                    mine.append(halo_copy(source, s * span, rows, target, sem))
             mine.append(
-                (gout_hbm.at[s, pl.ds(side.query_row, side.queries)], gout_ref.at[block])
+                pltpu.make_async_copy(
+                    gout_hbm.at[s, pl.ds(side.query_row, side.queries)],
+                    gout_ref.at[block],
+                    in_sem.at[block, 2],
+                )
             )
-            block_copies.append(
-                [
-                    pltpu.make_async_copy(source, target, in_sem.at[block, i])
-                    for i, (source, target) in enumerate(mine)
-                ]
-            )
+            block_copies.append(mine)
     code_copies = []
     if edge:
-        for i, name in enumerate(("lo", "hi")):
+        for i, source in enumerate(("lo", "hi")):
             code_copies.append(
-                pltpu.make_async_copy(
-                    halo[name].at[pl.ds(samples * span, CODE_ROWS)],
+                halo_copy(
+                    source,
+                    samples * span,
+                    CODE_ROWS,
                     halo_code_ref.at[i],
                     pair_sem.at[len(sides) + i],
                 )
@@ -246,79 +284,92 @@
             halves.append(total)
         return jnp.concatenate(halves, axis=0)
 
-    def one_window(n, side, first, w, tok_sum):
-        slot = first + w
-        window = side.first + w
-        start = jnp.clip(
-            anchor + window * win_rows + offsets_ref[window], 0, all_atoms - span
-        ) - (anchor + side.origin)
-        start = jnp.clip(start, 0, side.rows - span)
-        key_codes = code_ref[pl.ds(start + (side.origin + span), span), :]
-        query_codes = qcode_ref[window % per_row, pl.ds(window // per_row, 1), :]
-        same = key_codes == query_codes
-        pair_w = pair_ref[slot]
-        bias = dot_tn(pair_w, wexp_ref[...]) + jnp.where(same, wtok, 0.0)
-        bias_ref[...] = jnp.where(key_codes > 0.0, bias, MASKED) * LOG2E
-        qrows = pl.ds(pl.multiple_of(w * win_rows, win_rows), win_rows)
-        keys = pl.ds(start, span)
-
-        def products(s):
-            block = n * samples + s
-            kb = k_refs[block][keys, :].astype(BF16)
-            vb = v_refs[block][keys, :].astype(BF16)
-            qh = by_head(q_ref[block, qrows, :])
-            dh = by_head(datt_ref[block, qrows, :])
-            return block, kb, vb, qh, dh, dot_nt(kb, qh), dot_nt(vb, dh)
-
-        def softmax(state):
-            block, kb, vb, qh, dh, x, dp = state
-            x = x * (scale * LOG2E) + bias_ref[...]
+    def window_group(members, w, tok_sum):
+        keys, qrows, same, pair_w = [], [], [], []
+        for lane_slot, (n, side, first, shift) in enumerate(members):
+            window = side.first + shift + w
+            start = jnp.clip(
+                anchor + window * win_rows + offsets_ref[window], 0, all_atoms - span
+            ) - (anchor + side.origin)
+            start = jnp.clip(start, 0, side.rows - span)
+            key_codes = code_ref[pl.ds(start + (side.origin + span), span), :]
+            query_codes = qcode_ref[window % per_row, pl.ds(window // per_row, 1), :]
+            same.append(key_codes == query_codes)
+            pair_w.append(pair_ref.at[first + shift + w])
+            bias = dot_tn(pair_w[-1][...], wexp_ref[...]) + jnp.where(same[-1], wtok, 0.0)
+            bias_ref[lane_slot] = jnp.where(key_codes > 0.0, bias, MASKED) * LOG2E
+            at = pl.multiple_of((shift + w) * win_rows, win_rows)
+            qrows.append(pl.ds(at, win_rows))
+            keys.append(pl.ds(start, span))
+
+        def products(m, s):
+            block = members[m][0] * samples + s
+            kb = k_refs[block][keys[m], :].astype(BF16)
+            vb = v_refs[block][keys[m], :].astype(BF16)
+            qh = by_head(q_ref[block, qrows[m], :])
+            dh = by_head(datt_ref[block, qrows[m], :])
+            return kb, vb, qh, dh, dot_nt(kb, qh), dot_nt(vb, dh)
+
+        def softmax(m, state):
+            kb, vb, qh, dh, x, dp = state
+            x = x * (scale * LOG2E) + bias_ref[m]
             e = jnp.exp2(x - jnp.max(x, axis=0, keepdims=True))
             p = e * (1.0 / jnp.sum(e, axis=0, keepdims=True))
             t = p * dp
             ds = t - p * jnp.sum(t, axis=0, keepdims=True)
-            return block, kb, vb, qh, dh, p.astype(BF16), ds
-
-        def gradients(state, first_sample):
-            block, kb, vb, qh, dh, pb, ds = state
+            return kb, vb, qh, dh, p.astype(BF16), ds
+
+        def gradients(m, s, state):
+            block = members[m][0] * samples + s
+            kb, vb, qh, dh, pb, ds = state
             dsb = ds.astype(BF16)
-            if first_sample:
-                bsum_ref[...] = ds
+            if s == 0:
+                bsum_ref[m] = ds
             else:
-                bsum_ref[...] += ds
-            dk_refs[block][keys, :] += dot(dsb, qh)
-            dv_refs[block][keys, :] += dot(pb, dh)
+                bsum_ref[m] += ds
+            dk_refs[block][keys[m], :] += dot(dsb, qh)
+            dv_refs[block][keys[m], :] += dot(pb, dh)
             att = own_head(dot_tn(pb, vb))
-            dq_ref[block, qrows, :] = (own_head(dot_tn(dsb, kb)) * scale).astype(BF16)
-            gate = g_ref[block, qrows, :]
+            rows = qrows[m]
+            dq_ref[block, rows, :] = (own_head(dot_tn(dsb, kb)) * scale).astype(BF16)
+            gate = g_ref[block, rows, :]
             ga = gate * att
-            gated_ref[block, qrows, :] = ga.astype(BF16)
-            dgate_ref[block, qrows, :] = (gy_ref[block, qrows, :] * ga * (1.0 - gate)).astype(BF16)
-
-        states = [products(s) for s in range(samples)]
-        states = [softmax(state) for state in states]
-        for s, state in enumerate(states):
-            gradients(state, s == 0)
-        total = bsum_ref[...]
-        total_b = total.astype(BF16)
-        pw_ref[...] += dot(pair_w, total_b)
-        straight = total.T
-        bsum_ref[...] = straight
+            gated_ref[block, rows, :] = ga.astype(BF16)
+            dgate_ref[block, rows, :] = (gy_ref[block, rows, :] * ga * (1.0 - gate)).astype(BF16)
+
+        order = [(m, s) for s in range(samples) for m in range(len(members))]
+        states = [products(m, s) for m, s in order]
+        states = [softmax(m, state) for (m, _), state in zip(order, states)]
+        for (m, s), state in zip(order, states):
+            gradients(m, s, state)
         width = heads * half_rows
-        mine_ref[slot] = bsum_ref[pl.ds(pl.multiple_of(core * width, width), width), :]
-        other_ref[slot] = bsum_ref[
-            pl.ds(pl.multiple_of((1 - core) * width, width), width), :
-        ].astype(BF16)
-        return tok_sum + jnp.sum(jnp.where(same, total, 0.0), axis=0, keepdims=True)
+        for m, (n, side, first, shift) in enumerate(members):
+            total = bsum_ref[m]
+            pw_ref[...] += dot(pair_w[m][...], total.astype(BF16))
+            tok_sum += jnp.sum(jnp.where(same[m], total, 0.0), axis=0, keepdims=True)
+            bsum_ref[m] = total.T
+            slot = first + shift + w
+            mine_ref[slot] = bsum_ref[m, pl.ds(pl.multiple_of(core * width, width), width), :]
+            other_ref[slot] = bsum_ref[
+                m, pl.ds(pl.multiple_of((1 - core) * width, width), width), :
+            ].astype(BF16)
+        return tok_sum
 
     tok_sum = jnp.zeros((1, lanes), F32)
-    first = 0
-    for n, side in enumerate(sides):
+    if len(sides) == 2:
+        members = [(0, sides[0], 0, 0), (1, sides[1], sides[0].count, 0)]
         tok_sum = lax.fori_loop(
-            0, side.count, functools.partial(one_window, n, side, first), tok_sum
+            0, sides[0].count, functools.partial(window_group, members), tok_sum
         )
-        first += side.count
-
+    else:
+        half = sides[0].count // 2
+        members = [(0, sides[0], 0, 0), (0, sides[0], 0, half)]
+        tok_sum = lax.fori_loop(0, half, functools.partial(window_group, members), tok_sum)
+        if sides[0].count % 2:
+            rest = [(0, sides[0], 0, sides[0].count - 1)]
+            tok_sum = window_group(rest, 0, tok_sum)
+
+    pending = []
     acc_kv = jnp.zeros((channels, 2 * channels), F32)
     acc_qg = jnp.zeros((channels, 2 * channels), F32)
     acc_o = jnp.zeros((channels, channels), F32)
@@ -345,11 +396,22 @@
                         continue
                     value = run[low - run_at : high - run_at]
                     if source == "lo":
-                        ga_lo_ref[s, low - piece_at : high - piece_at, :] = value
+                        ga_halo_ref[1 - odd, s, low - piece_at : high - piece_at, :] = value
                     elif source == "hi":
-                        ga_hi_ref[s, low - piece_at : high - piece_at, :] = value
+                        ga_halo_ref[odd, s, low - piece_at : high - piece_at, :] = value
                     else:
                         ga_refs[n][s, low - piece_at : high - piece_at, :] = value
+            pending.append((dkv_b, dqg))
+    ga_copies = []
+    if edge:
+        for i, out_ref in enumerate(ga_out_refs):
+            ga_copies.append(pltpu.make_async_copy(ga_halo_ref.at[i], out_ref, ga_sem.at[i]))
+            ga_copies[-1].start()
+    for n, side in enumerate(sides):
+        at = side.query_row - side.origin
+        for s in range(samples):
+            block = n * samples + s
+            dkv_b, dqg = pending[block]
             acc_kv = acc_kv + dot_tn(act_ref[block], dkv_b)
             acc_qg = acc_qg + dot_tn(act_ref[block, at : at + side.queries, :], dqg)
             acc_o = acc_o + dot_tn(gated_ref[block], gout_ref[block])
@@ -386,6 +448,8 @@
                 part = part + acc_in_ref[half, at : at + rows, :]
             acc_ref[half, at : at + rows, :] = part
             at += rows
+    for copy in ga_copies:
+        copy.wait()
     if last:
         acc_mine_ref[...] = acc_ref[core]
         value = acc_ref[1 - core]
@@ -419,12 +483,20 @@
 def act_sum_kernel(firsts, *refs):
     out_ref = refs[-1]
     atoms = out_ref.shape[1]
-    marks = {0, atoms}
+    is_odd = lax.axis_index("atoms") % 2 == 1
+    from_a, from_b = refs[-3][...].astype(F32), refs[-2][...].astype(F32)
+    halos = [jnp.where(is_odd, from_a, from_b), jnp.where(is_odd, from_b, from_a)]
+    span = from_a.shape[1]
+    halo_rows = [(0, halos[0]), (atoms - span, halos[1])]
+    marks = {0, span, atoms - span, atoms}
     for first, ref in zip(firsts, refs):
         marks |= {first, first + ref.shape[1]}
     marks = sorted(marks)
     for low, high in zip(marks[:-1], marks[1:]):
         total = None
+        for first, halo in halo_rows:
+            if first <= low and high <= first + span:
+                total = halo[:, low - first : high - first]
         for first, ref in zip(firsts, refs):
             if first <= low and high <= first + ref.shape[1]:
                 term = ref[:, low - first : high - first, :].astype(F32)
@@ -432,11 +504,11 @@
         out_ref[:, low:high, :] = total.astype(BF16)
 
 
-def finish_kernel(place_ref, sent_ref, got_ref, gw_ref, gpw_ref, gtok_ref, *, heads):
+def finish_kernel(sent_ref, got_ref, gw_ref, gpw_ref, gtok_ref, *, heads):
     rows = sent_ref.shape[0]
     wide = rows - 2 * SMALL_ROWS
     channels = gw_ref.shape[1]
-    is_first = place_ref[1] == 0
+    is_first = lax.axis_index("samples") == 0
     sent, got = sent_ref[...].astype(F32), got_ref[...].astype(F32)
     first = jnp.where(is_first, sent, got)
     second = jnp.where(is_first, got, sent)
@@ -483,18 +555,18 @@
     ranges = lax.axis_size("atoms")
     cores = lax.axis_size("samples")
     assert cores == 2 and ranges & (ranges - 1) == 0
-    core = lax.axis_index("samples")
-    place = jnp.stack([lax.axis_index("atoms"), core, jnp.int32(ranges)]).astype(jnp.int32)
     tok = atom_token.reshape(atoms // span, span)
     w_pair_t = w_pair.T
     vmem = pl.BlockSpec(memory_space=pltpu.VMEM)
     smem = pl.BlockSpec(memory_space=pltpu.SMEM)
     hbm = pl.BlockSpec(memory_space=pl.ANY)
 
-    up = [(i, i + 1) for i in range(ranges - 1)]
-    down = [(j, i) for i, j in up]
+    exchanges = [
+        [pair for i in range(first, ranges - 1, 2) for pair in ((i, i + 1), (i + 1, i))]
+        for first in range(2)
+    ]
     last_block = atoms // span - 1
-    to_up, to_down = pl.pallas_call(
+    to_send = pl.pallas_call(
         payload_kernel,
         out_shape=[jax.ShapeDtypeStruct((samples * span + CODE_ROWS, channels), BF16)] * 2,
         grid=(1,),
@@ -506,8 +578,7 @@
         ],
         out_specs=[vmem, vmem],
     )(act, act, tok, padding)
-    halo_lo = lax.ppermute(to_up, "atoms", up)
-    halo_hi = lax.ppermute(to_down, "atoms", down)
+    halos = [lax.ppermute(part, "atoms", swaps) for part, swaps in zip(to_send, exchanges)]
 
     out_half = 5 * channels // 2
     part_rows = out_half + SMALL_ROWS
@@ -516,7 +587,6 @@
     pair_flat = pair.reshape(windows, win_rows * cp, span)
     width = heads * half_rows
     common = (
-        place,
         offsets,
         padding,
         w_token,
@@ -536,7 +606,7 @@
     def call(sides, halos=(), acc_in=None, last=False):
         edge, chained = len(halos) > 0, acc_in is not None
         args = common + tuple(halos) + ((acc_in,) if chained else ())
-        in_specs = [smem] * 4 + [vmem] + [hbm] * 3 + [vmem] * 6 + [hbm] * len(halos)
+        in_specs = [smem] * 3 + [vmem] + [hbm] * 3 + [vmem] * 6 + [hbm] * len(halos)
         in_specs += [vmem] * chained
         count = sum(side.count for side in sides)
         queries, rows = sides[0].queries, sides[0].rows
@@ -549,6 +619,10 @@
             out_shape += [shape((part_rows, channels), F32), shape((coded_rows, channels), BF16)]
         else:
             out_shape += [shape((2, part_rows, channels), F32)]
+        out_specs = [vmem] * (len(out_shape) + 2)
+        if edge:
+            at = len(own_rows)
+            out_specs[at : at + 2] = [hbm] * 2
         out_shape += [shape((count, width, span), F32), shape((count, width, span), BF16)]
         per_query = (blocks, queries, channels)
         scratch = [
@@ -569,18 +643,23 @@
             pltpu.VMEM(per_query, BF16),
             pltpu.VMEM(per_query, BF16),
             pltpu.VMEM(per_query, BF16),
-            pltpu.VMEM((span, lanes), F32),
-            pltpu.VMEM((span, lanes), F32),
+            pltpu.VMEM((2, span, lanes), F32),
+            pltpu.VMEM((2, span, lanes), F32),
         ]
         if last:
             scratch += [pltpu.VMEM((2, part_rows, channels), F32)]
+        if edge:
+            scratch += [
+                pltpu.VMEM((2, samples, span, channels), BF16),
+                pltpu.SemaphoreType.DMA((2,)),
+            ]
         scratch += [pltpu.VMEM((rows, channels), F32)] * (4 * blocks)
         units = 6 * count * samples + 8 * count + 14 * blocks
         return pl.pallas_call(
             functools.partial(attention_kernel, geo, sides, edge, chained, last),
             out_shape=out_shape,
             in_specs=in_specs,
-            out_specs=[vmem] * len(out_shape),
+            out_specs=out_specs,
             scratch_shapes=scratch,
             compiler_params=pltpu.CompilerParams(vmem_limit_bytes=VMEM_LIMIT),
             cost_estimate=pl.CostEstimate(
@@ -612,12 +691,11 @@
         [("act", atoms - own, own, 0), ("hi", 0, span, own)],
         atoms - own,
     )
-    ga_low, ga_high, ga_lo, ga_hi, acc, mine2, other2 = call(
-        [low_side, high_side], (halo_lo, halo_hi), acc
-    )
+    ga_low, ga_high, ga_a, ga_b, acc, mine2, other2 = call([low_side, high_side], halos, acc)
     recv2 = lax.ppermute(other2, "samples", swap)
-    from_upper = lax.ppermute(ga_lo, "atoms", down)
-    from_lower = lax.ppermute(ga_hi, "atoms", up)
+    from_a, from_b = [
+        lax.ppermute(part, "atoms", swaps) for part, swaps in zip((ga_a, ga_b), exchanges)
+    ]
 
     late_rows = atoms - late_first
     late_side = Side(
@@ -637,8 +715,8 @@
             [sent[:wide], sent[wide : wide + SMALL_ROWS] + sent[wide + SMALL_ROWS :]]
         )
 
-    acc_other, other3, from_upper, from_lower = lax.optimization_barrier(
-        (acc_other, other3, from_upper, from_lower)
+    acc_other, other3, from_a, from_b = lax.optimization_barrier(
+        (acc_other, other3, from_a, from_b)
     )
     recv3 = lax.ppermute(other3, "samples", swap)
     total = acc_mine + decode(lax.ppermute(acc_other, "samples", swap))
@@ -658,23 +736,22 @@
         (late_first, ga_late),
         (0, ga_low),
         (atoms - own, ga_high),
-        (0, from_lower),
-        (atoms - span, from_upper),
     ]
+    parts = [part for _, part in pieces] + [from_a, from_b]
     grad_act = pl.pallas_call(
         functools.partial(act_sum_kernel, [first for first, _ in pieces]),
         out_shape=shape((samples, atoms, channels), BF16),
         grid=(2,),
         in_specs=[
             pl.BlockSpec((samples // 2,) + part.shape[1:], lambda s: (s, 0, 0))
-            for _, part in pieces
+            for part in parts
         ],
         out_specs=pl.BlockSpec((samples // 2, atoms, channels), lambda s: (s, 0, 0)),
         compiler_params=pltpu.CompilerParams(vmem_limit_bytes=VMEM_LIMIT),
         cost_estimate=pl.CostEstimate(
             flops=4 * samples * atoms * channels, bytes_accessed=6_000_000, transcendentals=0
         ),
-    )(*[part for _, part in pieces])
+    )(*parts)
     step = ranges // 2
     while step >= 1:
         if step == ranges // 4:
@@ -694,9 +771,9 @@
             shape((heads, cp), F32),
             shape((heads,), F32),
         ],
-        in_specs=[smem, vmem, vmem],
+        in_specs=[vmem, vmem],
         out_specs=[vmem, vmem, smem],
-    )(place, sent, got)
+    )(sent, got)
 
     return (
         grad_act,

time: 86.1 us -> 81.6 us (0.948)
  starting transfers between devices: 20.4 us -> 17.6 us
    ppermute x4, starting transfers between devices: 12.8 us -> 8.83 us  [per_device(): lax.ppermute(part, 'atoms', swaps)]
    ppermute x3, starting transfers between devices: 6.42 us -> 7.63 us  [per_device(): got = lax.ppermute(sent, 'atoms', [(i, i ^ step) for i in range(ranges)])]
  transfers between devices with their start and end apart: 12 -> 12, of which waited for: 4 -> 4; matrix products, arithmetic and copies ran while one was open for 1% -> 0% of each run, Pallas kernels for 35% -> 36%
where the time goes in v4:
time: 81.6 us; the launch traced here: 81.1 us
  Pallas kernels  50.4 us (62%)
  starting transfers between devices  17.6 us (22%)
  waiting for transfers between devices  8.68 us (11%)
  local copies, waits for them, and re-layouts  2.17 us (3%)
  between operations  1.86 us (2%)
    pallas_call x3, Pallas kernels, call(): pl.pallas_call(functools.partial(attention_kernel, geo, sides, edge, chai...  40.8 us
    ppermute x4, starting transfers between devices, per_device(): lax.ppermute(part, 'atoms', swaps)  8.83 us
    ppermute x3, starting transfers between devices, per_device(): got = lax.ppermute(sent, 'atoms', [(i, i ^ step) for i in range(ranges)])  7.63 us
    ppermute x3, waiting for transfers between devices, per_device(): got = lax.ppermute(sent, 'atoms', [(i, i ^ step) for i in range(ranges)])  7.38 us
    pallas_call x1, Pallas kernels, per_device(): pl.pallas_call(functools.partial(act_sum_kernel, [first for first, _ in p...  3.02 us
    pallas_call x1, Pallas kernels, per_device(): pl.pallas_call(functools.partial(pair_kernel, order=(early, low + high, l...  2.96 us
    unnamed x24, local copies, waits for them, and re-layouts  2.08 us
    pallas_call x1, Pallas kernels, per_device(): pl.pallas_call(payload_kernel, out_shape=[jax.ShapeDtypeStruct((samples *...  1.88 us
  transfers between devices with their start and end apart: 12, of which 4 were waited for; matrix products, arithmetic and copies ran while one was open for 0% of the time, Pallas kernels for 36%

profile of v4, /device:TPU:0, one launch (start us, length us, event | category | flops | bytes accessed | tf_op | source)
XLA Modules:
  0.0 81.1 jit_solution(3467011915581286708)
XLA Ops:
  1.3 1.9 %shard_map.164 = (bf16[1040,128]{1,0:T(8,128)(2,1)}, bf16[1040,128]{1,0:T(8,128)(2,1)}) custom-call(bf16[8,640,128]{2,1,0:T(8,128)(2,1)} %refs_4_.5, bf16[8,640,128]{2,1,0:T(8,128)(2,1)} %refs_4_.5, s32[5,128]{1,0:T(8,128)} %bitcast.6, s32[1]{0:T(128)S(6)} %copy.18.padding_ref.refs_1_), custom_call_target="tpu_custom_call" | custom-call | tf_op jit(solution)/shard_map/pallas_call | solution.py:569
  3.2 2.9 %collective-permute-start = (bf16[1040,128]{1,0:T(8,128)(2,1)}, bf16[1040,128]{1,0:T(8,128)(2,1)S(1)}, u32[]{:S(2)}, u32[]{:S(2)}) collective-permute-start(bf16[1040,128]{1,0:T(8,128)(2,1)} %get-tuple-element.34), channel_id=1, source_target_pairs={{0,2},{2,0},{4,6},{6,4},{8,10},{10,8},{12,14},{14,12},{1,3},{3,1},... | collective-permute-start | bytes 798728 | tf_op jit(solution)/shard_map/ppermute | solution.py:581
  6.1 0.7 collective-permute-start.1
  6.8 11.4 %shard_map.165 = (bf16[8,448,128]{2,1,0:T(8,128)(2,1)}, f32[2,336,128]{2,1,0:T(8,128)}, f32[6,64,128]{2,1,0:T(8,128)}, bf16[6,64,128]{2,1,0:T(8,128)(2,1)}) custom-call(s32[20]{0:T(128)} %refs_0_.5, s32[1]{0:T(128)S(6)} %copy.18.padding_ref.refs_1_, f32[4]{0:T(128)} %refs_2_.5, s32[5,128]{1,0:T(8,128)} %bitcast.7, bf16[8,640,128]{2,1,0:T(8,128)(2,1)} %refs_4_.5, ...), custom_call_target="tpu_custom_call" | custom-call | flops 7516192768 | bytes 12000000 | tf_op jit(solution)/shard_map/pallas_call | solution.py:658
  18.3 0.7 copy-done.5
  19.0 17.5 %shard_map.166 = (bf16[8,256,128]{2,1,0:T(8,128)(2,1)}, bf16[8,256,128]{2,1,0:T(8,128)(2,1)}, bf16[8,128,128]{2,1,0:T(8,128)(2,1)}, bf16[8,128,128]{2,1,0:T(8,12...) custom-call(s32[20]{0:T(128)} %refs_0_.5, s32[1]{0:T(128)S(6)} %copy.18.padding_ref.refs_1_, ...), custom_call_target="tpu_custom_call" | custom-call | flops 11274289152 | bytes 12000000 | tf_op jit(solution)/shard_map/pallas_call | solution.py:658
  36.6 4.4 %collective-permute-start.2 = (bf16[8,128,128]{2,1,0:T(8,128)(2,1)}, bf16[8,128,128]{2,1,0:T(8,128)(2,1)S(1)}, u32[]{:S(2)}, u32[]{:S(2)}) collective-permute-start(bf16[8,128,128]{2,1,0:T(8,128)(2,1)} %get-tuple-element.41), channel_id=1, source_target_pairs={{0,2},{2,0},{4,6},{6,4},{8,10},{10,8},{12,14},{14,12},{1,3},{3,1},... | collective-permute-start | bytes 786440 | tf_op jit(solution)/shard_map/ppermute | solution.py:697
  40.9 0.8 %collective-permute-start.3 = (bf16[8,128,128]{2,1,0:T(8,128)(2,1)}, bf16[8,128,128]{2,1,0:T(8,128)(2,1)S(1)}, u32[]{:S(2)}, u32[]{:S(2)}) collective-permute-start(bf16[8,128,128]{2,1,0:T(8,128)(2,1)} %get-tuple-element.42), channel_id=1, source_target_pairs={{2,4},{4,2},{6,8},{8,6},{10,12},{12,10},{3,5},{5,3},{7,9},{9,7},{1... | collective-permute-start | bytes 786440 | tf_op jit(solution)/shard_map/ppermute | solution.py:697
  41.8 11.8 %shard_map.167 = (bf16[8,448,128]{2,1,0:T(8,128)(2,1)}, f32[336,128]{1,0:T(8,128)}, bf16[352,128]{1,0:T(8,128)(2,1)}, f32[6,64,128]{2,1,0:T(8,128)}, bf16[6,64,128]{2,1,0:T(8,128)(2,1)}) custom-call(s32[20]{0:T(128)} %refs_0_.5, s32[1]{0:T(128)S(6)} %copy.18.padding_ref.refs_1_, f32[4]{0:T(128)} %refs_2_.5, s32[5,128]{1,0:T(8,128)} %bitcast.9, ...), custom_call_target="tpu_custom_call" | custom-call | flops 7516192768 | bytes 12000000 | tf_op jit(solution)/shard_map/pallas_call | solution.py:658
  53.8 0.5 collective-permute-start.6
  54.3 0.1 collective-permute-start.7
  54.4 0.4 collective-permute-start.8
  54.8 3.0 %shard_map.169 = bf16[8,640,128]{2,1,0:T(8,128)(2,1)} custom-call(bf16[8,448,128]{2,1,0:T(8,128)(2,1)} %get-tuple-element.51.refs_0_, bf16[8,448,128]{2,1,0:T(8,128)(2,1)} %get-tuple-element.52.refs_1_, bf16[8,256,128]{2,1,0:T(8,128)(2,1)} %get-tuple-element.53.refs_2_, bf16[8,256,128]{2,1,0:T(8,128)(2,1)} %get-tuple-element.54.refs_3_, ...), custom_call_target="tpu_custom_call" | custom-call | flops 2621440 | bytes 6000000 | tf_op jit(solution)/shard_map/pallas_call | solution.py:741
  58.0 3.6 %collective-permute-start.5 = (bf16[352,128]{1,0:T(8,128)(2,1)S(1)}, bf16[352,128]{1,0:T(8,128)(2,1)S(1)}, u32[]{:S(2)}, u32[]{:S(2)}) collective-permute-start(bf16[352,128]{1,0:T(8,128)(2,1)S(1)} %get-tuple-element.75), channel_id=1, source_target_pairs={{0,8},{2,10},{4,12},{6,14},{8,0},{10,2},{12,4},{14,6},{1,9},{3,11}... | collective-permute-start | bytes 270344 | tf_op jit(solution)/shard_map/ppermute | solution.py:762
  61.7 0.6 copy-done.10
  62.4 3.0 %shard_map.168 = bf16[20,256,128]{2,1,0:T(8,128)(2,1)} custom-call(bf16[4,16]{1,0:T(4,128)(2,1)} %bitcast.18, f32[6,64,128]{2,1,0:T(8,128)} %get-tuple-element.44.refs_0_, bf16[6,64,128]{2,1,0:T(8,128)(2,1)} %copy-done.10, f32[8,64,128]{2,1,0:T(8,128)} %get-tuple-element.46.refs_2_, bf16[8,64,128]{2,1,0:T(8,128)(2,1)} %copy-done.8, ...), custom_call_target="tpu_custom_call" | custom-call | flops 671088640 | bytes 4000000 | tf_op jit(solution)/shard_map/pallas_call | solution.py:723
  65.3 1.1 %collective-permute-done.5 = bf16[352,128]{1,0:T(8,128)(2,1)S(1)} collective-permute-done((bf16[352,128]{1,0:T(8,128)(2,1)S(1)}, bf16[352,128]{1,0:T(8,128)(2,1)S(1)}, u32[]{:S(2)}, u32[]{:S(2)}) %collective-permute-start.5) | collective-permute-done | bytes 90144 | tf_op jit(solution)/shard_map/ppermute | solution.py:762
  66.6 0.8 collective-permute-start.9
  67.4 3.8 %collective-permute-done.9 = bf16[352,128]{1,0:T(8,128)(2,1)S(1)} collective-permute-done((bf16[352,128]{1,0:T(8,128)(2,1)S(1)}, bf16[352,128]{1,0:T(8,128)(2,1)S(1)}, u32[]{:S(2)}, u32[]{:S(2)}) %collective-permute-start.9) | collective-permute-done | bytes 90144 | tf_op jit(solution)/shard_map/ppermute | solution.py:762
  71.3 3.2 %collective-permute-start.10 = (bf16[352,128]{1,0:T(8,128)(2,1)S(1)}, bf16[352,128]{1,0:T(8,128)(2,1)S(1)}, u32[]{:S(2)}, u32[]{:S(2)}) collective-permute-start(bf16[352,128]{1,0:T(8,128)(2,1)S(1)} %get-tuple-element.72), channel_id=1, source_target_pairs={{0,2},{2,0},{4,6},{6,4},{8,10},{10,8},{12,14},{14,12},{1,3},{3,1},... | collective-permute-start | bytes 270344 | tf_op jit(solution)/shard_map/ppermute | solution.py:762
  74.6 2.5 %collective-permute-done.10 = bf16[352,128]{1,0:T(8,128)(2,1)S(1)} collective-permute-done((bf16[352,128]{1,0:T(8,128)(2,1)S(1)}, bf16[352,128]{1,0:T(8,128)(2,1)S(1)}, u32[]{:S(2)}, u32[]{:S(2)}) %collective-permute-start.10) | collective-permute-done | bytes 90144 | tf_op jit(solution)/shard_map/ppermute | solution.py:762
  77.3 1.3 %collective-permute-done.11.got_ref = bf16[352,128]{1,0:T(8,128)(2,1)S(1)} collective-permute-done((bf16[352,128]{1,0:T(8,128)(2,1)S(1)}, bf16[352,128]{1,0:T(8,128)(2,1)S(1)}, u32[]{:S(2)}, u32[]{:S(2)}) %collective-permute-start.11) | collective-permute-done | bytes 90144 | tf_op jit(solution)/shard_map/ppermute | solution.py:766
  78.6 0.6 copy-done.4
  79.2 1.8 %shard_map.170 = (f32[640,128]{1,0:T(8,128)}, f32[4,16]{1,0:T(4,128)}, f32[4]{0:T(128)}) custom-call(bf16[352,128]{1,0:T(8,128)(2,1)} %copy-done, bf16[352,128]{1,0:T(8,128)(2,1)} %copy-done.4), custom_call_target="tpu_custom_call" | custom-call | tf_op jit(solution)/shard_map/pallas_call | solution.py:767
  (65 shorter events, 0.8 us)
Async XLA Ops:
  3.2 15.1 %collective-permute-start = (bf16[1040,128]{1,0:T(8,128)(2,1)}, bf16[1040,128]{1,0:T(8,128)(2,1)S(1)}, u32[]{:S(2)}, u32[]{:S(2)}) collective-permute-start(bf16[1040,128]{1,0:T(8,128)(2,1)} %get-tuple-element.34), channel_id=1, source_target_pairs={{0,2},{2,0},{4,6},{6,4},{8,10},{10,8},{12,14},{14,12},{1,3},{3,1},... | collective-permute-start | bytes 798728 | tf_op jit(solution)/shard_map/ppermute | solution.py:581
  6.1 12.1 %collective-permute-start.1 = (bf16[1040,128]{1,0:T(8,128)(2,1)}, bf16[1040,128]{1,0:T(8,128)(2,1)S(1)}, u32[]{:S(2)}, u32[]{:S(2)}) collective-permute-start(bf16[1040,128]{1,0:T(8,128)(2,1)} %get-tuple-element.35), channel_id=1, source_target_pairs={{2,4},{4,2},{6,8},{8,6},{10,12},{12,10},{3,5},{5,3},{7,9},{9,7},{1... | collective-permute-start | bytes 798728 | tf_op jit(solution)/shard_map/ppermute | solution.py:581
  18.2 0.7 copy-start.5
  18.2 0.8 copy-start.6
  36.6 17.1 %collective-permute-start.2 = (bf16[8,128,128]{2,1,0:T(8,128)(2,1)}, bf16[8,128,128]{2,1,0:T(8,128)(2,1)S(1)}, u32[]{:S(2)}, u32[]{:S(2)}) collective-permute-start(bf16[8,128,128]{2,1,0:T(8,128)(2,1)} %get-tuple-element.41), channel_id=1, source_target_pairs={{0,2},{2,0},{4,6},{6,4},{8,10},{10,8},{12,14},{14,12},{1,3},{3,1},... | collective-permute-start | bytes 786440 | tf_op jit(solution)/shard_map/ppermute | solution.py:697
  40.9 12.8 %collective-permute-start.3 = (bf16[8,128,128]{2,1,0:T(8,128)(2,1)}, bf16[8,128,128]{2,1,0:T(8,128)(2,1)S(1)}, u32[]{:S(2)}, u32[]{:S(2)}) collective-permute-start(bf16[8,128,128]{2,1,0:T(8,128)(2,1)} %get-tuple-element.42), channel_id=1, source_target_pairs={{2,4},{4,2},{6,8},{8,6},{10,12},{12,10},{3,5},{5,3},{7,9},{9,7},{1... | collective-permute-start | bytes 786440 | tf_op jit(solution)/shard_map/ppermute | solution.py:697
  41.8 12.0 %copy-start.9 = (bf16[6,64,128]{2,1,0:T(8,128)(2,1)S(1)}, bf16[6,64,128]{2,1,0:T(8,128)(2,1)}, u32[]{:S(2)}) copy-start(bf16[6,64,128]{2,1,0:T(8,128)(2,1)} %get-tuple-element.45) | copy-start | bytes 294916
  41.8 12.5 %copy-start.7 = (bf16[8,64,128]{2,1,0:T(8,128)(2,1)S(1)}, bf16[8,64,128]{2,1,0:T(8,128)(2,1)}, u32[]{:S(2)}) copy-start(bf16[8,64,128]{2,1,0:T(8,128)(2,1)} %get-tuple-element.47) | copy-start | bytes 393220
  53.7 1.1 %copy-start.1 = (bf16[8,128,128]{2,1,0:T(8,128)(2,1)}, bf16[8,128,128]{2,1,0:T(8,128)(2,1)S(1)}, u32[]{:S(2)}) copy-start(bf16[8,128,128]{2,1,0:T(8,128)(2,1)S(1)} %collective-permute-done.2.refs_4_) | copy-start | bytes 786436
  53.7 1.1 %copy-start.2 = (bf16[8,128,128]{2,1,0:T(8,128)(2,1)}, bf16[8,128,128]{2,1,0:T(8,128)(2,1)S(1)}, u32[]{:S(2)}) copy-start(bf16[8,128,128]{2,1,0:T(8,128)(2,1)S(1)} %collective-permute-done.3.refs_5_) | copy-start | bytes 786436
  53.7 4.1 %collective-permute-start.4 = (bf16[352,128]{1,0:T(8,128)(2,1)}, bf16[352,128]{1,0:T(8,128)(2,1)S(1)}, u32[]{:S(2)}, u32[]{:S(2)}) collective-permute-start(bf16[352,128]{1,0:T(8,128)(2,1)} %get-tuple-element.43), channel_id=1, source_target_pairs={{0,1},{1,0},{2,3},{3,2},{4,5},{5,4},{6,7},{7,6},{8,9},{9,8},{10,11... | collective-permute-start | bytes 270344 | tf_op jit(solution)/shard_map/ppermute | solution.py:722
  53.8 7.8 %collective-permute-start.6 = (bf16[6,64,128]{2,1,0:T(8,128)(2,1)S(1)}, bf16[6,64,128]{2,1,0:T(8,128)(2,1)S(1)}, u32[]{:S(2)}, u32[]{:S(2)}) collective-permute-start(bf16[6,64,128]{2,1,0:T(8,128)(2,1)S(1)} %copy-done.9), channel_id=1, source_target_pairs={{0,1},{1,0},{2,3},{3,2},{4,5},{5,4},{6,7},{7,6},{8,9},{9,8},{10,11... | collective-permute-start | bytes 294920 | tf_op jit(solution)/shard_map/ppermute | solution.py:684
  54.3 7.4 %collective-permute-start.7 = (bf16[8,64,128]{2,1,0:T(8,128)(2,1)S(1)}, bf16[8,64,128]{2,1,0:T(8,128)(2,1)S(1)}, u32[]{:S(2)}, u32[]{:S(2)}) collective-permute-start(bf16[8,64,128]{2,1,0:T(8,128)(2,1)S(1)} %copy-done.7), channel_id=1, source_target_pairs={{0,1},{1,0},{2,3},{3,2},{4,5},{5,4},{6,7},{7,6},{8,9},{9,8},{10,11... | collective-permute-start | bytes 393224 | tf_op jit(solution)/shard_map/ppermute | solution.py:695
  54.4 7.3 %collective-permute-start.8 = (bf16[6,64,128]{2,1,0:T(8,128)(2,1)}, bf16[6,64,128]{2,1,0:T(8,128)(2,1)S(1)}, u32[]{:S(2)}, u32[]{:S(2)}) collective-permute-start(bf16[6,64,128]{2,1,0:T(8,128)(2,1)} %get-tuple-element.49), channel_id=1, source_target_pairs={{0,1},{1,0},{2,3},{3,2},{4,5},{5,4},{6,7},{7,6},{8,9},{9,8},{10,11... | collective-permute-start | bytes 294920 | tf_op jit(solution)/shard_map/ppermute | solution.py:721
  54.8 3.1 %copy-start.3 = (f32[336,128]{1,0:T(8,128)S(1)}, f32[336,128]{1,0:T(8,128)}, u32[]{:S(2)}) copy-start(f32[336,128]{1,0:T(8,128)} %get-tuple-element.38) | copy-start | bytes 516100
  58.0 8.4 %collective-permute-start.5 = (bf16[352,128]{1,0:T(8,128)(2,1)S(1)}, bf16[352,128]{1,0:T(8,128)(2,1)S(1)}, u32[]{:S(2)}, u32[]{:S(2)}) collective-permute-start(bf16[352,128]{1,0:T(8,128)(2,1)S(1)} %get-tuple-element.75), channel_id=1, source_target_pairs={{0,8},{2,10},{4,12},{6,14},{8,0},{10,2},{12,4},{14,6},{1,9},{3,11}... | collective-permute-start | bytes 270344 | tf_op jit(solution)/shard_map/ppermute | solution.py:762
  61.6 0.7 copy-start.10
  61.7 0.7 copy-start.8
  61.7 0.7 copy-start.11
  66.6 4.6 %collective-permute-start.9 = (bf16[352,128]{1,0:T(8,128)(2,1)S(1)}, bf16[352,128]{1,0:T(8,128)(2,1)S(1)}, u32[]{:S(2)}, u32[]{:S(2)}) collective-permute-start(bf16[352,128]{1,0:T(8,128)(2,1)S(1)} %get-tuple-element.73), channel_id=1, source_target_pairs={{0,4},{2,6},{4,0},{6,2},{8,12},{10,14},{12,8},{14,10},{1,5},{3,7},... | collective-permute-start | bytes 270344 | tf_op jit(solution)/shard_map/ppermute | solution.py:762
  71.3 5.7 %collective-permute-start.10 = (bf16[352,128]{1,0:T(8,128)(2,1)S(1)}, bf16[352,128]{1,0:T(8,128)(2,1)S(1)}, u32[]{:S(2)}, u32[]{:S(2)}) collective-permute-start(bf16[352,128]{1,0:T(8,128)(2,1)S(1)} %get-tuple-element.72), channel_id=1, source_target_pairs={{0,2},{2,0},{4,6},{6,4},{8,10},{10,8},{12,14},{14,12},{1,3},{3,1},... | collective-permute-start | bytes 270344 | tf_op jit(solution)/shard_map/ppermute | solution.py:762
  77.2 1.4 %copy-start = (bf16[352,128]{1,0:T(8,128)(2,1)}, bf16[352,128]{1,0:T(8,128)(2,1)S(1)}, u32[]{:S(2)}) copy-start(bf16[352,128]{1,0:T(8,128)(2,1)S(1)} %pad_maximum_fusion.3.sent_ref) | copy-start | bytes 270340
  77.2 1.4 %collective-permute-start.11 = (bf16[352,128]{1,0:T(8,128)(2,1)S(1)}, bf16[352,128]{1,0:T(8,128)(2,1)S(1)}, u32[]{:S(2)}, u32[]{:S(2)}) collective-permute-start(bf16[352,128]{1,0:T(8,128)(2,1)S(1)} %pad_maximum_fusion.3.sent_ref), channel_id=1, source_target_pairs={{0,1},{1,0},{2,3},{3,2},{4,5},{5,4},{6,7},{7,6},{8,9},{9,8},{10,11... | collective-permute-start | bytes 270344 | tf_op jit(solution)/shard_map/ppermute | solution.py:766
  78.5 0.6 copy-start.4

commit v5 on v4

--- a/solution.py
+++ b/solution.py
@@ -63,17 +63,16 @@
     samples, span, _ = high_ref.shape
     rows = tok_ref.shape[0]
     atoms = rows * span
-    index = lax.broadcasted_iota(jnp.int32, (CODE_ROWS, span), 0)
+    index = lax.broadcasted_iota(jnp.int32, (span, span), 0)
     place = lax.broadcasted_iota(jnp.int32, (1, span), 1)
 
     def write(out_ref, act_ref, row):
-        for s in range(samples):
-            out_ref[s * span : (s + 1) * span, :] = act_ref[s]
+        out_ref[:samples] = act_ref[...]
         live = place + row * span < atoms - padding_ref[0]
         code = jnp.where(live, tok_ref[row : row + 1, :] + 1, 0)
         top, low = code // CODE_BASE, code % CODE_BASE
         both = jnp.where(index == 0, top, jnp.where(index == 1, low, 0))
-        out_ref[samples * span :, :] = both.astype(F32).astype(BF16)
+        out_ref[samples] = both.astype(F32).astype(BF16)
 
     is_odd = lax.axis_index("atoms") % 2 == 1
 
@@ -99,21 +98,23 @@
         halo_a, halo_b = take(2)
     if chained:
         (acc_in_ref,) = take(1)
-    ga_refs = take(len(sides))
+    ga_hbm = take(len(sides))
     if edge:
         ga_out_refs = take(2)
     if last:
         acc_mine_ref, acc_other_ref = take(2)
     else:
         (acc_ref,) = take(1)
-    mine_ref, other_ref = take(2)
+    mine_hbm, other_hbm = take(2)
     pair_ref, pair_sem, wexp_ref, pw_ref, code_ref, qcode_ref, halo_code_ref = take(7)
     act_ref, gout_ref, in_sem, q_ref, datt_ref, g_ref, gy_ref = take(7)
     dq_ref, dgate_ref, gated_ref, bias_ref, bsum_ref = take(5)
     if last:
         (acc_ref,) = take(1)
     if edge:
-        ga_halo_ref, ga_sem = take(2)
+        (ga_halo_ref,) = take(1)
+    ga_refs = take(len(sides))
+    mine_ref, other_ref, out_sem = take(3)
     n_blocks = len(sides) * samples
     k_refs = take(n_blocks)
     v_refs = take(n_blocks)
@@ -130,40 +131,41 @@
     odd = rank % 2
     is_odd = odd == 1
 
-    def halo_copy(source, row, rows, target, sem):
+    def halo_copy(source, place, target, sem):
         refs = (halo_a, halo_b) if source == "lo" else (halo_b, halo_a)
-        return HaloCopy(is_odd, *[ref.at[pl.ds(row, rows)] for ref in refs], target, sem)
-
-
-    block_copies = []
+        return HaloCopy(is_odd, *[ref.at[place] for ref in refs], target, sem)
+
+
+    part = samples // 2
+    part_copies = {}
     for n, side in enumerate(sides):
-        for s in range(samples):
-            block = n * samples + s
+        for s in range(0, samples, part):
+            run = pl.ds(s, part)
+            block_run = pl.ds(n * samples + s, part)
             mine = []
             for i, (source, row, rows, at) in enumerate(side.pieces):
-                target, sem = act_ref.at[block, pl.ds(at, rows)], in_sem.at[block, i]
+                target, sem = act_ref.at[block_run, pl.ds(at, rows)], in_sem.at[n, s // part, i]
                 if source == "act":
                     mine.append(
-                        pltpu.make_async_copy(act_hbm.at[s, pl.ds(row, rows)], target, sem)
+                        pltpu.make_async_copy(act_hbm.at[run, pl.ds(row, rows)], target, sem)
                     )
                 else:
-                    mine.append(halo_copy(source, s * span, rows, target, sem))
+                    mine.append(halo_copy(source, run, target, sem))
             mine.append(
                 pltpu.make_async_copy(
-                    gout_hbm.at[s, pl.ds(side.query_row, side.queries)],
-                    gout_ref.at[block],
-                    in_sem.at[block, 2],
+                    gout_hbm.at[run, pl.ds(side.query_row, side.queries)],
+                    gout_ref.at[block_run],
+                    in_sem.at[n, s // part, 2],
                 )
             )
-            block_copies.append(mine)
+            part_copies[n, s] = mine
     code_copies = []
     if edge:
         for i, source in enumerate(("lo", "hi")):
             code_copies.append(
                 halo_copy(
                     source,
-                    samples * span,
-                    CODE_ROWS,
+                    (samples, pl.ds(0, CODE_ROWS)),
                     halo_code_ref.at[i],
                     pair_sem.at[len(sides) + i],
                 )
@@ -181,7 +183,7 @@
         first += side.count
     for copy in code_copies:
         copy.start()
-    for copies in block_copies:
+    for copies in part_copies.values():
         for copy in copies:
             copy.start()
     for copy in pair_copies:
@@ -244,7 +246,7 @@
     for n, side in enumerate(sides):
         for s in range(samples):
             block = n * samples + s
-            for copy in block_copies[block]:
+            for copy in part_copies.get((n, s), []):
                 copy.wait()
             kv = dot(act_ref[block], w_kv)
             k_refs[block][...] = kv[:, :channels]
@@ -368,6 +370,15 @@
         if sides[0].count % 2:
             rest = [(0, sides[0], 0, sides[0].count - 1)]
             tok_sum = window_group(rest, 0, tok_sum)
+
+    out_copies = []
+
+    def send_out(source, target):
+        out_copies.append(pltpu.make_async_copy(source, target, out_sem.at[len(out_copies)]))
+        out_copies[-1].start()
+
+    send_out(mine_ref, mine_hbm)
+    send_out(other_ref, other_hbm)
 
     pending = []
     acc_kv = jnp.zeros((channels, 2 * channels), F32)
@@ -402,11 +413,11 @@
                     else:
                         ga_refs[n][s, low - piece_at : high - piece_at, :] = value
             pending.append((dkv_b, dqg))
-    ga_copies = []
     if edge:
         for i, out_ref in enumerate(ga_out_refs):
-            ga_copies.append(pltpu.make_async_copy(ga_halo_ref.at[i], out_ref, ga_sem.at[i]))
-            ga_copies[-1].start()
+            send_out(ga_halo_ref.at[i], out_ref)
+    for ga_ref, out_ref in zip(ga_refs, ga_hbm):
+        send_out(ga_ref, out_ref)
     for n, side in enumerate(sides):
         at = side.query_row - side.origin
         for s in range(samples):
@@ -448,8 +459,6 @@
                 part = part + acc_in_ref[half, at : at + rows, :]
             acc_ref[half, at : at + rows, :] = part
             at += rows
-    for copy in ga_copies:
-        copy.wait()
     if last:
         acc_mine_ref[...] = acc_ref[core]
         value = acc_ref[1 - core]
@@ -458,6 +467,8 @@
         acc_other_ref[: wide + SMALL_ROWS, :] = top
         rest = value[wide:] - top[wide:].astype(F32)
         acc_other_ref[wide + SMALL_ROWS :, :] = rest.astype(BF16)
+    for copy in out_copies:
+        copy.wait()
 
 
 def pair_kernel(wpair_ref, *refs, order, heads, cp):
@@ -568,7 +579,7 @@
     last_block = atoms // span - 1
     to_send = pl.pallas_call(
         payload_kernel,
-        out_shape=[jax.ShapeDtypeStruct((samples * span + CODE_ROWS, channels), BF16)] * 2,
+        out_shape=[jax.ShapeDtypeStruct((samples + 1, span, channels), BF16)] * 2,
         grid=(1,),
         in_specs=[
             pl.BlockSpec((samples, span, channels), lambda i: (0, last_block, 0)),
@@ -619,10 +630,7 @@
             out_shape += [shape((part_rows, channels), F32), shape((coded_rows, channels), BF16)]
         else:
             out_shape += [shape((2, part_rows, channels), F32)]
-        out_specs = [vmem] * (len(out_shape) + 2)
-        if edge:
-            at = len(own_rows)
-            out_specs[at : at + 2] = [hbm] * 2
+        out_specs = [hbm] * (len(own_rows) + 2 * edge) + [vmem] * (1 + last) + [hbm] * 2
         out_shape += [shape((count, width, span), F32), shape((count, width, span), BF16)]
         per_query = (blocks, queries, channels)
         scratch = [
@@ -635,7 +643,7 @@
             pltpu.VMEM((2, CODE_ROWS, span), BF16),
             pltpu.VMEM((blocks, rows, channels), BF16),
             pltpu.VMEM(per_query, BF16),
-            pltpu.SemaphoreType.DMA((blocks, 3)),
+            pltpu.SemaphoreType.DMA((len(sides), 2, 3)),
             pltpu.VMEM(per_query, BF16),
             pltpu.VMEM(per_query, BF16),
             pltpu.VMEM(per_query, F32),
@@ -651,8 +659,13 @@
         if edge:
             scratch += [
                 pltpu.VMEM((2, samples, span, channels), BF16),
-                pltpu.SemaphoreType.DMA((2,)),
             ]
+        scratch += [pltpu.VMEM((samples, n, channels), BF16) for n in own_rows]
+        scratch += [
+            pltpu.VMEM((count, width, span), F32),
+            pltpu.VMEM((count, width, span), BF16),
+            pltpu.SemaphoreType.DMA((len(sides) + 2 + 2 * edge,)),
+        ]
         scratch += [pltpu.VMEM((rows, channels), F32)] * (4 * blocks)
         units = 6 * count * samples + 8 * count + 14 * blocks
         return pl.pallas_call(
@@ -720,48 +733,62 @@
     )
     recv3 = lax.ppermute(other3, "samples", swap)
     total = acc_mine + decode(lax.ppermute(acc_other, "samples", swap))
-    grad_pair = pl.pallas_call(
-        functools.partial(pair_kernel, order=(early, low + high, late), heads=heads, cp=cp),
-        out_shape=shape((windows, half_rows * cp, span), BF16),
-        in_specs=[vmem] * 7,
-        out_specs=vmem,
-        compiler_params=pltpu.CompilerParams(vmem_limit_bytes=VMEM_LIMIT),
-        cost_estimate=pl.CostEstimate(
-            flops=2 * windows * 256 * 256 * 256, bytes_accessed=4_000_000, transcendentals=0
-        ),
-    )(w_pair_t, mine1, recv1, mine2, recv2, mine3, recv3)
-
-    pieces = [
-        (0, ga_early),
-        (late_first, ga_late),
-        (0, ga_low),
-        (atoms - own, ga_high),
-    ]
-    parts = [part for _, part in pieces] + [from_a, from_b]
-    grad_act = pl.pallas_call(
-        functools.partial(act_sum_kernel, [first for first, _ in pieces]),
-        out_shape=shape((samples, atoms, channels), BF16),
-        grid=(2,),
-        in_specs=[
-            pl.BlockSpec((samples // 2,) + part.shape[1:], lambda s: (s, 0, 0))
-            for part in parts
-        ],
-        out_specs=pl.BlockSpec((samples // 2, atoms, channels), lambda s: (s, 0, 0)),
-        compiler_params=pltpu.CompilerParams(vmem_limit_bytes=VMEM_LIMIT),
-        cost_estimate=pl.CostEstimate(
-            flops=4 * samples * atoms * channels, bytes_accessed=6_000_000, transcendentals=0
-        ),
-    )(*parts)
+    def sum_pair(mine3):
+        return pl.pallas_call(
+            functools.partial(pair_kernel, order=(early, low + high, late), heads=heads, cp=cp),
+            out_shape=shape((windows, half_rows * cp, span), BF16),
+            in_specs=[vmem] * 7,
+            out_specs=vmem,
+            compiler_params=pltpu.CompilerParams(vmem_limit_bytes=VMEM_LIMIT),
+            cost_estimate=pl.CostEstimate(
+                flops=2 * windows * 256 * 256 * 256, bytes_accessed=4_000_000, transcendentals=0
+            ),
+        )(w_pair_t, mine1, recv1, mine2, recv2, mine3, recv3)
+
+    def sum_act(ga_late):
+        pieces = [
+            (0, ga_early),
+            (late_first, ga_late),
+            (0, ga_low),
+            (atoms - own, ga_high),
+        ]
+        parts = [part for _, part in pieces] + [from_a, from_b]
+        return pl.pallas_call(
+            functools.partial(act_sum_kernel, [first for first, _ in pieces]),
+            out_shape=shape((samples, atoms, channels), BF16),
+            grid=(2,),
+            in_specs=[
+                pl.BlockSpec((samples // 2,) + part.shape[1:], lambda s: (s, 0, 0))
+                for part in parts
+            ],
+            out_specs=pl.BlockSpec((samples // 2, atoms, channels), lambda s: (s, 0, 0)),
+            compiler_params=pltpu.CompilerParams(vmem_limit_bytes=VMEM_LIMIT),
+            cost_estimate=pl.CostEstimate(
+                flops=4 * samples * atoms * channels, bytes_accessed=6_000_000, transcendentals=0
+            ),
+        )(*parts)
+
     step = ranges // 2
+    grad_pair = grad_act = None
     while step >= 1:
-        if step == ranges // 4:
-            total, grad_pair = lax.optimization_barrier((total, grad_pair))
-        if step == ranges // 8:
-            total, grad_act = lax.optimization_barrier((total, grad_act))
         sent = encode(total)
+        if grad_pair is None:
+            sent, mine3 = lax.optimization_barrier((sent, mine3))
+            grad_pair = sum_pair(mine3)
+        elif grad_act is None:
+            sent, ga_late = lax.optimization_barrier((sent, ga_late))
+            grad_act = sum_act(ga_late)
         got = lax.ppermute(sent, "atoms", [(i, i ^ step) for i in range(ranges)])
         total = decode(sent) + decode(got)
+        if step == ranges // 2:
+            total, grad_pair = lax.optimization_barrier((total, grad_pair))
+        elif step == ranges // 4:
+            total, grad_act = lax.optimization_barrier((total, grad_act))
         step //= 2
+    if grad_pair is None:
+        grad_pair = sum_pair(mine3)
+    if grad_act is None:
+        grad_act = sum_act(ga_late)
     sent = encode(total)
     got = lax.ppermute(sent, "samples", swap)
     grad_weights, grad_pair_weight, grad_token_weight = pl.pallas_call(

time: 81.6 us -> 76.1 us (0.933)
  Pallas kernels: 50.4 us -> 46.4 us
  starting transfers between devices: 17.6 us -> 16.4 us
  waiting for transfers between devices: 8.68 us -> 7.62 us
  other arithmetic: 0.36 us -> 1.28 us
    pallas_call x3, Pallas kernels: 40.8 us -> 36.8 us  [call(): pl.pallas_call(functools.partial(attention_kernel, geo, sides, edge, chai...]
    ppermute x3, waiting for transfers between devices: 7.38 us -> 4.37 us  [per_device(): got = lax.ppermute(sent, 'atoms', [(i, i ^ step) for i in range(ranges)])]
    ppermute x4, starting transfers between devices: 8.83 us -> 7.24 us  [per_device(): lax.ppermute(part, 'atoms', swaps)]
    ppermute x4, waiting for transfers between devices: 0.01 us -> 1.49 us  [per_device(): lax.ppermute(part, 'atoms', swaps)]
    another operation x8, other arithmetic: 0.13 us -> 1.05 us
    unnamed x24 -> x22, local copies, waits for them, and re-layouts: 2.08 us -> 2.12 us
  transfers between devices with their start and end apart: 12 -> 12, of which waited for: 4 -> 6; matrix products, arithmetic and copies ran while one was open for 0% -> 1% of each run, Pallas kernels for 36% -> 37%
where the time goes in v5:
time: 76.1 us; the launch traced here: 75.7 us
  Pallas kernels  46.4 us (61%)
  starting transfers between devices  16.4 us (22%)
  waiting for transfers between devices  7.62 us (10%)
  local copies, waits for them, and re-layouts  2.21 us (3%)
  between operations  1.86 us (2%)
  other arithmetic  1.28 us (2%)
    pallas_call x3, Pallas kernels, call(): pl.pallas_call(functools.partial(attention_kernel, geo, sides, edge, chai...  36.8 us
    ppermute x3, starting transfers between devices, per_device(): got = lax.ppermute(sent, 'atoms', [(i, i ^ step) for i in range(ranges)])  7.99 us
    ppermute x4, starting transfers between devices, per_device(): lax.ppermute(part, 'atoms', swaps)  7.24 us
    ppermute x3, waiting for transfers between devices, per_device(): got = lax.ppermute(sent, 'atoms', [(i, i ^ step) for i in range(ranges)])  4.37 us
    pallas_call x1, Pallas kernels, sum_act(): pl.pallas_call(functools.partial(act_sum_kernel, [first for first, _ in p...  3 us
    pallas_call x1, Pallas kernels, sum_pair(): pl.pallas_call(functools.partial(pair_kernel, order=(early, low + high, l...  2.96 us
    unnamed x22, local copies, waits for them, and re-layouts  2.12 us
    pallas_call x1, Pallas kernels, per_device(): pl.pallas_call(payload_kernel, out_shape=[jax.ShapeDtypeStruct((samples +...  1.9 us
  transfers between devices with their start and end apart: 12, of which 6 were waited for; matrix products, arithmetic and copies ran while one was open for 1% of the time, Pallas kernels for 37%

profile of v5, /device:TPU:0, one launch (start us, length us, event | category | flops | bytes accessed | tf_op | source)
XLA Modules:
  0.0 75.7 jit_solution(16820223028234164936)
XLA Ops:
  1.3 1.9 %shard_map.164 = (bf16[9,128,128]{2,1,0:T(8,128)(2,1)}, bf16[9,128,128]{2,1,0:T(8,128)(2,1)}) custom-call(bf16[8,640,128]{2,1,0:T(8,128)(2,1)} %refs_4_.5, bf16[8,640,128]{2,1,0:T(8,128)(2,1)} %refs_4_.5, s32[5,128]{1,0:T(8,128)} %bitcast.6, s32[1]{0:T(128)S(6)} %copy.18.padding_ref.refs_1_), custom_call_target="tpu_custom_call" | custom-call | tf_op jit(solution)/shard_map/pallas_call | solution.py:580
  3.2 2.9 %collective-permute-start = (bf16[9,128,128]{2,1,0:T(8,128)(2,1)}, bf16[9,128,128]{2,1,0:T(8,128)(2,1)S(1)}, u32[]{:S(2)}, u32[]{:S(2)}) collective-permute-start(bf16[9,128,128]{2,1,0:T(8,128)(2,1)} %get-tuple-element.38), channel_id=1, source_target_pairs={{0,2},{2,0},{4,6},{6,4},{8,10},{10,8},{12,14},{14,12},{1,3},{3,1},... | collective-permute-start | bytes 884744 | tf_op jit(solution)/shard_map/ppermute | solution.py:592
  6.1 0.7 collective-permute-start.1
  6.8 10.7 %shard_map.165 = (bf16[8,448,128]{2,1,0:T(8,128)(2,1)}, f32[2,336,128]{2,1,0:T(8,128)}, f32[6,64,128]{2,1,0:T(8,128)}, bf16[6,64,128]{2,1,0:T(8,128)(2,1)}) custom-call(s32[20]{0:T(128)} %refs_0_.5, s32[1]{0:T(128)S(6)} %copy.18.padding_ref.refs_1_, f32[4]{0:T(128)} %refs_2_.5, s32[5,128]{1,0:T(8,128)} %bitcast.7, bf16[8,640,128]{2,1,0:T(8,128)(2,1)} %refs_4_.5, ...), custom_call_target="tpu_custom_call" | custom-call | flops 7516192768 | bytes 12000000 | tf_op jit(solution)/shard_map/pallas_call | solution.py:671
  17.5 1.5 %collective-permute-done.refs_13_ = bf16[9,128,128]{2,1,0:T(8,128)(2,1)S(1)} collective-permute-done((bf16[9,128,128]{2,1,0:T(8,128)(2,1)}, bf16[9,128,128]{2,1,0:T(8,128)(2,1)S(1)}, u32[]{:S(2)}, u32[]{:S(2)}) %collective-permute-start) | collective-permute-done | bytes 294944 | tf_op jit(solution)/shard_map/ppermute | solution.py:592
  19.0 0.7 copy-done.4
  19.8 14.9 %shard_map.166 = (bf16[8,256,128]{2,1,0:T(8,128)(2,1)}, bf16[8,256,128]{2,1,0:T(8,128)(2,1)}, bf16[8,128,128]{2,1,0:T(8,128)(2,1)}, bf16[8,128,128]{2,1,0:T(8,12...) custom-call(s32[20]{0:T(128)} %refs_0_.5, s32[1]{0:T(128)S(6)} %copy.18.padding_ref.refs_1_, ...), custom_call_target="tpu_custom_call" | custom-call | flops 11274289152 | bytes 12000000 | tf_op jit(solution)/shard_map/pallas_call | solution.py:671
  34.7 2.8 %collective-permute-start.2 = (bf16[8,128,128]{2,1,0:T(8,128)(2,1)}, bf16[8,128,128]{2,1,0:T(8,128)(2,1)S(1)}, u32[]{:S(2)}, u32[]{:S(2)}) collective-permute-start(bf16[8,128,128]{2,1,0:T(8,128)(2,1)} %get-tuple-element.45), channel_id=1, source_target_pairs={{0,2},{2,0},{4,6},{6,4},{8,10},{10,8},{12,14},{14,12},{1,3},{3,1},... | collective-permute-start | bytes 786440 | tf_op jit(solution)/shard_map/ppermute | solution.py:710
  37.5 0.8 %collective-permute-start.3 = (bf16[8,128,128]{2,1,0:T(8,128)(2,1)}, bf16[8,128,128]{2,1,0:T(8,128)(2,1)S(1)}, u32[]{:S(2)}, u32[]{:S(2)}) collective-permute-start(bf16[8,128,128]{2,1,0:T(8,128)(2,1)} %get-tuple-element.46), channel_id=1, source_target_pairs={{2,4},{4,2},{6,8},{8,6},{10,12},{12,10},{3,5},{5,3},{7,9},{9,7},{1... | collective-permute-start | bytes 786440 | tf_op jit(solution)/shard_map/ppermute | solution.py:710
  38.4 11.1 %shard_map.167 = (bf16[8,448,128]{2,1,0:T(8,128)(2,1)}, f32[336,128]{1,0:T(8,128)}, bf16[352,128]{1,0:T(8,128)(2,1)}, f32[6,64,128]{2,1,0:T(8,128)}, bf16[6,64,128]{2,1,0:T(8,128)(2,1)}) custom-call(s32[20]{0:T(128)} %refs_0_.5, s32[1]{0:T(128)S(6)} %copy.18.padding_ref.refs_1_, f32[4]{0:T(128)} %refs_2_.5, s32[5,128]{1,0:T(8,128)} %bitcast.9, ...), custom_call_target="tpu_custom_call" | custom-call | flops 7516192768 | bytes 12000000 | tf_op jit(solution)/shard_map/pallas_call | solution.py:671
  49.7 0.5 collective-permute-start.6
  51.2 0.9 %reduce-precision_convert_fusion.3 = (bf16[336,128]{1,0:T(8,128)(2,1)S(1)}, f32[336,128]{1,0:T(8,128)S(1)}) fusion(f32[336,128]{1,0:T(8,128)} %get-tuple-element.42, f32[16,128]{1,0:T(8,128)S(1)} %slice_add_fusion.6, f32[320,128]{1,0:T(8,128)S(1)} %slice.116), kind=kLoop, calls=%fused_computation.26 | loop fusion | flops 172032 | bytes 602112 | tf_op jit(solution)/shard_map/convert.6
  52.2 3.9 %collective-permute-start.5 = (bf16[352,128]{1,0:T(8,128)(2,1)S(1)}, bf16[352,128]{1,0:T(8,128)(2,1)S(1)}, u32[]{:S(2)}, u32[]{:S(2)}) collective-permute-start(bf16[352,128]{1,0:T(8,128)(2,1)S(1)} %pad_maximum_fusion), channel_id=1, source_target_pairs={{0,8},{2,10},{4,12},{6,14},{8,0},{10,2},{12,4},{14,6},{1,9},{3,11}... | collective-permute-start | bytes 270344 | tf_op jit(solution)/shard_map/ppermute | solution.py:781
  56.3 0.6 copy-done.9
  56.9 3.0 %shard_map.168 = bf16[20,256,128]{2,1,0:T(8,128)(2,1)} custom-call(bf16[4,16]{1,0:T(4,128)(2,1)} %bitcast.18, f32[6,64,128]{2,1,0:T(8,128)} %get-tuple-element.50.refs_0_, bf16[6,64,128]{2,1,0:T(8,128)(2,1)} %copy-done.9, f32[8,64,128]{2,1,0:T(8,128)} %get-tuple-element.52.refs_2_, bf16[8,64,128]{2,1,0:T(8,128)(2,1)} %copy-done.7, ...), custom_call_target="tpu_custom_call" | custom-call | flops 671088640 | bytes 4000000 | tf_op jit(solution)/shard_map/pallas_call | solution.py:737
  59.9 1.1 %collective-permute-done.5 = bf16[352,128]{1,0:T(8,128)(2,1)S(1)} collective-permute-done((bf16[352,128]{1,0:T(8,128)(2,1)S(1)}, bf16[352,128]{1,0:T(8,128)(2,1)S(1)}, u32[]{:S(2)}, u32[]{:S(2)}) %collective-permute-start.5) | collective-permute-done | bytes 90144 | tf_op jit(solution)/shard_map/ppermute | solution.py:781
  61.2 0.8 %collective-permute-start.9 = (bf16[352,128]{1,0:T(8,128)(2,1)S(1)}, bf16[352,128]{1,0:T(8,128)(2,1)S(1)}, u32[]{:S(2)}, u32[]{:S(2)}) collective-permute-start(bf16[352,128]{1,0:T(8,128)(2,1)S(1)} %pad_maximum_fusion.1), channel_id=1, source_target_pairs={{0,4},{2,6},{4,0},{6,2},{8,12},{10,14},{12,8},{14,10},{1,5},{3,7},... | collective-permute-start | bytes 270344 | tf_op jit(solution)/shard_map/ppermute | solution.py:781
  62.0 3.0 %shard_map.169 = bf16[8,640,128]{2,1,0:T(8,128)(2,1)} custom-call(bf16[8,448,128]{2,1,0:T(8,128)(2,1)} %get-tuple-element.59.refs_0_, bf16[8,448,128]{2,1,0:T(8,128)(2,1)} %get-tuple-element.60.refs_1_, bf16[8,256,128]{2,1,0:T(8,128)(2,1)} %get-tuple-element.61.refs_2_, bf16[8,256,128]{2,1,0:T(8,128)(2,1)} %get-tuple-element.62.refs_3_, ...), custom_call_target="tpu_custom_call" | custom-call | flops 2621440 | bytes 6000000 | tf_op jit(solution)/shard_map/pallas_call | solution.py:756
  65.0 0.7 collective-permute-done.9
  65.9 3.3 %collective-permute-start.10 = (bf16[352,128]{1,0:T(8,128)(2,1)S(1)}, bf16[352,128]{1,0:T(8,128)(2,1)S(1)}, u32[]{:S(2)}, u32[]{:S(2)}) collective-permute-start(bf16[352,128]{1,0:T(8,128)(2,1)S(1)} %get-tuple-element.80), channel_id=1, source_target_pairs={{0,2},{2,0},{4,6},{6,4},{8,10},{10,8},{12,14},{14,12},{1,3},{3,1},... | collective-permute-start | bytes 270344 | tf_op jit(solution)/shard_map/ppermute | solution.py:781
  69.2 2.5 %collective-permute-done.10 = bf16[352,128]{1,0:T(8,128)(2,1)S(1)} collective-permute-done((bf16[352,128]{1,0:T(8,128)(2,1)S(1)}, bf16[352,128]{1,0:T(8,128)(2,1)S(1)}, u32[]{:S(2)}, u32[]{:S(2)}) %collective-permute-start.10) | collective-permute-done | bytes 90144 | tf_op jit(solution)/shard_map/ppermute | solution.py:781
  71.9 1.3 %collective-permute-done.11.got_ref = bf16[352,128]{1,0:T(8,128)(2,1)S(1)} collective-permute-done((bf16[352,128]{1,0:T(8,128)(2,1)S(1)}, bf16[352,128]{1,0:T(8,128)(2,1)S(1)}, u32[]{:S(2)}, u32[]{:S(2)}) %collective-permute-start.11) | collective-permute-done | bytes 90144 | tf_op jit(solution)/shard_map/ppermute | solution.py:793
  73.2 0.6 copy-done.3
  73.8 1.8 %shard_map.170 = (f32[640,128]{1,0:T(8,128)}, f32[4,16]{1,0:T(4,128)}, f32[4]{0:T(128)}) custom-call(bf16[352,128]{1,0:T(8,128)(2,1)} %copy-done, bf16[352,128]{1,0:T(8,128)(2,1)} %copy-done.3), custom_call_target="tpu_custom_call" | custom-call | tf_op jit(solution)/shard_map/pallas_call | solution.py:794
  (65 shorter events, 1.8 us)
Async XLA Ops:
  3.2 15.8 %collective-permute-start = (bf16[9,128,128]{2,1,0:T(8,128)(2,1)}, bf16[9,128,128]{2,1,0:T(8,128)(2,1)S(1)}, u32[]{:S(2)}, u32[]{:S(2)}) collective-permute-start(bf16[9,128,128]{2,1,0:T(8,128)(2,1)} %get-tuple-element.38), channel_id=1, source_target_pairs={{0,2},{2,0},{4,6},{6,4},{8,10},{10,8},{12,14},{14,12},{1,3},{3,1},... | collective-permute-start | bytes 884744 | tf_op jit(solution)/shard_map/ppermute | solution.py:592
  6.1 12.9 %collective-permute-start.1 = (bf16[9,128,128]{2,1,0:T(8,128)(2,1)}, bf16[9,128,128]{2,1,0:T(8,128)(2,1)S(1)}, u32[]{:S(2)}, u32[]{:S(2)}) collective-permute-start(bf16[9,128,128]{2,1,0:T(8,128)(2,1)} %get-tuple-element.39), channel_id=1, source_target_pairs={{2,4},{4,2},{6,8},{8,6},{10,12},{12,10},{3,5},{5,3},{7,9},{9,7},{1... | collective-permute-start | bytes 884744 | tf_op jit(solution)/shard_map/ppermute | solution.py:592
  19.0 0.7 copy-start.4
  19.0 0.8 %copy-start.5 = (bf16[9,128,128]{2,1,0:T(8,128)(2,1)}, bf16[9,128,128]{2,1,0:T(8,128)(2,1)S(1)}, u32[]{:S(2)}) copy-start(bf16[9,128,128]{2,1,0:T(8,128)(2,1)S(1)} %collective-permute-done.1.refs_14_) | copy-start | bytes 884740
  34.7 14.8 %collective-permute-start.2 = (bf16[8,128,128]{2,1,0:T(8,128)(2,1)}, bf16[8,128,128]{2,1,0:T(8,128)(2,1)S(1)}, u32[]{:S(2)}, u32[]{:S(2)}) collective-permute-start(bf16[8,128,128]{2,1,0:T(8,128)(2,1)} %get-tuple-element.45), channel_id=1, source_target_pairs={{0,2},{2,0},{4,6},{6,4},{8,10},{10,8},{12,14},{14,12},{1,3},{3,1},... | collective-permute-start | bytes 786440 | tf_op jit(solution)/shard_map/ppermute | solution.py:710
  37.5 12.0 %collective-permute-start.3 = (bf16[8,128,128]{2,1,0:T(8,128)(2,1)}, bf16[8,128,128]{2,1,0:T(8,128)(2,1)S(1)}, u32[]{:S(2)}, u32[]{:S(2)}) collective-permute-start(bf16[8,128,128]{2,1,0:T(8,128)(2,1)} %get-tuple-element.46), channel_id=1, source_target_pairs={{2,4},{4,2},{6,8},{8,6},{10,12},{12,10},{3,5},{5,3},{7,9},{9,7},{1... | collective-permute-start | bytes 786440 | tf_op jit(solution)/shard_map/ppermute | solution.py:710
  38.4 11.3 %copy-start.8 = (bf16[6,64,128]{2,1,0:T(8,128)(2,1)S(1)}, bf16[6,64,128]{2,1,0:T(8,128)(2,1)}, u32[]{:S(2)}) copy-start(bf16[6,64,128]{2,1,0:T(8,128)(2,1)} %get-tuple-element.51) | copy-start | bytes 294916
  38.4 11.8 %copy-start.6 = (bf16[8,64,128]{2,1,0:T(8,128)(2,1)S(1)}, bf16[8,64,128]{2,1,0:T(8,128)(2,1)}, u32[]{:S(2)}) copy-start(bf16[8,64,128]{2,1,0:T(8,128)(2,1)} %get-tuple-element.53) | copy-start | bytes 393220
  49.6 10.3 %copy-start.1 = (bf16[8,128,128]{2,1,0:T(8,128)(2,1)}, bf16[8,128,128]{2,1,0:T(8,128)(2,1)S(1)}, u32[]{:S(2)}) copy-start(bf16[8,128,128]{2,1,0:T(8,128)(2,1)S(1)} %collective-permute-done.2.refs_4_) | copy-start | bytes 786436
  49.6 10.3 %copy-start.2 = (bf16[8,128,128]{2,1,0:T(8,128)(2,1)}, bf16[8,128,128]{2,1,0:T(8,128)(2,1)S(1)}, u32[]{:S(2)}) copy-start(bf16[8,128,128]{2,1,0:T(8,128)(2,1)S(1)} %collective-permute-done.3.refs_5_) | copy-start | bytes 786436
  49.6 1.6 %collective-permute-start.4 = (bf16[352,128]{1,0:T(8,128)(2,1)}, bf16[352,128]{1,0:T(8,128)(2,1)S(1)}, u32[]{:S(2)}, u32[]{:S(2)}) collective-permute-start(bf16[352,128]{1,0:T(8,128)(2,1)} %get-tuple-element.47), channel_id=1, source_target_pairs={{0,1},{1,0},{2,3},{3,2},{4,5},{5,4},{6,7},{7,6},{8,9},{9,8},{10,11... | collective-permute-start | bytes 270344 | tf_op jit(solution)/shard_map/ppermute | solution.py:735
  49.7 6.5 %collective-permute-start.6 = (bf16[6,64,128]{2,1,0:T(8,128)(2,1)S(1)}, bf16[6,64,128]{2,1,0:T(8,128)(2,1)S(1)}, u32[]{:S(2)}, u32[]{:S(2)}) collective-permute-start(bf16[6,64,128]{2,1,0:T(8,128)(2,1)S(1)} %copy-done.8), channel_id=1, source_target_pairs={{0,1},{1,0},{2,3},{3,2},{4,5},{5,4},{6,7},{7,6},{8,9},{9,8},{10,11... | collective-permute-start | bytes 294920 | tf_op jit(solution)/shard_map/ppermute | solution.py:697
  50.2 6.0 %collective-permute-start.7 = (bf16[8,64,128]{2,1,0:T(8,128)(2,1)S(1)}, bf16[8,64,128]{2,1,0:T(8,128)(2,1)S(1)}, u32[]{:S(2)}, u32[]{:S(2)}) collective-permute-start(bf16[8,64,128]{2,1,0:T(8,128)(2,1)S(1)} %copy-done.6), channel_id=1, source_target_pairs={{0,1},{1,0},{2,3},{3,2},{4,5},{5,4},{6,7},{7,6},{8,9},{9,8},{10,11... | collective-permute-start | bytes 393224 | tf_op jit(solution)/shard_map/ppermute | solution.py:708
  50.3 6.0 %collective-permute-start.8 = (bf16[6,64,128]{2,1,0:T(8,128)(2,1)}, bf16[6,64,128]{2,1,0:T(8,128)(2,1)S(1)}, u32[]{:S(2)}, u32[]{:S(2)}) collective-permute-start(bf16[6,64,128]{2,1,0:T(8,128)(2,1)} %get-tuple-element.55), channel_id=1, source_target_pairs={{0,1},{1,0},{2,3},{3,2},{4,5},{5,4},{6,7},{7,6},{8,9},{9,8},{10,11... | collective-permute-start | bytes 294920 | tf_op jit(solution)/shard_map/ppermute | solution.py:734
  52.2 8.8 %collective-permute-start.5 = (bf16[352,128]{1,0:T(8,128)(2,1)S(1)}, bf16[352,128]{1,0:T(8,128)(2,1)S(1)}, u32[]{:S(2)}, u32[]{:S(2)}) collective-permute-start(bf16[352,128]{1,0:T(8,128)(2,1)S(1)} %pad_maximum_fusion), channel_id=1, source_target_pairs={{0,8},{2,10},{4,12},{6,14},{8,0},{10,2},{12,4},{14,6},{1,9},{3,11}... | collective-permute-start | bytes 270344 | tf_op jit(solution)/shard_map/ppermute | solution.py:781
  56.2 0.6 copy-start.9
  56.2 0.7 copy-start.7
  56.3 0.7 copy-start.10
  61.2 4.6 %collective-permute-start.9 = (bf16[352,128]{1,0:T(8,128)(2,1)S(1)}, bf16[352,128]{1,0:T(8,128)(2,1)S(1)}, u32[]{:S(2)}, u32[]{:S(2)}) collective-permute-start(bf16[352,128]{1,0:T(8,128)(2,1)S(1)} %pad_maximum_fusion.1), channel_id=1, source_target_pairs={{0,4},{2,6},{4,0},{6,2},{8,12},{10,14},{12,8},{14,10},{1,5},{3,7},... | collective-permute-start | bytes 270344 | tf_op jit(solution)/shard_map/ppermute | solution.py:781
  65.9 5.8 %collective-permute-start.10 = (bf16[352,128]{1,0:T(8,128)(2,1)S(1)}, bf16[352,128]{1,0:T(8,128)(2,1)S(1)}, u32[]{:S(2)}, u32[]{:S(2)}) collective-permute-start(bf16[352,128]{1,0:T(8,128)(2,1)S(1)} %get-tuple-element.80), channel_id=1, source_target_pairs={{0,2},{2,0},{4,6},{6,4},{8,10},{10,8},{12,14},{14,12},{1,3},{3,1},... | collective-permute-start | bytes 270344 | tf_op jit(solution)/shard_map/ppermute | solution.py:781
  71.8 1.4 %copy-start = (bf16[352,128]{1,0:T(8,128)(2,1)}, bf16[352,128]{1,0:T(8,128)(2,1)S(1)}, u32[]{:S(2)}) copy-start(bf16[352,128]{1,0:T(8,128)(2,1)S(1)} %pad_maximum_fusion.3.sent_ref) | copy-start | bytes 270340
  71.8 1.4 %collective-permute-start.11 = (bf16[352,128]{1,0:T(8,128)(2,1)S(1)}, bf16[352,128]{1,0:T(8,128)(2,1)S(1)}, u32[]{:S(2)}, u32[]{:S(2)}) collective-permute-start(bf16[352,128]{1,0:T(8,128)(2,1)S(1)} %pad_maximum_fusion.3.sent_ref), channel_id=1, source_target_pairs={{0,1},{1,0},{2,3},{3,2},{4,5},{5,4},{6,7},{7,6},{8,9},{9,8},{10,11... | collective-permute-start | bytes 270344 | tf_op jit(solution)/shard_map/ppermute | solution.py:793
  73.2 0.6 copy-start.3

commit v6 on v5

--- a/solution.py
+++ b/solution.py
@@ -15,7 +15,7 @@
 CODE_ROWS = 16
 CODE_BASE = 128
 SMALL_ROWS = 16
-VMEM_LIMIT = 56 * 1024 * 1024
+VMEM_LIMIT = 62 * 1024 * 1024
 EARLY_SHARE = 6
 
 
@@ -136,7 +136,7 @@
         return HaloCopy(is_odd, *[ref.at[place] for ref in refs], target, sem)
 
 
-    part = samples // 2
+    part = samples // 4
     part_copies = {}
     for n, side in enumerate(sides):
         for s in range(0, samples, part):
@@ -643,7 +643,7 @@
             pltpu.VMEM((2, CODE_ROWS, span), BF16),
             pltpu.VMEM((blocks, rows, channels), BF16),
             pltpu.VMEM(per_query, BF16),
-            pltpu.SemaphoreType.DMA((len(sides), 2, 3)),
+            pltpu.SemaphoreType.DMA((len(sides), 4, 3)),
             pltpu.VMEM(per_query, BF16),
             pltpu.VMEM(per_query, BF16),
             pltpu.VMEM(per_query, F32),

time: 76.1 us -> 77.4 us (1.017)
  Pallas kernels: 46.4 us -> 47.8 us
    pallas_call x3, Pallas kernels: 36.8 us -> 38.2 us  [call(): pl.pallas_call(functools.partial(attention_kernel, geo, sides, edge, chai...]
where the time goes in v6:
time: 77.4 us; the launch traced here: 76.9 us
  Pallas kernels  47.8 us (62%)
  starting transfers between devices  16.5 us (21%)
  waiting for transfers between devices  7.29 us (9%)
  local copies, waits for them, and re-layouts  2.21 us (3%)
  between operations  1.86 us (2%)
  other arithmetic  1.28 us (2%)
    pallas_call x3, Pallas kernels, call(): pl.pallas_call(functools.partial(attention_kernel, geo, sides, edge, chai...  38.2 us
    ppermute x3, starting transfers between devices, per_device(): got = lax.ppermute(sent, 'atoms', [(i, i ^ step) for i in range(ranges)])  7.81 us
    ppermute x4, starting transfers between devices, per_device(): lax.ppermute(part, 'atoms', swaps)  7.54 us
    ppermute x3, waiting for transfers between devices, per_device(): got = lax.ppermute(sent, 'atoms', [(i, i ^ step) for i in range(ranges)])  4.42 us
    pallas_call x1, Pallas kernels, sum_act(): pl.pallas_call(functools.partial(act_sum_kernel, [first for first, _ in p...  3 us
    pallas_call x1, Pallas kernels, sum_pair(): pl.pallas_call(functools.partial(pair_kernel, order=(early, low + high, l...  2.96 us
    unnamed x22, local copies, waits for them, and re-layouts  2.12 us
    pallas_call x1, Pallas kernels, per_device(): pl.pallas_call(payload_kernel, out_shape=[jax.ShapeDtypeStruct((samples +...  1.9 us
  transfers between devices with their start and end apart: 12, of which 6 were waited for; matrix products, arithmetic and copies ran while one was open for 1% of the time, Pallas kernels for 37%

profile of v6, /device:TPU:0, one launch (start us, length us, event | category | flops | bytes accessed | tf_op | source)
XLA Modules:
  0.0 76.9 jit_solution(8323504710754888361)
XLA Ops:
  1.3 1.9 %shard_map.164 = (bf16[9,128,128]{2,1,0:T(8,128)(2,1)}, bf16[9,128,128]{2,1,0:T(8,128)(2,1)}) custom-call(bf16[8,640,128]{2,1,0:T(8,128)(2,1)} %refs_4_.5, bf16[8,640,128]{2,1,0:T(8,128)(2,1)} %refs_4_.5, s32[5,128]{1,0:T(8,128)} %bitcast.6, s32[1]{0:T(128)S(6)} %copy.18.padding_ref.refs_1_), custom_call_target="tpu_custom_call" | custom-call | tf_op jit(solution)/shard_map/pallas_call | solution.py:580
  3.2 2.9 %collective-permute-start = (bf16[9,128,128]{2,1,0:T(8,128)(2,1)}, bf16[9,128,128]{2,1,0:T(8,128)(2,1)S(1)}, u32[]{:S(2)}, u32[]{:S(2)}) collective-permute-start(bf16[9,128,128]{2,1,0:T(8,128)(2,1)} %get-tuple-element.38), channel_id=1, source_target_pairs={{0,2},{2,0},{4,6},{6,4},{8,10},{10,8},{12,14},{14,12},{1,3},{3,1},... | collective-permute-start | bytes 884744 | tf_op jit(solution)/shard_map/ppermute | solution.py:592
  6.1 0.7 collective-permute-start.1
  6.8 11.1 %shard_map.165 = (bf16[8,448,128]{2,1,0:T(8,128)(2,1)}, f32[2,336,128]{2,1,0:T(8,128)}, f32[6,64,128]{2,1,0:T(8,128)}, bf16[6,64,128]{2,1,0:T(8,128)(2,1)}) custom-call(s32[20]{0:T(128)} %refs_0_.5, s32[1]{0:T(128)S(6)} %copy.18.padding_ref.refs_1_, f32[4]{0:T(128)} %refs_2_.5, s32[5,128]{1,0:T(8,128)} %bitcast.7, bf16[8,640,128]{2,1,0:T(8,128)(2,1)} %refs_4_.5, ...), custom_call_target="tpu_custom_call" | custom-call | flops 7516192768 | bytes 12000000 | tf_op jit(solution)/shard_map/pallas_call | solution.py:671
  17.9 1.1 %collective-permute-done.refs_13_ = bf16[9,128,128]{2,1,0:T(8,128)(2,1)S(1)} collective-permute-done((bf16[9,128,128]{2,1,0:T(8,128)(2,1)}, bf16[9,128,128]{2,1,0:T(8,128)(2,1)S(1)}, u32[]{:S(2)}, u32[]{:S(2)}) %collective-permute-start) | collective-permute-done | bytes 294944 | tf_op jit(solution)/shard_map/ppermute | solution.py:592
  19.0 0.7 copy-done.4
  19.8 15.7 %shard_map.166 = (bf16[8,256,128]{2,1,0:T(8,128)(2,1)}, bf16[8,256,128]{2,1,0:T(8,128)(2,1)}, bf16[8,128,128]{2,1,0:T(8,128)(2,1)}, bf16[8,128,128]{2,1,0:T(8,12...) custom-call(s32[20]{0:T(128)} %refs_0_.5, s32[1]{0:T(128)S(6)} %copy.18.padding_ref.refs_1_, ...), custom_call_target="tpu_custom_call" | custom-call | flops 11274289152 | bytes 12000000 | tf_op jit(solution)/shard_map/pallas_call | solution.py:671
  35.5 3.1 %collective-permute-start.2 = (bf16[8,128,128]{2,1,0:T(8,128)(2,1)}, bf16[8,128,128]{2,1,0:T(8,128)(2,1)S(1)}, u32[]{:S(2)}, u32[]{:S(2)}) collective-permute-start(bf16[8,128,128]{2,1,0:T(8,128)(2,1)} %get-tuple-element.45), channel_id=1, source_target_pairs={{0,2},{2,0},{4,6},{6,4},{8,10},{10,8},{12,14},{14,12},{1,3},{3,1},... | collective-permute-start | bytes 786440 | tf_op jit(solution)/shard_map/ppermute | solution.py:710
  38.6 0.8 %collective-permute-start.3 = (bf16[8,128,128]{2,1,0:T(8,128)(2,1)}, bf16[8,128,128]{2,1,0:T(8,128)(2,1)S(1)}, u32[]{:S(2)}, u32[]{:S(2)}) collective-permute-start(bf16[8,128,128]{2,1,0:T(8,128)(2,1)} %get-tuple-element.46), channel_id=1, source_target_pairs={{2,4},{4,2},{6,8},{8,6},{10,12},{12,10},{3,5},{5,3},{7,9},{9,7},{1... | collective-permute-start | bytes 786440 | tf_op jit(solution)/shard_map/ppermute | solution.py:710
  39.5 11.4 %shard_map.167 = (bf16[8,448,128]{2,1,0:T(8,128)(2,1)}, f32[336,128]{1,0:T(8,128)}, bf16[352,128]{1,0:T(8,128)(2,1)}, f32[6,64,128]{2,1,0:T(8,128)}, bf16[6,64,128]{2,1,0:T(8,128)(2,1)}) custom-call(s32[20]{0:T(128)} %refs_0_.5, s32[1]{0:T(128)S(6)} %copy.18.padding_ref.refs_1_, f32[4]{0:T(128)} %refs_2_.5, s32[5,128]{1,0:T(8,128)} %bitcast.9, ...), custom_call_target="tpu_custom_call" | custom-call | flops 7516192768 | bytes 12000000 | tf_op jit(solution)/shard_map/pallas_call | solution.py:671
  51.0 0.5 collective-permute-start.6
  52.5 0.9 %reduce-precision_convert_fusion.3 = (bf16[336,128]{1,0:T(8,128)(2,1)S(1)}, f32[336,128]{1,0:T(8,128)S(1)}) fusion(f32[336,128]{1,0:T(8,128)} %get-tuple-element.42, f32[16,128]{1,0:T(8,128)S(1)} %slice_add_fusion.6, f32[320,128]{1,0:T(8,128)S(1)} %slice.116), kind=kLoop, calls=%fused_computation.26 | loop fusion | flops 172032 | bytes 602112 | tf_op jit(solution)/shard_map/convert.6
  53.5 3.9 %collective-permute-start.5 = (bf16[352,128]{1,0:T(8,128)(2,1)S(1)}, bf16[352,128]{1,0:T(8,128)(2,1)S(1)}, u32[]{:S(2)}, u32[]{:S(2)}) collective-permute-start(bf16[352,128]{1,0:T(8,128)(2,1)S(1)} %pad_maximum_fusion), channel_id=1, source_target_pairs={{0,8},{2,10},{4,12},{6,14},{8,0},{10,2},{12,4},{14,6},{1,9},{3,11}... | collective-permute-start | bytes 270344 | tf_op jit(solution)/shard_map/ppermute | solution.py:781
  57.6 0.6 copy-done.9
  58.2 3.0 %shard_map.168 = bf16[20,256,128]{2,1,0:T(8,128)(2,1)} custom-call(bf16[4,16]{1,0:T(4,128)(2,1)} %bitcast.18, f32[6,64,128]{2,1,0:T(8,128)} %get-tuple-element.50.refs_0_, bf16[6,64,128]{2,1,0:T(8,128)(2,1)} %copy-done.9, f32[8,64,128]{2,1,0:T(8,128)} %get-tuple-element.52.refs_2_, bf16[8,64,128]{2,1,0:T(8,128)(2,1)} %copy-done.7, ...), custom_call_target="tpu_custom_call" | custom-call | flops 671088640 | bytes 4000000 | tf_op jit(solution)/shard_map/pallas_call | solution.py:737
  61.2 1.1 %collective-permute-done.5 = bf16[352,128]{1,0:T(8,128)(2,1)S(1)} collective-permute-done((bf16[352,128]{1,0:T(8,128)(2,1)S(1)}, bf16[352,128]{1,0:T(8,128)(2,1)S(1)}, u32[]{:S(2)}, u32[]{:S(2)}) %collective-permute-start.5) | collective-permute-done | bytes 90144 | tf_op jit(solution)/shard_map/ppermute | solution.py:781
  62.5 0.8 collective-permute-start.9
  63.3 3.0 %shard_map.169 = bf16[8,640,128]{2,1,0:T(8,128)(2,1)} custom-call(bf16[8,448,128]{2,1,0:T(8,128)(2,1)} %get-tuple-element.59.refs_0_, bf16[8,448,128]{2,1,0:T(8,128)(2,1)} %get-tuple-element.60.refs_1_, bf16[8,256,128]{2,1,0:T(8,128)(2,1)} %get-tuple-element.61.refs_2_, bf16[8,256,128]{2,1,0:T(8,128)(2,1)} %get-tuple-element.62.refs_3_, ...), custom_call_target="tpu_custom_call" | custom-call | flops 2621440 | bytes 6000000 | tf_op jit(solution)/shard_map/pallas_call | solution.py:756
  66.3 0.8 %collective-permute-done.9 = bf16[352,128]{1,0:T(8,128)(2,1)S(1)} collective-permute-done((bf16[352,128]{1,0:T(8,128)(2,1)S(1)}, bf16[352,128]{1,0:T(8,128)(2,1)S(1)}, u32[]{:S(2)}, u32[]{:S(2)}) %collective-permute-start.9) | collective-permute-done | bytes 90144 | tf_op jit(solution)/shard_map/ppermute | solution.py:781
  67.2 3.1 %collective-permute-start.10 = (bf16[352,128]{1,0:T(8,128)(2,1)S(1)}, bf16[352,128]{1,0:T(8,128)(2,1)S(1)}, u32[]{:S(2)}, u32[]{:S(2)}) collective-permute-start(bf16[352,128]{1,0:T(8,128)(2,1)S(1)} %get-tuple-element.80), channel_id=1, source_target_pairs={{0,2},{2,0},{4,6},{6,4},{8,10},{10,8},{12,14},{14,12},{1,3},{3,1},... | collective-permute-start | bytes 270344 | tf_op jit(solution)/shard_map/ppermute | solution.py:781
  70.4 2.5 %collective-permute-done.10 = bf16[352,128]{1,0:T(8,128)(2,1)S(1)} collective-permute-done((bf16[352,128]{1,0:T(8,128)(2,1)S(1)}, bf16[352,128]{1,0:T(8,128)(2,1)S(1)}, u32[]{:S(2)}, u32[]{:S(2)}) %collective-permute-start.10) | collective-permute-done | bytes 90144 | tf_op jit(solution)/shard_map/ppermute | solution.py:781
  73.1 1.3 %collective-permute-done.11.got_ref = bf16[352,128]{1,0:T(8,128)(2,1)S(1)} collective-permute-done((bf16[352,128]{1,0:T(8,128)(2,1)S(1)}, bf16[352,128]{1,0:T(8,128)(2,1)S(1)}, u32[]{:S(2)}, u32[]{:S(2)}) %collective-permute-start.11) | collective-permute-done | bytes 90144 | tf_op jit(solution)/shard_map/ppermute | solution.py:793
  74.4 0.6 copy-done.3
  75.0 1.8 %shard_map.170 = (f32[640,128]{1,0:T(8,128)}, f32[4,16]{1,0:T(4,128)}, f32[4]{0:T(128)}) custom-call(bf16[352,128]{1,0:T(8,128)(2,1)} %copy-done, bf16[352,128]{1,0:T(8,128)(2,1)} %copy-done.3), custom_call_target="tpu_custom_call" | custom-call | tf_op jit(solution)/shard_map/pallas_call | solution.py:794
  (65 shorter events, 1.8 us)
Async XLA Ops:
  3.2 15.8 %collective-permute-start = (bf16[9,128,128]{2,1,0:T(8,128)(2,1)}, bf16[9,128,128]{2,1,0:T(8,128)(2,1)S(1)}, u32[]{:S(2)}, u32[]{:S(2)}) collective-permute-start(bf16[9,128,128]{2,1,0:T(8,128)(2,1)} %get-tuple-element.38), channel_id=1, source_target_pairs={{0,2},{2,0},{4,6},{6,4},{8,10},{10,8},{12,14},{14,12},{1,3},{3,1},... | collective-permute-start | bytes 884744 | tf_op jit(solution)/shard_map/ppermute | solution.py:592
  6.1 12.9 %collective-permute-start.1 = (bf16[9,128,128]{2,1,0:T(8,128)(2,1)}, bf16[9,128,128]{2,1,0:T(8,128)(2,1)S(1)}, u32[]{:S(2)}, u32[]{:S(2)}) collective-permute-start(bf16[9,128,128]{2,1,0:T(8,128)(2,1)} %get-tuple-element.39), channel_id=1, source_target_pairs={{2,4},{4,2},{6,8},{8,6},{10,12},{12,10},{3,5},{5,3},{7,9},{9,7},{1... | collective-permute-start | bytes 884744 | tf_op jit(solution)/shard_map/ppermute | solution.py:592
  19.0 0.7 copy-start.4
  19.0 0.8 %copy-start.5 = (bf16[9,128,128]{2,1,0:T(8,128)(2,1)}, bf16[9,128,128]{2,1,0:T(8,128)(2,1)S(1)}, u32[]{:S(2)}) copy-start(bf16[9,128,128]{2,1,0:T(8,128)(2,1)S(1)} %collective-permute-done.1.refs_14_) | copy-start | bytes 884740
  35.5 15.4 %collective-permute-start.2 = (bf16[8,128,128]{2,1,0:T(8,128)(2,1)}, bf16[8,128,128]{2,1,0:T(8,128)(2,1)S(1)}, u32[]{:S(2)}, u32[]{:S(2)}) collective-permute-start(bf16[8,128,128]{2,1,0:T(8,128)(2,1)} %get-tuple-element.45), channel_id=1, source_target_pairs={{0,2},{2,0},{4,6},{6,4},{8,10},{10,8},{12,14},{14,12},{1,3},{3,1},... | collective-permute-start | bytes 786440 | tf_op jit(solution)/shard_map/ppermute | solution.py:710
  38.6 12.3 %collective-permute-start.3 = (bf16[8,128,128]{2,1,0:T(8,128)(2,1)}, bf16[8,128,128]{2,1,0:T(8,128)(2,1)S(1)}, u32[]{:S(2)}, u32[]{:S(2)}) collective-permute-start(bf16[8,128,128]{2,1,0:T(8,128)(2,1)} %get-tuple-element.46), channel_id=1, source_target_pairs={{2,4},{4,2},{6,8},{8,6},{10,12},{12,10},{3,5},{5,3},{7,9},{9,7},{1... | collective-permute-start | bytes 786440 | tf_op jit(solution)/shard_map/ppermute | solution.py:710
  39.5 11.6 %copy-start.8 = (bf16[6,64,128]{2,1,0:T(8,128)(2,1)S(1)}, bf16[6,64,128]{2,1,0:T(8,128)(2,1)}, u32[]{:S(2)}) copy-start(bf16[6,64,128]{2,1,0:T(8,128)(2,1)} %get-tuple-element.51) | copy-start | bytes 294916
  39.5 12.0 %copy-start.6 = (bf16[8,64,128]{2,1,0:T(8,128)(2,1)S(1)}, bf16[8,64,128]{2,1,0:T(8,128)(2,1)}, u32[]{:S(2)}) copy-start(bf16[8,64,128]{2,1,0:T(8,128)(2,1)} %get-tuple-element.53) | copy-start | bytes 393220
  50.9 10.3 %copy-start.1 = (bf16[8,128,128]{2,1,0:T(8,128)(2,1)}, bf16[8,128,128]{2,1,0:T(8,128)(2,1)S(1)}, u32[]{:S(2)}) copy-start(bf16[8,128,128]{2,1,0:T(8,128)(2,1)S(1)} %collective-permute-done.2.refs_4_) | copy-start | bytes 786436
  50.9 10.3 %copy-start.2 = (bf16[8,128,128]{2,1,0:T(8,128)(2,1)}, bf16[8,128,128]{2,1,0:T(8,128)(2,1)S(1)}, u32[]{:S(2)}) copy-start(bf16[8,128,128]{2,1,0:T(8,128)(2,1)S(1)} %collective-permute-done.3.refs_5_) | copy-start | bytes 786436
  50.9 1.6 %collective-permute-start.4 = (bf16[352,128]{1,0:T(8,128)(2,1)}, bf16[352,128]{1,0:T(8,128)(2,1)S(1)}, u32[]{:S(2)}, u32[]{:S(2)}) collective-permute-start(bf16[352,128]{1,0:T(8,128)(2,1)} %get-tuple-element.47), channel_id=1, source_target_pairs={{0,1},{1,0},{2,3},{3,2},{4,5},{5,4},{6,7},{7,6},{8,9},{9,8},{10,11... | collective-permute-start | bytes 270344 | tf_op jit(solution)/shard_map/ppermute | solution.py:735
  51.0 6.5 %collective-permute-start.6 = (bf16[6,64,128]{2,1,0:T(8,128)(2,1)S(1)}, bf16[6,64,128]{2,1,0:T(8,128)(2,1)S(1)}, u32[]{:S(2)}, u32[]{:S(2)}) collective-permute-start(bf16[6,64,128]{2,1,0:T(8,128)(2,1)S(1)} %copy-done.8), channel_id=1, source_target_pairs={{0,1},{1,0},{2,3},{3,2},{4,5},{5,4},{6,7},{7,6},{8,9},{9,8},{10,11... | collective-permute-start | bytes 294920 | tf_op jit(solution)/shard_map/ppermute | solution.py:697
  51.5 6.0 %collective-permute-start.7 = (bf16[8,64,128]{2,1,0:T(8,128)(2,1)S(1)}, bf16[8,64,128]{2,1,0:T(8,128)(2,1)S(1)}, u32[]{:S(2)}, u32[]{:S(2)}) collective-permute-start(bf16[8,64,128]{2,1,0:T(8,128)(2,1)S(1)} %copy-done.6), channel_id=1, source_target_pairs={{0,1},{1,0},{2,3},{3,2},{4,5},{5,4},{6,7},{7,6},{8,9},{9,8},{10,11... | collective-permute-start | bytes 393224 | tf_op jit(solution)/shard_map/ppermute | solution.py:708
  51.6 6.0 %collective-permute-start.8 = (bf16[6,64,128]{2,1,0:T(8,128)(2,1)}, bf16[6,64,128]{2,1,0:T(8,128)(2,1)S(1)}, u32[]{:S(2)}, u32[]{:S(2)}) collective-permute-start(bf16[6,64,128]{2,1,0:T(8,128)(2,1)} %get-tuple-element.55), channel_id=1, source_target_pairs={{0,1},{1,0},{2,3},{3,2},{4,5},{5,4},{6,7},{7,6},{8,9},{9,8},{10,11... | collective-permute-start | bytes 294920 | tf_op jit(solution)/shard_map/ppermute | solution.py:734
  53.5 8.8 %collective-permute-start.5 = (bf16[352,128]{1,0:T(8,128)(2,1)S(1)}, bf16[352,128]{1,0:T(8,128)(2,1)S(1)}, u32[]{:S(2)}, u32[]{:S(2)}) collective-permute-start(bf16[352,128]{1,0:T(8,128)(2,1)S(1)} %pad_maximum_fusion), channel_id=1, source_target_pairs={{0,8},{2,10},{4,12},{6,14},{8,0},{10,2},{12,4},{14,6},{1,9},{3,11}... | collective-permute-start | bytes 270344 | tf_op jit(solution)/shard_map/ppermute | solution.py:781
  57.5 0.6 copy-start.9
  57.5 0.7 copy-start.7
  57.6 0.7 copy-start.10
  62.5 4.6 %collective-permute-start.9 = (bf16[352,128]{1,0:T(8,128)(2,1)S(1)}, bf16[352,128]{1,0:T(8,128)(2,1)S(1)}, u32[]{:S(2)}, u32[]{:S(2)}) collective-permute-start(bf16[352,128]{1,0:T(8,128)(2,1)S(1)} %pad_maximum_fusion.1), channel_id=1, source_target_pairs={{0,4},{2,6},{4,0},{6,2},{8,12},{10,14},{12,8},{14,10},{1,5},{3,7},... | collective-permute-start | bytes 270344 | tf_op jit(solution)/shard_map/ppermute | solution.py:781
  67.2 5.6 %collective-permute-start.10 = (bf16[352,128]{1,0:T(8,128)(2,1)S(1)}, bf16[352,128]{1,0:T(8,128)(2,1)S(1)}, u32[]{:S(2)}, u32[]{:S(2)}) collective-permute-start(bf16[352,128]{1,0:T(8,128)(2,1)S(1)} %get-tuple-element.80), channel_id=1, source_target_pairs={{0,2},{2,0},{4,6},{6,4},{8,10},{10,8},{12,14},{14,12},{1,3},{3,1},... | collective-permute-start | bytes 270344 | tf_op jit(solution)/shard_map/ppermute | solution.py:781
  73.0 1.4 %copy-start = (bf16[352,128]{1,0:T(8,128)(2,1)}, bf16[352,128]{1,0:T(8,128)(2,1)S(1)}, u32[]{:S(2)}) copy-start(bf16[352,128]{1,0:T(8,128)(2,1)S(1)} %pad_maximum_fusion.3.sent_ref) | copy-start | bytes 270340
  73.0 1.4 %collective-permute-start.11 = (bf16[352,128]{1,0:T(8,128)(2,1)S(1)}, bf16[352,128]{1,0:T(8,128)(2,1)S(1)}, u32[]{:S(2)}, u32[]{:S(2)}) collective-permute-start(bf16[352,128]{1,0:T(8,128)(2,1)S(1)} %pad_maximum_fusion.3.sent_ref), channel_id=1, source_target_pairs={{0,1},{1,0},{2,3},{3,2},{4,5},{5,4},{6,7},{7,6},{8,9},{9,8},{10,11... | collective-permute-start | bytes 270344 | tf_op jit(solution)/shard_map/ppermute | solution.py:793
  74.4 0.6 copy-start.3
